TPU v7x, 32 devices: a whole 2x2x4 slice. The times are simulated.
32 devices in a mesh: section: 2 (over core), dp: 4 (over z), tensor: 4 (over y, x).
Axes of the slice: x: 2, y: 2, z: 4, core: 2. Of those that a mesh axis runs over, the one named last changes fastest.
Arguments:
- inputs: bfloat16 [4, 2, 256, 768], P('dp', None, 'tensor'), may hold values from -6 to 6
- cotangent: bfloat16 [4, 2, 256, 768], P('dp', None, 'tensor'), may hold values from -6 to 6
- segments: int32 [4, 2, 256], P('dp'), may hold values from 0 to 31, never falling along the last dimension, each value on 1 to 128 neighbouring positions
- row_params: bfloat16 [2, 6, 768], P('section', None, 'dp'), may hold values from 0.5 to 1.5
- qv_bias: bfloat16 [2, 2, 4, 192], P('section', None, 'tensor', 'dp'), may hold values from -3 to 3
- w_qkv: bfloat16 [2, 3, 768, 768], P('section', None, 'dp', 'tensor'), may hold values from -0.21875 to 0.21875
- w_out: bfloat16 [2, 768, 768], P('section', 'tensor', 'dp'), may hold values from -0.4375 to 0.4375
- fc1_bias: bfloat16 [2, 4, 768], P('section', 'tensor', 'dp'), may hold values from -3 to 3
- w_fc1: bfloat16 [2, 768, 3072], P('section', 'dp', 'tensor'), may hold values from -0.4375 to 0.4375
- w_fc2: bfloat16 [2, 3072, 768], P('section', 'tensor', 'dp'), may hold values from -0.21875 to 0.21875
Outputs:
- block_out: bfloat16 [2, 4, 2, 256, 768], P('section', 'dp', None, 'tensor')
- input_grads: float32 [2, 4, 2, 256, 768], P('section', 'dp', None, 'tensor')
- row_params_grad: float32 [2, 6, 768], P('section', None, ('dp', 'tensor'))
- qv_bias_grad: float32 [2, 2, 4, 192], P('section', None, 'tensor', 'dp')
- w_qkv_grad: float32 [2, 3, 768, 768], P('section', None, 'dp', 'tensor')
- w_out_grad: float32 [2, 768, 768], P('section', 'tensor', 'dp')
- fc1_bias_grad: float32 [2, 4, 768], P('section', 'tensor', 'dp')
- w_fc1_grad: float32 [2, 768, 3072], P('section', 'dp', 'tensor')
- w_fc2_grad: float32 [2, 3072, 768], P('section', 'tensor', 'dp')
Inputs may be any that keep to these rules, and one draw needn't show every extreme that they name: `segments`: document numbers never fall along a pack; every document spans 1 to 128 tokens and one spans exactly 128.
All inputs are finite; a program needn't handle non-finite values.
Results may differ from a plain program's by a relative error of at most 0.014.
Values may be sent and summed in bfloat16 or wider, within the bound.
No kernel may reach another device: no remote copies, remote signals or barrier semaphores. Data moves between devices by JAX's collectives and lax.ppermute only.
A program may use at most 128 MiB of HBM per device.

v0:
```python
import math

import jax
import jax.numpy as jnp
from jax import lax
from jax.sharding import PartitionSpec as P

HEAD_DIM = 64


EPSILON = 1e-05
NEG_LARGE = -1e30
GELU_SCALE = 0.7978845608028654
GELU_CUBIC = 0.044715


def passed_along(block, axis, distance):
    devices = range(lax.axis_size(axis))
    route = [(i - distance, i) for i in devices if i - distance in devices]
    return lax.ppermute(block, axis, route)


def norm_rows(values):
    center = values - jnp.mean(values, axis=-1, keepdims=True)
    inverse = lax.rsqrt(jnp.mean(center * center, axis=-1, keepdims=True) + EPSILON)
    return (center * inverse, inverse)


def norm_back(grads, normed, inverse, gain):
    scaled = grads * gain
    back = inverse * (
        scaled
        - jnp.mean(scaled, axis=-1, keepdims=True)
        - normed * jnp.mean(scaled * normed, axis=-1, keepdims=True)
    )
    return (back, jnp.sum(grads * normed, axis=0), jnp.sum(grads, axis=0))


def gelu_parts(hidden):
    tangent = jnp.tanh(GELU_SCALE * (hidden + GELU_CUBIC * hidden * hidden * hidden))
    activated = 0.5 * hidden * (1.0 + tangent)
    derivative = 0.5 * (1.0 + tangent) + 0.5 * hidden * (1.0 - tangent * tangent) * GELU_SCALE * (
        1.0 + 3.0 * GELU_CUBIC * hidden * hidden
    )
    return (activated, derivative)


def allowed_mask(segment_ids):
    position = jnp.arange(segment_ids.shape[0], dtype=jnp.int32)
    flags = (segment_ids[:, None] == segment_ids[None, :]) & (
        position[None, :] <= position[:, None]
    )
    return flags.astype(jnp.int32)


def scores_of(queries, keys_all, allowed):
    raw = jnp.einsum(
        "qhd,khd->hqk", queries, keys_all, preferred_element_type=jnp.float32
    ) / math.sqrt(HEAD_DIM)
    return jnp.where(allowed[None] == 1, raw, NEG_LARGE)


def inner_rows(left, right):
    return lax.dot_general(
        left, right, (((0,), (0,)), ((), ())), preferred_element_type=jnp.float32
    )


def by_transpose(left, right):
    return lax.dot_general(
        left, right, (((1,), (1,)), ((), ())), preferred_element_type=jnp.float32
    )


def slice_times(left, right):
    return jnp.dot(left, right, preferred_element_type=jnp.float32)


def slice_by_transpose(left, right):
    return by_transpose(left, right)


def three_by_transpose(lefts, proj_qkv):
    running = slice_by_transpose(lefts[0], proj_qkv[0])
    running = running + slice_by_transpose(lefts[1], proj_qkv[1])
    return running + slice_by_transpose(lefts[2], proj_qkv[2])


def unpack(gathered):
    return (
        gathered[0][0].astype(jnp.float32),
        gathered[1][0, :, 0].astype(jnp.float32),
        gathered[2][0],
        gathered[3][0],
        gathered[4][0, 0].astype(jnp.float32),
        gathered[5][0],
        gathered[6][0],
    )


def column_terms(grads):
    return (
        grads[1][None, :, None, :],
        grads[2][None],
        grads[3][None],
        grads[4][None, None],
        grads[5][None],
        grads[6][None],
    )


def layer_forward(stream_in, segment_ids, params):
    row_values, column_bias, proj_qkv, proj_out, hidden_bias, proj_up, proj_down = params
    stream = stream_in.astype(jnp.float32)
    normed_one, inverse_one = norm_rows(stream)
    attn_input = (normed_one * row_values[0] + row_values[1]).astype(jnp.bfloat16)
    attn_rows = lax.all_gather(attn_input, "tensor", axis=0, tiled=True)
    pack_len = attn_rows.shape[0]
    head_count = proj_qkv.shape[2] // HEAD_DIM
    queries = (
        (jnp.dot(attn_rows, proj_qkv[0], preferred_element_type=jnp.float32) + column_bias[0])
        .astype(jnp.bfloat16)
        .reshape(pack_len, head_count, HEAD_DIM)
    )
    keys_all = (
        jnp.dot(attn_rows, proj_qkv[1], preferred_element_type=jnp.float32)
        .astype(jnp.bfloat16)
        .reshape(pack_len, head_count, HEAD_DIM)
    )
    values_all = (
        (jnp.dot(attn_rows, proj_qkv[2], preferred_element_type=jnp.float32) + column_bias[1])
        .astype(jnp.bfloat16)
        .reshape(pack_len, head_count, HEAD_DIM)
    )
    allowed = allowed_mask(segment_ids)
    scores = scores_of(queries, keys_all, allowed)
    row_maximum = jnp.max(scores, axis=-1, keepdims=True)
    log_total = row_maximum + jnp.log(
        jnp.sum(jnp.exp(scores - row_maximum), axis=-1, keepdims=True)
    )
    weights_soft = jnp.exp(scores - log_total).astype(jnp.bfloat16)
    attended = (
        jnp.einsum("hqk,khd->qhd", weights_soft, values_all, preferred_element_type=jnp.float32)
        .reshape(pack_len, -1)
        .astype(jnp.bfloat16)
    )
    attn_out = lax.psum_scatter(
        slice_times(attended, proj_out), "tensor", scatter_dimension=0, tiled=True
    )
    middle = stream + attn_out + row_values[2]
    normed_two, inverse_two = norm_rows(middle)
    mlp_input = (normed_two * row_values[3] + row_values[4]).astype(jnp.bfloat16)
    mlp_rows = lax.all_gather(mlp_input, "tensor", axis=0, tiled=True)
    activated, derivative = gelu_parts(
        jnp.dot(mlp_rows, proj_up, preferred_element_type=jnp.float32) + hidden_bias
    )
    activated = activated.astype(jnp.bfloat16)
    mlp_out = lax.psum_scatter(
        slice_times(activated, proj_down), "tensor", scatter_dimension=0, tiled=True
    )
    result = middle + mlp_out + row_values[5]
    saved_state = (
        normed_one,
        inverse_one,
        attn_rows,
        queries,
        keys_all,
        values_all,
        log_total,
        attended,
        normed_two,
        inverse_two,
        mlp_rows,
        derivative,
        activated,
        allowed,
    )
    return (result, saved_state)


def layer_backward(grad_out, saved_state, params):
    row_values, column_bias, proj_qkv, proj_out, hidden_bias, proj_up, proj_down = params
    (
        normed_one,
        inverse_one,
        attn_rows,
        queries,
        keys_all,
        values_all,
        log_total,
        attended,
        normed_two,
        inverse_two,
        mlp_rows,
        derivative,
        activated,
        allowed,
    ) = saved_state
    pack_len = queries.shape[0]
    head_count = queries.shape[1]
    grad_low = grad_out.astype(jnp.bfloat16)
    grad_rows = lax.all_gather(grad_low, "tensor", axis=0, tiled=True)
    grad_down = inner_rows(activated, grad_rows)
    grad_hidden = by_transpose(grad_rows, proj_down) * derivative
    hidden_low = grad_hidden.astype(jnp.bfloat16)
    grad_hbias = jnp.sum(grad_hidden, axis=0)
    grad_up = inner_rows(mlp_rows, hidden_low)
    grad_mlp_in = lax.psum_scatter(
        slice_by_transpose(hidden_low, proj_up), "tensor", scatter_dimension=0, tiled=True
    )
    back_two, gain_two, shift_two = norm_back(grad_mlp_in, normed_two, inverse_two, row_values[3])
    grad_middle = grad_out + back_two
    middle_low = grad_middle.astype(jnp.bfloat16)
    middle_rows = lax.all_gather(middle_low, "tensor", axis=0, tiled=True)
    grad_proj_out = inner_rows(attended, middle_rows)
    grad_attended = (
        by_transpose(middle_rows, proj_out)
        .astype(jnp.bfloat16)
        .reshape(pack_len, head_count, HEAD_DIM)
    )
    probabilities = jnp.exp(scores_of(queries, keys_all, allowed) - log_total)
    probs_low = probabilities.astype(jnp.bfloat16)
    grad_values = jnp.einsum(
        "hqk,qhd->khd", probs_low, grad_attended, preferred_element_type=jnp.float32
    ).reshape(pack_len, -1)
    grad_probs = jnp.einsum(
        "qhd,khd->hqk", grad_attended, values_all, preferred_element_type=jnp.float32
    )
    row_delta = jnp.sum(probabilities * grad_probs, axis=-1, keepdims=True)
    grad_scores = (probabilities * (grad_probs - row_delta) / math.sqrt(HEAD_DIM)).astype(
        jnp.bfloat16
    )
    grad_queries = jnp.einsum(
        "hqk,khd->qhd", grad_scores, keys_all, preferred_element_type=jnp.float32
    ).reshape(pack_len, -1)
    grad_keys = jnp.einsum(
        "hqk,qhd->khd", grad_scores, queries, preferred_element_type=jnp.float32
    ).reshape(pack_len, -1)
    rounded_grads = (
        grad_queries.astype(jnp.bfloat16),
        grad_keys.astype(jnp.bfloat16),
        grad_values.astype(jnp.bfloat16),
    )
    grad_cbias = jnp.stack([jnp.sum(grad_queries, axis=0), jnp.sum(grad_values, axis=0)])
    grad_qkv = jnp.stack(
        [
            inner_rows(attn_rows, rounded_grads[0]),
            inner_rows(attn_rows, rounded_grads[1]),
            inner_rows(attn_rows, rounded_grads[2]),
        ]
    )
    grad_attn_in = lax.psum_scatter(
        three_by_transpose(rounded_grads, proj_qkv), "tensor", scatter_dimension=0, tiled=True
    )
    back_one, gain_one, shift_one = norm_back(grad_attn_in, normed_one, inverse_one, row_values[0])
    grad_in = grad_middle + back_one
    grad_rowvals = jnp.stack(
        [
            gain_one,
            shift_one,
            jnp.sum(grad_middle, axis=0),
            gain_two,
            shift_two,
            jnp.sum(grad_out, axis=0),
        ]
    )
    return (
        grad_in,
        (grad_rowvals, grad_cbias, grad_qkv, grad_proj_out, grad_hbias, grad_up, grad_down),
    )


def shards(inputs, cotangent, segments, row_params, qv_bias, w_qkv, w_out, fc1_bias, w_fc1, w_fc2):
    section_first = lax.axis_index("section") == 0
    micro_batch = inputs.shape[1]
    local_rows = inputs.shape[2]
    width = inputs.shape[3]
    forward_params = unpack(
        (
            lax.all_gather(row_params, "dp", axis=2, tiled=True),
            lax.all_gather(qv_bias, "dp", axis=3, tiled=True),
            lax.all_gather(w_qkv, "dp", axis=2, tiled=True),
            lax.all_gather(w_out, "dp", axis=2, tiled=True),
            lax.all_gather(fc1_bias, "dp", axis=2, tiled=True),
            lax.all_gather(w_fc1, "dp", axis=1, tiled=True),
            lax.all_gather(w_fc2, "dp", axis=2, tiled=True),
        )
    )
    received = jnp.zeros((local_rows, width), jnp.bfloat16)
    outputs_seen = []
    saved_states = []
    for clock_step in range(micro_batch + 1):
        section_input = jnp.where(
            section_first, inputs[0, min(clock_step, micro_batch - 1)], received
        )
        segment_now = jnp.where(
            section_first,
            segments[0, min(clock_step, micro_batch - 1)],
            segments[0, max(clock_step - 1, 0)],
        )
        result, saved_state = layer_forward(section_input, segment_now, forward_params)
        result_low = result.astype(jnp.bfloat16)
        if clock_step < micro_batch:
            received = passed_along(result_low, "section", 1)
        outputs_seen.append(result_low)
        saved_states.append(saved_state)
    block_out = jnp.where(
        section_first, jnp.stack(outputs_seen[:micro_batch]), jnp.stack(outputs_seen[1:])
    )[None, None]
    backward_params = unpack(
        (
            lax.all_gather(row_params, "dp", axis=2, tiled=True),
            lax.all_gather(qv_bias, "dp", axis=3, tiled=True),
            lax.all_gather(w_qkv, "dp", axis=2, tiled=True),
            lax.all_gather(w_out, "dp", axis=2, tiled=True),
            lax.all_gather(fc1_bias, "dp", axis=2, tiled=True),
            lax.all_gather(w_fc1, "dp", axis=1, tiled=True),
            lax.all_gather(w_fc2, "dp", axis=2, tiled=True),
        )
    )
    grad_received = jnp.zeros((local_rows, width), jnp.float32)
    grads_seen = []
    total_sums = None
    for clock_step in range(micro_batch + 1):
        own_grad = cotangent[0, min(clock_step, micro_batch - 1)].astype(jnp.float32)
        grad_out = jnp.where(section_first, grad_received, own_grad)
        saved_state = jax.tree.map(
            lambda earlier, later: jnp.where(section_first, earlier, later),
            saved_states[max(clock_step - 1, 0)],
            saved_states[min(clock_step + 1, micro_batch)],
        )
        grad_in, grads = layer_backward(grad_out, saved_state, backward_params)
        useful = jnp.where(section_first, clock_step >= 1, clock_step < micro_batch)
        masked = jax.tree.map(
            lambda current: jnp.where(useful, current, jnp.zeros_like(current)), grads
        )
        if total_sums is None:
            total_sums = masked
        else:
            total_sums = jax.tree.map(
                lambda running, current: running + current, total_sums, masked
            )
        if clock_step < micro_batch:
            grad_received = passed_along(grad_in, "section", -1)
        grads_seen.append(grad_in)
    input_grads = jnp.where(
        section_first, jnp.stack(grads_seen[1:]), jnp.stack(grads_seen[:micro_batch])
    )[None, None]
    row_total = total_sums[0]
    end_terms = column_terms(total_sums)
    column_grads = (
        lax.psum_scatter(end_terms[0], "dp", scatter_dimension=3, tiled=True),
        lax.psum_scatter(end_terms[1], "dp", scatter_dimension=2, tiled=True),
        lax.psum_scatter(end_terms[2], "dp", scatter_dimension=2, tiled=True),
        lax.psum_scatter(end_terms[3], "dp", scatter_dimension=2, tiled=True),
        lax.psum_scatter(end_terms[4], "dp", scatter_dimension=1, tiled=True),
        lax.psum_scatter(end_terms[5], "dp", scatter_dimension=2, tiled=True),
    )
    row_grad = lax.psum_scatter(row_total, ("dp", "tensor"), scatter_dimension=1, tiled=True)[None]
    return (
        block_out,
        input_grads,
        row_grad,
        column_grads[0],
        column_grads[1],
        column_grads[2],
        column_grads[3],
        column_grads[4],
        column_grads[5],
    )


def solution(mesh):
    placed = (
        P("dp", None, "tensor", None),
        P("dp", None, "tensor", None),
        P("dp", None, None),
        P("section", None, "dp"),
        P("section", None, "tensor", "dp"),
        P("section", None, "dp", "tensor"),
        P("section", "tensor", "dp"),
        P("section", "tensor", "dp"),
        P("section", "dp", "tensor"),
        P("section", "tensor", "dp"),
    )
    return jax.shard_map(
        shards,
        mesh=mesh,
        in_specs=placed,
        out_specs=(
            P("section", "dp", None, "tensor", None),
            P("section", "dp", None, "tensor", None),
            P("section", None, ("dp", "tensor")),
            P("section", None, "tensor", "dp"),
            P("section", None, "dp", "tensor"),
            P("section", "tensor", "dp"),
            P("section", "tensor", "dp"),
            P("section", "dp", "tensor"),
            P("section", "tensor", "dp"),
        ),
        check_vma=False,
    )
```

profile of v0, /device:TPU:0, one launch (start us, length us, event | category | flops | bytes accessed | tf_op | source)
XLA Modules:
  0.0 979.6 jit_solution(2448515328142853771)
XLA Ops:
  8.9 16.2 %all_gather.62 = bf16[1,6,768]{1,0,2:T(2,128)(2,1)S(1)} all-gather(bf16[1,6,192]{1,0,2:T(2,128)(2,1)S(1)} %copy.52), channel_id=1, replica_groups=mesh['section'=2,'dp'=4,'tensor'=4] {'dp'}, dimensions={2}, use_global_device_ids=true | all-gather | bytes 11520 | tf_op jit(solution)/shard_map/all_gather | solution.py:280
  25.6 12.8 %slice_reduce_fusion = (f32[768]{0:T(1024)S(1)}, f32[768]{0:T(1024)S(1)}, f32[768]{0:T(1024)S(1)}, f32[768]{0:T(1024)S(1)}, f32[768]{0:T(1024)S(1)}, /*index=5*/f32[768]{0:T(1024)S(1)}) fusion(f32[1,6,768]{1,0,2:T(1,128)S(1)} %convert_element_type.317), kind=kLoop, calls=%fused_computation.159 | loop fusion | bytes 36864 | tf_op jit(solution)/shard_map/slice | solution.py:161
  49.4 21.1 %all_gather.64 = bf16[1,3,768,192]{3,2,1,0:T(8,128)(2,1)S(1)} all-gather(bf16[1,3,192,192]{3,2,1,0:T(8,128)(2,1)S(1)} %copy-done.102), channel_id=1, replica_groups=mesh['section'=2,'dp'=4,'tensor'=4] {'dp'}, dimensions={2}, use_global_device_ids=true | all-gather | bytes 1105920 | tf_op jit(solution)/shard_map/all_gather | solution.py:282
  70.5 13.5 %all_gather.65 = bf16[1,2,1,192]{2,1,0,3:T(2,128)(2,1)S(1)} all-gather(bf16[1,2,1,48]{2,1,0,3:T(2,128)(2,1)S(1)} %copy.53), channel_id=1, replica_groups=mesh['section'=2,'dp'=4,'tensor'=4] {'dp'}, dimensions={3}, use_global_device_ids=true | all-gather | bytes 960 | tf_op jit(solution)/shard_map/all_gather | solution.py:281
  88.1 16.5 %all_gather.66 = bf16[1,192,768]{1,0,2:T(2,128)(2,1)} all-gather(bf16[1,192,192]{1,0,2:T(2,128)(2,1)S(1)} %copy.55), channel_id=1, replica_groups=mesh['section'=2,'dp'=4,'tensor'=4] {'dp'}, dimensions={2}, use_global_device_ids=true | all-gather | bytes 368640 | tf_op jit(solution)/shard_map/all_gather | solution.py:283
  111.0 11.5 %all-reduce = bf16[768]{0:T(1024)(128)(2,1)S(1)} all-reduce(bf16[768]{0:T(1024)(128)(2,1)S(1)} %dynamic-update-slice), channel_id=1, replica_groups=mesh['section'=2,'dp'=4,'tensor'=4] {'dp'}, use_global_device_ids=true, to_apply=%add | all-reduce | flops 768 | bytes 3072
  122.5 11.7 %reduce-scatter.29.cloned.1.call-done = f32[64,768]{1,0:T(8,128)} async-done(((f32[256,768]{1,0:T(8,128)}), f32[64,768]{1,0:T(8,128)}) %reduce-scatter.29.cloned.1.call-update) | async-done | bytes 196624 | tf_op jit(solution)/shard_map/reduce_scatter | solution.py:147
  147.2 23.8 %all-gather.5.cloned.1.call-done = bf16[1,768,768]{1,2,0:T(8,128)(2,1)} async-done(((bf16[1,768,192]{1,2,0:T(8,128)(2,1)}), bf16[1,768,768]{1,2,0:T(8,128)(2,1)}) %all-gather.5.cloned.1.call-update) | async-done | bytes 1179664 | tf_op jit(solution)/shard_map/all_gather | solution.py:286
  173.9 25.4 %reduce-scatter.31.cloned.1.call-done = f32[64,768]{1,0:T(8,128)} async-done(((f32[256,768]{1,0:T(8,128)}), f32[64,768]{1,0:T(8,128)}) %reduce-scatter.31.cloned.1.call-update) | async-done | bytes 196624 | tf_op jit(solution)/shard_map/reduce_scatter | solution.py:158
  230.5 14.8 %reduce-scatter.33.cloned.1.call-done = f32[64,768]{1,0:T(8,128)} async-done(((f32[256,768]{1,0:T(8,128)}), f32[64,768]{1,0:T(8,128)}) %reduce-scatter.33.cloned.1.call-update) | async-done | bytes 196624 | tf_op jit(solution)/shard_map/reduce_scatter | solution.py:147
  269.4 20.9 %reduce-scatter.41.cloned.1.call-done = f32[64,768]{1,0:T(8,128)} async-done(((f32[256,768]{1,0:T(8,128)}), f32[64,768]{1,0:T(8,128)}) %reduce-scatter.41.cloned.1.call-update) | async-done | bytes 196624 | tf_op jit(solution)/shard_map/reduce_scatter | solution.py:208
  290.3 28.9 %reduce-scatter.35.cloned.1.call-done = f32[64,768]{1,0:T(8,128)} async-done(((f32[256,768]{1,0:T(8,128)}), f32[64,768]{1,0:T(8,128)}) %reduce-scatter.35.cloned.1.call-update) | async-done | bytes 196624 | tf_op jit(solution)/shard_map/reduce_scatter | solution.py:158
  349.4 24.2 %reduce-scatter.43.cloned.1.call-done = f32[64,768]{1,0:T(8,128)} async-done(((f32[256,768]{1,0:T(8,128)}), f32[64,768]{1,0:T(8,128)}) %reduce-scatter.43.cloned.1.call-update) | async-done | bytes 196624 | tf_op jit(solution)/shard_map/reduce_scatter | solution.py:252
  397.8 12.0 %all_gather.77 = bf16[256,768]{1,0:T(8,128)(2,1)} all-gather(bf16[64,768]{1,0:T(8,128)(2,1)S(1)} %fusion.175), channel_id=1, replica_groups=mesh['section'=2,'dp'=4,'tensor'=4] {'tensor'}, dimensions={0}, use_global_device_ids=true | all-gather | bytes 491520 | tf_op jit(solution)/shard_map/all_gather | solution.py:202
  442.1 23.9 %reduce-scatter.45.cloned.1.call-done = f32[64,768]{1,0:T(8,128)} async-done(((f32[256,768]{1,0:T(8,128)}), f32[64,768]{1,0:T(8,128)}) %reduce-scatter.45.cloned.1.call-update) | async-done | bytes 196624 | tf_op jit(solution)/shard_map/reduce_scatter | solution.py:208
  496.7 23.1 %reduce-scatter.47.cloned.1.call-done = f32[64,768]{1,0:T(8,128)} async-done(((f32[256,768]{1,0:T(8,128)}), f32[64,768]{1,0:T(8,128)}) %reduce-scatter.47.cloned.1.call-update) | async-done | bytes 196624 | tf_op jit(solution)/shard_map/reduce_scatter | solution.py:252
  527.4 12.0 %all_gather.79 = bf16[256,768]{1,0:T(8,128)(2,1)S(1)} all-gather(bf16[64,768]{1,0:T(8,128)(2,1)S(1)} %fusion.177), channel_id=1, replica_groups=mesh['section'=2,'dp'=4,'tensor'=4] {'tensor'}, dimensions={0}, use_global_device_ids=true | all-gather | bytes 491520 | tf_op jit(solution)/shard_map/all_gather | solution.py:202
  550.7 29.0 %reduce-scatter.49.cloned.1.call-done = f32[64,768]{1,0:T(8,128)} async-done(((f32[256,768]{1,0:T(8,128)}), f32[64,768]{1,0:T(8,128)}) %reduce-scatter.49.cloned.1.call-update) | async-done | bytes 196624 | tf_op jit(solution)/shard_map/reduce_scatter | solution.py:208
  662.8 18.4 %reduce-scatter.63.cloned.1.call-done = f32[192,1]{1,0:T(8,128)} async-done(((f32[768,1]{1,0:T(8,128)}), f32[192,1]{1,0:T(8,128)}) %reduce-scatter.63.cloned.1.call-update) | async-done | bytes 784
  683.5 45.9 %reduce-scatter.57.cloned.1.call-done = f32[48,2]{1,0:T(8,128)} async-done(((f32[192,2]{1,0:T(8,128)}), f32[48,2]{1,0:T(8,128)}) %reduce-scatter.57.cloned.1.call-update) | async-done | bytes 400
  733.2 19.9 %reduce-scatter.61.cloned.1.call-done = f32[192,192]{1,0:T(8,128)} async-done(((f32[768,192]{1,0:T(8,128)}), f32[192,192]{1,0:T(8,128)}) %reduce-scatter.61.cloned.1.call-update) | async-done | bytes 147472
  756.0 122.6 %reduce-scatter.55.cloned.1.call-done = f32[48,6]{1,0:T(8,128)} async-done(((f32[768,6]{1,0:T(8,128)}), f32[48,6]{1,0:T(8,128)}) %reduce-scatter.55.cloned.1.call-update) | async-done | bytes 1168
  880.0 41.4 %reduce-scatter.59.cloned.1.call-done = f32[192,576]{1,0:T(8,128)} async-done(((f32[768,576]{1,0:T(8,128)}), f32[192,576]{1,0:T(8,128)}) %reduce-scatter.59.cloned.1.call-update) | async-done | bytes 442384
  923.7 47.9 %reduce-scatter.53.cloned.1.call-done = f32[1,192,768]{2,1,0:T(8,128)} async-done(((f32[1,768,768]{2,1,0:T(8,128)}), f32[1,192,768]{2,1,0:T(8,128)}) %reduce-scatter.53.cloned.1.call-update) | async-done | bytes 589840 | tf_op jit(solution)/shard_map/reduce_scatter | solution.py:356
  (653 shorter events, 322.2 us)
Async XLA Ops:
  8.0 126.2 %reduce-scatter.29.cloned.1.call-start = ((), (), s32[]{:S(2)}) async-start(), calls=%async_computation.18 | async-start | bytes 983040 | tf_op jit(solution)/shard_map/reduce_scatter | solution.py:147
  108.2 37.0 %all-gather.3.cloned.1.call-start = ((), (), s32[]{:S(2)}) async-start(), calls=%async_computation.19 | async-start | bytes 1474560 | tf_op jit(solution)/shard_map/all_gather | solution.py:285
  108.8 62.2 %all-gather.5.cloned.1.call-start = ((), (), s32[]{:S(2)}) async-start(), calls=%async_computation.20 | async-start | bytes 1474560 | tf_op jit(solution)/shard_map/all_gather | solution.py:286
  109.4 89.9 %reduce-scatter.31.cloned.1.call-start = ((), (), s32[]{:S(2)}) async-start(), calls=%async_computation.21 | async-start | bytes 983040 | tf_op jit(solution)/shard_map/reduce_scatter | solution.py:158
  173.8 71.5 %reduce-scatter.33.cloned.1.call-start = ((), (), s32[]{:S(2)}) async-start(), calls=%async_computation.22 | async-start | bytes 983040 | tf_op jit(solution)/shard_map/reduce_scatter | solution.py:147
  218.5 71.8 %reduce-scatter.41.cloned.1.call-start = ((), (), s32[]{:S(2)}) async-start(), calls=%async_computation.26 | async-start | bytes 983040 | tf_op jit(solution)/shard_map/reduce_scatter | solution.py:208
  264.0 55.1 %reduce-scatter.35.cloned.1.call-start = ((), (), s32[]{:S(2)}) async-start(), calls=%async_computation.23 | async-start | bytes 983040 | tf_op jit(solution)/shard_map/reduce_scatter | solution.py:158
  267.1 106.6 %reduce-scatter.43.cloned.1.call-start = ((), (), s32[]{:S(2)}) async-start(), calls=%async_computation.27 | async-start | bytes 983040 | tf_op jit(solution)/shard_map/reduce_scatter | solution.py:252
  347.5 73.5 %reduce-scatter.37.cloned.1.call-start = ((), (), s32[]{:S(2)}) async-start(), calls=%async_computation.24 | async-start | bytes 983040 | tf_op jit(solution)/shard_map/reduce_scatter | solution.py:147
  347.5 27.9 %collective-permute-start.1 = (bf16[64,768]{1,0:T(8,128)(2,1)}, bf16[64,768]{1,0:T(8,128)(2,1)}, u32[]{:S(2)}, u32[]{:S(2)}) collective-permute-start(bf16[64,768]{1,0:T(8,128)(2,1)} %get-tuple-element.114), channel_id=1, source_target_pairs={{0,16},{1,17},{2,18},{3,19},{4,20},{5,21},{6,22},{7,23},{8,24},{9,... | collective-permute-start | bytes 294920 | tf_op jit(solution)/shard_map/ppermute | solution.py:20
  392.6 73.5 %reduce-scatter.45.cloned.1.call-start = ((), (), s32[]{:S(2)}) async-start(), calls=%async_computation.28 | async-start | bytes 983040 | tf_op jit(solution)/shard_map/reduce_scatter | solution.py:208
  392.7 3.5 collective-permute-start.2
  439.8 80.0 %reduce-scatter.47.cloned.1.call-start = ((), (), s32[]{:S(2)}) async-start(), calls=%async_computation.29 | async-start | bytes 983040 | tf_op jit(solution)/shard_map/reduce_scatter | solution.py:252
  493.6 57.1 %reduce-scatter.39.cloned.1.call-start = ((), (), s32[]{:S(2)}) async-start(), calls=%async_computation.25 | async-start | bytes 983040 | tf_op jit(solution)/shard_map/reduce_scatter | solution.py:158
  496.7 83.0 %reduce-scatter.49.cloned.1.call-start = ((), (), s32[]{:S(2)}) async-start(), calls=%async_computation.30 | async-start | bytes 983040 | tf_op jit(solution)/shard_map/reduce_scatter | solution.py:208
  523.1 3.3 collective-permute-start.3
  545.0 99.9 %reduce-scatter.51.cloned.1.call-start = ((), (), s32[]{:S(2)}) async-start(), calls=%async_computation.31 | async-start | bytes 983040 | tf_op jit(solution)/shard_map/reduce_scatter | solution.py:252
  603.8 77.4 %reduce-scatter.63.cloned.1.call-start = ((), (), s32[]{:S(2)}) async-start(), calls=%async_computation.37 | async-start | bytes 491520
  614.6 114.7 %reduce-scatter.57.cloned.1.call-start = ((), (), s32[]{:S(2)}) async-start(), calls=%async_computation.34 | async-start | bytes 122880
  616.0 114.9 %all-reduce.4.cloned.1.call-start = ((), (), s32[]{:S(2)}) async-start(), calls=%async_computation.38 | async-start | bytes 4718592
  626.8 126.3 %reduce-scatter.61.cloned.1.call-start = ((), (), s32[]{:S(2)}) async-start(), calls=%async_computation.36 | async-start | bytes 983040
  638.0 240.5 %reduce-scatter.55.cloned.1.call-start = ((), (), s32[]{:S(2)}) async-start(), calls=%async_computation.33 | async-start | bytes 417792
  647.2 274.2 %reduce-scatter.59.cloned.1.call-start = ((), (), s32[]{:S(2)}) async-start(), calls=%async_computation.35 | async-start | bytes 2457600
  657.4 314.1 %reduce-scatter.53.cloned.1.call-start = ((), (), s32[]{:S(2)}) async-start(), calls=%async_computation.32 | async-start | bytes 2949120 | tf_op jit(solution)/shard_map/reduce_scatter | solution.py:356
  (190 other events, 1614.5 us)
Sparse Core Ops, SparseCore 0:
  108.3 25.8 reduce-scatter.28
  174.0 25.2 reduce-scatter.30
  218.7 26.5 reduce-scatter.32
  264.1 26.1 reduce-scatter.40
  293.0 26.0 reduce-scatter.34
  347.6 26.0 reduce-scatter.42
  392.7 28.1 reduce-scatter.36
  440.0 26.0 reduce-scatter.44
  493.7 26.0 reduce-scatter.46
  522.6 28.0 reduce-scatter.38
  553.6 26.0 reduce-scatter.48
  603.9 26.1 reduce-scatter.50
  632.4 48.7 reduce-scatter.62
  683.4 45.8 reduce-scatter.56
  731.5 21.5 reduce-scatter.60
  757.6 120.8 reduce-scatter.54
  880.8 40.5 reduce-scatter.58
  924.2 47.2 reduce-scatter.52
Sparse Core Ops, SparseCore 1:
  110.3 30.0 all-gather.2
  141.7 29.3 all-gather.4
  626.9 100.5 all-reduce.3
where the time goes:
time: 990 us; the launch traced here: 980 us
  waiting for transfers between devices  543 us (55%)
  blocking collectives  199 us (20%)
  matrix products  98.6 us (10%)
  local copies, waits for them, and re-layouts  70.7 us (7%)
  other arithmetic  40.7 us (4%)
  between operations  20 us (2%)
    unnamed x27, waiting for transfers between devices  250 us
    reduce_scatter x3, waiting for transfers between devices, layer_backward(): lax.psum_scatter(slice_by_transpose(hidden_low, proj_up), 'tensor', scatt...  73.9 us
    reduce_scatter x3, waiting for transfers between devices, layer_forward(): lax.psum_scatter(slice_times(activated, proj_down), 'tensor', scatter_dim...  57.5 us
    reduce_scatter x1, waiting for transfers between devices, shards(): lax.psum_scatter(end_terms[4], 'dp', scatter_dimension=1, tiled=True)  47.9 us
    reduce_scatter x3, waiting for transfers between devices, layer_backward(): lax.psum_scatter(three_by_transpose(rounded_grads, proj_qkv), 'tensor', s...  47.4 us
    unnamed x402, local copies, waits for them, and re-layouts  42.1 us
    reduce_scatter x3, waiting for transfers between devices, layer_forward(): lax.psum_scatter(slice_times(attended, proj_out), 'tensor', scatter_dimen...  37.6 us
    all_gather x3, blocking collectives, layer_backward(): grad_rows = lax.all_gather(grad_low, 'tensor', axis=0, tiled=True)  34.3 us
  transfers between devices with their start and end apart: 25, of which 21 were waited for; matrix products, arithmetic and copies ran while one was open for 10% of the time, Pallas kernels for 0%

commit v1 on v0

v1 whole, which is shorter than its diff:
```python
import functools
import math

import jax
import jax.numpy as jnp
from jax import lax
from jax.experimental import pallas as pl
from jax.experimental.pallas import tpu as pltpu
from jax.sharding import PartitionSpec as P

HEAD_DIM = 64
EPSILON = 1e-05
NEG_LARGE = -1e30
GELU_SCALE = 0.7978845608028654
GELU_CUBIC = 0.044715
F32 = jnp.float32
BF16 = jnp.bfloat16
VMEM_LIMIT = 20 * 1024 * 1024


def dot(left, right):
    return jnp.dot(left, right, preferred_element_type=F32)


def dot_t(left, right):
    return lax.dot_general(left, right, (((1,), (1,)), ((), ())), preferred_element_type=F32)


def t_dot(left, right):
    return lax.dot_general(left, right, (((0,), (0,)), ((), ())), preferred_element_type=F32)


def norm_rows(values):
    center = values - jnp.mean(values, axis=-1, keepdims=True)
    inverse = lax.rsqrt(jnp.mean(center * center, axis=-1, keepdims=True) + EPSILON)
    return center * inverse, inverse


def norm_back(grads, normed, inverse, gain):
    scaled = grads * gain
    return inverse * (
        scaled
        - jnp.mean(scaled, axis=-1, keepdims=True)
        - normed * jnp.mean(scaled * normed, axis=-1, keepdims=True)
    )


def rows_of(refs):
    return jnp.concatenate([ref[...] for ref in refs], axis=0)


def store_blocks(outs, values, rows):
    for k, out in enumerate(outs):
        out[...] = values[k * rows : (k + 1) * rows].astype(out.dtype)


def summed(own, others):
    total = own[...]
    for ref in others:
        total = total + ref[...].astype(F32)
    return total


def struct(shape, dtype):
    return jax.ShapeDtypeStruct(shape, dtype)


def kept(shape, dtype):
    return pltpu.HBM(shape, dtype)


def far(array):
    return pltpu.with_memory_space_constraint(array, pltpu.HBM)


def call(body, outs, name, flops, args, specs=None, scratch=(), after=()):
    vmem = pl.BlockSpec(memory_space=pltpu.VMEM)
    specs = specs or [vmem] * len(args)
    if after:
        inner, count, extra = body, len(args), len(after)
        specs = specs + [pl.BlockSpec(memory_space=pl.ANY)] * extra
        args = [*args, *after]

        def body(*refs):
            inner(*refs[:count], *refs[count + extra :])

    nbytes = sum(math.prod(a.shape) * a.dtype.itemsize for a in (*args, *outs))
    return pl.pallas_call(
        body,
        out_shape=tuple(outs),
        in_specs=specs,
        out_specs=(vmem,) * len(outs),
        scratch_shapes=scratch,
        compiler_params=pltpu.CompilerParams(vmem_limit_bytes=VMEM_LIMIT),
        cost_estimate=pl.CostEstimate(flops=flops, bytes_accessed=nbytes, transcendentals=0),
        name=name,
    )(*args)


def attn_load(layer, weights, proj, sems):
    split = proj.shape[1] // 3
    copies = [
        pltpu.make_async_copy(weights.at[layer, :, at], proj.at[:, at], sems.at[i])
        for i, at in enumerate((pl.ds(0, split), pl.ds(split, 2 * split)))
    ]
    for copy in copies:
        copy.start()
    return copies


def mlp_load(weights, proj, sems, order):
    halves, rows = weights.shape[0], weights.shape[3]
    copies = [
        pltpu.make_async_copy(
            weights.at[i, :, g], proj.at[g, :, pl.ds(i * rows, rows), :], sems.at[i, g]
        )
        for g in order
        for i in range(halves)
    ]
    for copy in copies:
        copy.start()
    return copies[:halves], copies[halves:]


def wait_all(copies):
    for copy in copies:
        copy.wait()


def mlp_weight(proj, g):
    return proj[g].reshape(-1, proj.shape[-1])


def attn_fwd_body(n, layer, *refs):
    xs, (params, mask, weights), refs = refs[:n], refs[n : n + 3], refs[n + 3 :]
    (x_out, a_out, oqkv_out, lse_out), partials, (proj, sem) = refs[:4], refs[4:-2], refs[-2:]
    loading = attn_load(layer, weights, proj, sem)
    x = rows_of(xs)
    x_out[...] = x
    normed, _ = norm_rows(x.astype(F32))
    a = (normed * params[0:1] + params[1:2]).astype(BF16)
    a_out[...] = a
    width = proj.shape[1] // 4
    wait_all(loading)
    oqkv = (dot(a, proj[...]) + params[7:8]).astype(BF16)
    allowed = mask[...] > 0.5
    heads, logs = [], []
    for h in range(width // HEAD_DIM):
        q, k, v = (
            oqkv[:, (1 + i) * width + h * HEAD_DIM : (1 + i) * width + (h + 1) * HEAD_DIM]
            for i in range(3)
        )
        scores = jnp.where(allowed, dot_t(q, k) * HEAD_DIM**-0.5, NEG_LARGE)
        top = jnp.max(scores, axis=-1, keepdims=True)
        powers = jnp.exp(scores - top)
        total = jnp.sum(powers, axis=-1, keepdims=True)
        logs.append(top + jnp.log(total))
        heads.append(dot((powers * (1.0 / total)).astype(BF16), v).astype(BF16))
    o = jnp.concatenate(heads, axis=1)
    oqkv_out[...] = jnp.concatenate([o, oqkv[:, width:]], axis=1)
    lse_out[...] = jnp.concatenate(logs, axis=1)
    store_blocks(partials, dot_t(o, proj[:, :width]), xs[0].shape[0])


def middle_body(n, *refs):
    x, own, others, params, h_out, c_out = refs[0], refs[1], refs[2 : n + 1], *refs[n + 1 :]
    h = x[...].astype(F32) + summed(own, others) + params[2:3]
    h_out[...] = h
    normed, _ = norm_rows(h)
    c_out[...] = (normed * params[3:4] + params[4:5]).astype(BF16)


def mlp_fwd_body(n, *refs):
    cs, (params, weights) = refs[:n], refs[n : n + 2]
    c_out, m_out, der_out = refs[n + 2 : n + 5]
    partials, (proj, sems) = refs[n + 5 : -2], refs[-2:]
    first, second = mlp_load(weights, proj, sems, (0, 1))
    c = rows_of(cs)
    c_out[...] = c
    wait_all(first)
    u = dot(c, mlp_weight(proj, 0)) + params[6:7]
    tangent = jnp.tanh(GELU_SCALE * (u + GELU_CUBIC * u * u * u))
    m = (0.5 * u * (1.0 + tangent)).astype(BF16)
    der_out[...] = 0.5 * (1.0 + tangent) + 0.5 * u * (1.0 - tangent * tangent) * GELU_SCALE * (
        1.0 + 3.0 * GELU_CUBIC * u * u
    )
    m_out[...] = m
    wait_all(second)
    store_blocks(partials, dot_t(m, mlp_weight(proj, 1)), cs[0].shape[0])


def end_body(n, *refs):
    h, own, others, params, out = refs[0], refs[1], refs[2 : n + 1], *refs[n + 1 :]
    out[...] = (h[...] + summed(own, others) + params[5:6]).astype(BF16)


def mlp_bwd_body(n, *refs):
    es, (der, weights) = refs[:n], refs[n : n + 2]
    e_out, du_out, sum_out = refs[n + 2 : n + 5]
    partials, (proj, sems) = refs[n + 5 : -2], refs[-2:]
    first, second = mlp_load(weights, proj, sems, (1, 0))
    e = rows_of(es)
    e_out[...] = e
    wait_all(first)
    du = dot(e, mlp_weight(proj, 1)) * der[...]
    du_low = du.astype(BF16)
    du_out[...] = du_low
    sum_out[...] = jnp.sum(du, axis=0, keepdims=True)
    wait_all(second)
    store_blocks(partials, dot_t(du_low, mlp_weight(proj, 0)), es[0].shape[0])


def mlp_grads_body(dp, meta, c, e, du, m, keep, send, full):
    full[0] = t_dot(c[...], du[...])
    full[1] = t_dot(e[...], m[...])
    half = full.shape[1] // dp // 2
    first = meta[0] == 0
    for j in range(dp):
        for g in range(2):
            low, high = (full[g, (2 * j + i) * half : (2 * j + i + 1) * half].astype(BF16) for i in range(2))
            at = slice(g * half, (g + 1) * half)
            keep[j, at] = jnp.where(first, low, high)
            send[j, at] = jnp.where(first, high, low)


def middle_back_body(n, *refs):
    e, h, own, others, params = refs[0], refs[1], refs[2], refs[3 : n + 2], refs[n + 2]
    dh_out, low_out, sums_out = refs[n + 3 :]
    dc = summed(own, others)
    e_values = e[...].astype(F32)
    normed, inverse = norm_rows(h[...])
    dh = e_values + norm_back(dc, normed, inverse, params[3:4])
    dh_out[...] = dh
    low_out[...] = dh.astype(BF16)
    sums_out[...] = jnp.concatenate(
        [jnp.sum(v, axis=0, keepdims=True) for v in (dh, dc * normed, dc, e_values)], axis=0
    )


def attn_bwd_body(n, layer, *refs):
    carried = refs[n + 4 : 2 * n + 3] if layer == 0 else ()
    refs = refs[: n + 4] + refs[n + 4 + len(carried) :]
    dhs, (weights, oqkv_ref, lse, mask) = refs[:n], refs[n : n + 4]
    dh_out, dqkv_out, sums_out = refs[n + 4 : n + 7]
    partials, (proj, sem) = refs[n + 7 : -2], refs[-2:]
    loading = attn_load(layer, weights, proj, sem)
    dh = rows_of(dhs)
    dh_out[...] = dh
    loading[0].wait()
    width = proj.shape[1] // 4
    scale = HEAD_DIM**-0.5
    do = dot(dh, proj[:, :width]).astype(BF16)
    oqkv = oqkv_ref[...]
    allowed = mask[...] > 0.5
    dqs, dks, dvs = [], [], []
    for h in range(width // HEAD_DIM):
        q, k, v = (
            oqkv[:, (1 + i) * width + h * HEAD_DIM : (1 + i) * width + (h + 1) * HEAD_DIM]
            for i in range(3)
        )
        do_h = do[:, h * HEAD_DIM : (h + 1) * HEAD_DIM]
        scores = jnp.where(allowed, dot_t(q, k) * scale, NEG_LARGE)
        probs = jnp.exp(scores - lse[:, h : h + 1])
        dvs.append(t_dot(probs.astype(BF16), do_h))
        dp = dot_t(do_h, v)
        delta = jnp.sum(probs * dp, axis=-1, keepdims=True)
        ds = (probs * (dp - delta) * scale).astype(BF16)
        dqs.append(dot(ds, k))
        dks.append(t_dot(ds, q))
    dq, dk, dv = (jnp.concatenate(parts, axis=1) for parts in (dqs, dks, dvs))
    sums_out[...] = jnp.concatenate(
        [jnp.sum(dq, axis=0, keepdims=True), jnp.sum(dv, axis=0, keepdims=True)], axis=0
    )
    dqkv = jnp.concatenate([jnp.zeros_like(dq), dq, dk, dv], axis=1).astype(BF16)
    dqkv_out[...] = dqkv
    loading[1].wait()
    da = dot_t(dqkv, proj[...])
    if not carried:
        store_blocks(partials, da, dhs[0].shape[0])
        return
    rows = dhs[0].shape[0]
    partials[0][...] = da[:rows]
    for k, (out, ref) in enumerate(zip(partials[1:], carried), 1):
        out[:rows] = da[k * rows : (k + 1) * rows].astype(BF16)
        out[rows:] = ref[...]


def attn_grads_body(layer, dp, meta, x, dh, a, oqkv, dqkv_ref, weights, sums_mid, hidden_sum, qv_sums, *refs):
    outs, (full, proj, sems) = refs[:-3], refs[-3:]
    loading = attn_load(layer, weights, proj, sems)
    width = proj.shape[1] // 4
    dqkv = dqkv_ref[...]
    grad = t_dot(a[...], dqkv)
    grad_o = t_dot(dh[...], oqkv[:, :width])
    full[...] = jnp.concatenate([grad_o, grad[:, width:]], axis=1)
    wait_all(loading)
    da = dot_t(dqkv, proj[...])
    normed, _ = norm_rows(x[...].astype(F32))
    sums = jnp.concatenate(
        [
            jnp.sum(da * normed, axis=0, keepdims=True),
            jnp.sum(da, axis=0, keepdims=True),
            sums_mid[...],
            hidden_sum[...],
        ],
        axis=0,
    )
    rows = full.shape[0] // dp
    half = rows // 2
    first = meta[0] == 0
    beyond = jnp.zeros((7, full.shape[1]), F32)
    fill = lambda v: jnp.concatenate([v, jnp.zeros((v.shape[0], full.shape[1] - v.shape[1]), F32)], axis=1)
    for j in range(dp):
        little = jnp.concatenate(
            [fill(sums[:, j * rows : (j + 1) * rows]), fill(qv_sums[...]), beyond], axis=0
        )
        low, high = (full[(2 * j + i) * half : (2 * j + i + 1) * half] for i in range(2))
        if len(outs) == 1:
            outs[0][j] = jnp.concatenate([low, high, little], axis=0).astype(BF16)
        else:
            for out, values in zip(outs, (jnp.where(first, low, high), jnp.where(first, high, low))):
                out[j] = jnp.concatenate([values, little], axis=0).astype(BF16)


def last_body(n, *refs):
    dh, x, own, others, params = refs[0], refs[1], refs[2], refs[3 : n + 2], refs[n + 2]
    h, y_own, y_params, out, y_out = refs[n + 3 :]
    rows = own.shape[0]
    da, y = own[...], h[...] + y_own[...] + y_params[5:6]
    for ref in others:
        da = da + ref[:rows].astype(F32)
        y = y + ref[rows:].astype(F32)
    y_out[...] = y.astype(BF16)
    normed, inverse = norm_rows(x[...].astype(F32))
    out[...] = dh[...] + norm_back(da, normed, inverse, params[0:1])


def end_back_body(n, *refs):
    dh, x, own, others, params = refs[0], refs[1], refs[2], refs[3 : n + 2], refs[n + 2]
    out, low_out = refs[n + 3 :]
    da = summed(own, others)
    normed, inverse = norm_rows(x[...].astype(F32))
    grad = dh[...] + norm_back(da, normed, inverse, params[0:1])
    out[...] = grad
    low_out[...] = grad.astype(BF16)


def prepare_body(meta, w_qkv, w_out, w_fc1, w_fc2, attn_out, keep, send):
    attn_out[...] = jnp.concatenate([w_out[...].T, w_qkv[0], w_qkv[1], w_qkv[2]], axis=1)
    half = keep.shape[1]
    first = meta[0] == 0
    for g, values in enumerate((w_fc1[...], w_fc2[...])):
        low, high = values[:half], values[half:]
        keep[g] = jnp.where(first, low, high)
        send[g] = jnp.where(first, high, low)


def params_body(meta, mine, other, *outs):
    first = meta[0] == 0
    for out, flipped in zip(outs, (False, True)):
        pair = (other, mine) if flipped else (mine, other)
        values = [jnp.where(first, pair[0][j].astype(F32), pair[1][j].astype(F32)) for j in range(mine.shape[0])]
        out[0:7] = jnp.concatenate([v[0:7] for v in values], axis=1)
        cols = out.shape[1] // 4 // len(values)
        none = jnp.zeros((1, cols * len(values)), F32)
        out[7:8] = jnp.concatenate(
            [none, *(v[7:8, :cols] for v in values), none, *(v[8:9, :cols] for v in values)], axis=1
        )


def join_body(dp, *refs):
    keeps, sends, out = refs[: len(refs) // 2], refs[len(refs) // 2 : -1], refs[-1]
    for j in range(dp):
        out[j] = jnp.concatenate(
            [
                (keep[j].astype(F32) + send[j].astype(F32)).astype(BF16)
                for keep, send in zip(keeps, sends)
            ],
            axis=0,
        )


def split_body(meta, grad, received, own, *outs):
    for k, out in enumerate((own, *outs)):
        j = meta[1] ^ k
        out[...] = (grad[j].astype(F32) + received[j].astype(F32)).astype(out.dtype)


def turn_body(meta, mlp_1, mix, out):
    rows, half = mlp_1.shape[0], mlp_1.shape[0] // 2
    first = meta[0] == 0
    out[:rows] = jnp.where(first, mlp_1[...], mix[:rows])
    out[rows:] = mix[rows : rows + half]


def small_body(count, meta, mix, own, *refs):
    others, little, pieces = refs[:count], refs[count], refs[count + 1 :]
    total = mix[mix.shape[0] - 16 :].astype(F32)
    alone = own[own.shape[0] - 16 :]
    for ref in others:
        alone = alone + ref[ref.shape[0] - 16 :].astype(F32)
    total = jnp.where(meta[0] == 0, alone, total)
    little[...] = total
    share = pieces[0].shape[1]
    for k, out in enumerate(pieces):
        blocks = [
            jnp.where(meta[2] ^ k == j, total[0:6, j * share : (j + 1) * share], 0.0)
            for j in range(len(pieces))
        ]
        out[...] = sum(blocks[1:], blocks[0])


def finish_body(count, meta, mlp_1, mix, received, own, *refs):
    others, (qkv_out, out_out, fc1_out, fc2_out, attn) = refs[:count], refs[count:]
    first = meta[0] == 0
    rows, half = mlp_1.shape[0], mlp_1.shape[0] // 2

    def both(mine, theirs):
        mine, theirs = mine.astype(F32), theirs.astype(F32)
        return jnp.concatenate(
            [jnp.where(first, mine, theirs), jnp.where(first, theirs, mine)], axis=0
        )

    for out, at in ((fc1_out, slice(0, half)), (fc2_out, slice(half, rows))):
        out[...] = both(jnp.where(first, mix[at], mlp_1[at]), received[at])
    last = slice(rows, rows + half)

    @pl.when(first)
    def _():
        total = own[:rows]
        for ref in others:
            total = total + ref[:rows].astype(F32)
        attn[...] = total

    @pl.when(jnp.logical_not(first))
    def _():
        attn[...] = both(mix[last], received[last])

    width = attn.shape[1] // 4
    values = attn[...]
    out_out[...] = values[:, :width].T
    for i in range(3):
        qkv_out[i] = values[:, (i + 1) * width : (i + 2) * width]


def shards(sizes, inputs, cotangent, segments, row_params, qv_bias, w_qkv, w_out, fc1_bias, w_fc1, w_fc2):
    sections, dp, tensor = sizes
    s, d, t = (lax.axis_index(axis) for axis in ("section", "dp", "tensor"))
    smem = pl.BlockSpec(memory_space=pltpu.SMEM)
    vmem = pl.BlockSpec(memory_space=pltpu.VMEM)
    hbm = pl.BlockSpec(memory_space=pltpu.HBM)
    rows, width = inputs.shape[2], inputs.shape[3]
    tokens = rows * tensor
    head_cols, hidden = w_qkv.shape[3], w_fc1.shape[2]
    direct = dp <= 4 and w_qkv.shape[3] * dp == inputs.shape[3]
    pieces = dp if direct else 1
    meta = jnp.stack([s, d, t]).astype(jnp.int32)
    layer_first = s == 0

    def to_tensor(values):
        return [
            lax.ppermute(v, "tensor", [(i, i ^ k) for i in range(tensor)])
            for k, v in enumerate(values, 1)
        ]

    def everywhere(own):
        return [own, *to_tensor([own] * (tensor - 1))]

    def to_dp(values, layer):
        return [
            lax.ppermute(
                v, ("section", "dp"), [(layer * dp + i, layer * dp + (i ^ k)) for i in range(dp)]
            )
            for k, v in enumerate(values, 1)
        ]

    def to_other(value, source):
        return lax.ppermute(value, "section", [(source, 1 - source)])

    def pull(v, i):
        return lax.dynamic_index_in_dim(v, i, 0, keepdims=False, allow_negative_indices=False)

    mine = lambda v: pull(v[0], s)
    xs = everywhere(mine(inputs))
    cots = everywhere(mine(cotangent))
    ids = mine(segments).reshape(tensor, rows)
    order = [t ^ k for k in range(tensor)]
    ids = jnp.concatenate([pull(ids, i) for i in order])
    place = jnp.concatenate([i * rows + jnp.arange(rows, dtype=jnp.int32) for i in order])
    mask = ((ids[:, None] == ids[None, :]) & (place[None, :] <= place[:, None])).astype(F32)

    piece = width // dp
    pad = lambda v: jnp.pad(v, ((0, 0), (0, piece - v.shape[1])))
    small = jnp.concatenate([row_params[0], fc1_bias[0], pad(qv_bias[0, :, 0])], axis=0)
    small = jnp.pad(small, ((0, 16 - small.shape[0]), (0, 0)))
    if direct:
        found = [
            small,
            *(lax.ppermute(small, "dp", [(i, i ^ k) for i in range(dp)]) for k in range(1, dp)),
        ]
        small = jnp.stack(
            [sum(jnp.where(d ^ k == j, v, jnp.zeros_like(v)) for k, v in enumerate(found)) for j in range(dp)]
        )
    else:
        small = lax.all_gather(small, "dp", axis=0)
    other = lax.ppermute(small, "section", [(0, 1), (1, 0)])
    if direct:
        smalls = call(
            params_body, [struct((8, width), F32)] * 2, "params", 0, [meta, small, other],
            [smem, vmem, vmem],
        )
    else:
        smalls = []
        for values in (jnp.where(layer_first, small, other), jnp.where(layer_first, other, small)):
            values = values.astype(F32)
            whole = values.transpose(1, 0, 2).reshape(16, width)
            qv = values[:, 7:9, : head_cols // dp].transpose(1, 0, 2).reshape(2, head_cols)
            none = jnp.zeros((1, head_cols), F32)
            bias = jnp.concatenate([none, qv[0:1], none, qv[1:2]], axis=1)
            smalls.append(jnp.concatenate([whole[:7], bias], axis=0))

    half = piece // 2
    attn_piece, keep, send = call(
        prepare_body,
        [struct((piece, 4 * head_cols), BF16)] + [struct((2, half, hidden), BF16)] * 2,
        "prepare", 0, [meta, *(far(v) for v in (w_qkv[0], w_out[0], w_fc1[0], w_fc2[0].T))],
        [smem] + [vmem] * 4,
    )
    here = ("section", "dp")
    attn_w = far(lax.all_gather(attn_piece, here, axis=0, tiled=True).reshape(2, width, -1))
    other = lax.ppermute(send, "section", [(0, 1), (1, 0)])
    mlp_w = []
    for part in (jnp.where(layer_first, keep, other), jnp.where(layer_first, other, keep)):
        whole = lax.all_gather(part.reshape(2 * half, hidden), here, axis=0, tiled=True)
        whole = whole.reshape(2, dp, 2, half, hidden)
        if half % 16:
            whole = whole.transpose(2, 1, 0, 3, 4).reshape(1, 1, 2, width, hidden)
        mlp_w.append(far(whole))
    stacks, count, _, part_rows, _ = mlp_w[0].shape
    mlp_room = [
        pltpu.VMEM((2, count, stacks * part_rows, hidden), BF16),
        pltpu.SemaphoreType.DMA((stacks, 2)),
    ]

    attn_room = [pltpu.VMEM((width, 4 * head_cols), BF16), pltpu.SemaphoreType.DMA((2,))]
    blocks = [struct((rows, width), F32)] + [struct((rows, width), BF16)] * (tensor - 1)
    late_blocks = [kept(v.shape, v.dtype) for v in blocks]
    unit = 2 * tokens * width * width

    saved = []
    outputs = []
    for layer in range(2):
        params = smalls[layer]
        x_all, a, oqkv, lse, own, *away = call(
            functools.partial(attn_fwd_body, tensor, layer),
            [
                kept((tokens, width), BF16),
                kept((tokens, width), BF16),
                kept((tokens, 4 * head_cols), BF16),
                kept((tokens, head_cols // HEAD_DIM), F32),
                *blocks,
            ],
            "attn_fwd", 2 * unit, [*xs, params, mask, attn_w],
            [vmem] * (tensor + 2) + [hbm], attn_room,
        )
        h, c = call(
            functools.partial(middle_body, tensor),
            [kept((rows, width), F32), struct((rows, width), BF16)],
            "middle", 0, [xs[0], own, *to_tensor(away), params],
        )
        late = layer == 1
        c_all, m, der, own, *away = call(
            functools.partial(mlp_fwd_body, tensor),
            [
                kept((tokens, width), BF16),
                kept((tokens, hidden), BF16),
                kept((tokens, hidden), F32),
                *(late_blocks if late else blocks),
            ],
            "mlp_fwd", 2 * unit, [*everywhere(c), params, mlp_w[layer]],
            [vmem] * (tensor + 1) + [hbm], mlp_room,
        )
        saved.append((xs[0], x_all, a, oqkv, lse, h, c_all, m, der))
        if late:
            carried = (own, away)
            continue
        (y,) = call(
            functools.partial(end_body, tensor),
            [struct((rows, width), BF16)],
            "end", 0, [far(h), own, *to_tensor(away), params],
        )
        outputs.append(y)
        xs = everywhere(y)

    swap = lambda v: lax.ppermute(v, "section", [(0, 1), (1, 0)])

    def joined_halves(pairs, after=()):
        keeps, sends = [p[0] for p in pairs], [swap(p[1]) for p in pairs]
        rows_each = sum(k.shape[1] for k in keeps)
        (joined,) = call(
            functools.partial(join_body, dp),
            [struct((dp, rows_each, hidden), BF16)],
            "join", 0, [*keeps, *sends], after=after,
        )
        return joined

    def over_dp(joined):
        joined = joined.reshape(-1, hidden)
        return lax.psum_scatter(joined, "dp", scatter_dimension=0, tiled=True)

    input_grads = [None] * 2
    pairs = []
    extra = []
    e, es = cots[0], cots
    for layer in (1, 0):
        params = smalls[layer]
        x, x_all, a, oqkv, lse, h, c_all, m, der = saved[layer]
        e_all, du, hidden_sum, own, *away = call(
            functools.partial(mlp_bwd_body, tensor),
            [
                kept((tokens, width), BF16),
                kept((tokens, hidden), BF16),
                kept((1, hidden), F32),
                *blocks,
            ],
            "mlp_bwd", 2 * unit, [*es, far(der), mlp_w[layer]],
            [vmem] * (tensor + 1) + [hbm], mlp_room, extra,
        )
        received = to_tensor(away)
        mlp_grads = functools.partial(
            call,
            functools.partial(mlp_grads_body, dp),
            [struct((dp, 2 * half, hidden), BF16)] * 2,
            "mlp_grads", 2 * unit, [meta, far(c_all), far(e_all), far(du), far(m)],
            [smem] + [vmem] * 4, [pltpu.VMEM((2, width, hidden), F32)],
        )
        mlp_pair = mlp_grads(received)
        dh, dh_low, sums_mid = call(
            functools.partial(middle_back_body, tensor),
            [kept((rows, width), F32), struct((rows, width), BF16), kept((4, width), F32)],
            "middle_back", 0, [e, far(h), own, *received, params],
            after=[mlp_pair[0]],
        )
        dhs = everywhere(dh_low)
        if layer == 1:
            joined = joined_halves([mlp_pair], dhs[1:])
            mlp_1 = over_dp(joined)
        else:
            joined = joined_halves([mlp_pair, *pairs], [*dhs[1:], mlp_1])
            mix = over_dp(joined)
        dh_all, dqkv, qv_sums, own, *away = call(
            functools.partial(attn_bwd_body, tensor, layer),
            [
                kept((tokens, width), BF16),
                kept((tokens, 4 * head_cols), BF16),
                kept((2, head_cols), F32),
                blocks[0],
                *[struct((rows if layer == 1 else 2 * rows, width), BF16)] * (tensor - 1),
            ],
            "attn_bwd", 2 * unit,
            [*dhs, attn_w, far(oqkv), far(lse), mask, *(() if layer == 1 else map(far, carried[1]))],
            [vmem] * tensor + [hbm] + [vmem] * (3 if layer == 1 else tensor + 2),
            attn_room, [joined],
        )
        received = to_tensor(away)
        whole = direct and layer == 0
        attn_grads = functools.partial(
            call,
            functools.partial(attn_grads_body, layer, dp),
            [struct((dp, piece + 16, 4 * head_cols), BF16)]
            if whole
            else [struct((dp, half + 16, 4 * head_cols), BF16)] * 2,
            "attn_grads", 3 * unit,
            [
                meta, far(x_all), far(dh_all), far(a), far(oqkv), far(dqkv), attn_w,
                far(sums_mid), far(hidden_sum), far(qv_sums),
            ],
            [smem] + [vmem] * 5 + [hbm] + [vmem] * 3,
            [pltpu.VMEM((width, 4 * head_cols), F32), *attn_room],
        )
        if layer == 1:
            pass
        elif direct:
            (grad,) = attn_grads()
            attn_own, *attn_away = call(
                split_body,
                [struct((piece + 16, hidden), F32)]
                + [struct((piece + 16, hidden), BF16)] * (dp - 1),
                "split", 0, [meta, grad, to_other(grad, 1)], [smem, vmem, vmem],
            )
            attn_others = to_dp(attn_away, 0)
            follows = attn_own
        else:
            attn_0 = over_dp(joined_halves([attn_grads()]))
            there = swap(attn_0)
            attn_own = jnp.concatenate(
                [jnp.where(layer_first, v[:half], w[:half]) for v, w in ((attn_0, there), (there, attn_0))]
                + [attn_0[half:]]
            ).astype(F32)
            attn_others = []
            follows = attn_own
        if layer == 1:
            e, e_low = call(
                functools.partial(end_back_body, tensor),
                [struct((rows, width), F32), struct((rows, width), BF16)],
                "end_back", 0, [far(dh), x, own, *received, params],
            )
            es = everywhere(e_low)
            attn_pair = attn_grads(es[1:2])
            pairs.append(attn_pair)
            extra = [attn_pair[0]]
        else:
            e, y = call(
                functools.partial(last_body, tensor),
                [struct((rows, width), F32), struct((rows, width), BF16)],
                "last", 0,
                [far(dh), x, own, *received, params, far(saved[1][5]), far(carried[0]), smalls[1]],
                after=[follows],
            )
            outputs.append(y)
        input_grads[layer] = e

    pick = lambda pair: jnp.where(layer_first, pair[0], pair[1])
    flip = lambda pair: jnp.where(layer_first, pair[1], pair[0])
    def both(pair):
        here, there = pick(pair), swap(flip(pair))
        return jnp.stack([jnp.where(layer_first, here, there), jnp.where(layer_first, there, here)])[None, None]

    block_out = both(outputs)
    grads_out = both(input_grads)
    share = piece // tensor
    (sent,) = call(
        turn_body, [struct((3 * half, hidden), BF16)], "turn", 0, [meta, mlp_1, mix],
        [smem, vmem, vmem],
    )
    received = swap(sent)
    total, row_own, *row_away = call(
        functools.partial(small_body, len(attn_others)),
        [struct((16, width), F32)] + [struct((6, share), F32)] * tensor,
        "small", 0, [meta, mix, attn_own, *attn_others],
        [smem] + [vmem] * (2 + len(attn_others)),
    )
    row_grad = row_own + sum(to_tensor(row_away))
    qv_cols = head_cols // dp
    qv_grad = lax.dynamic_slice(
        total, (7, d * qv_cols), (2, qv_cols), allow_negative_indices=False
    )
    w_qkv_grad, w_out_grad, w_fc1_grad, w_fc2_grad = call(
        functools.partial(finish_body, len(attn_others)),
        [
            struct((3, piece, head_cols), F32),
            struct((head_cols, piece), F32),
            struct((piece, hidden), F32),
            struct((piece, hidden), F32),
        ],
        "finish", 0, [meta, mlp_1, mix, received, attn_own, *attn_others],
        [smem] + [vmem] * (4 + len(attn_others)),
        [pltpu.VMEM((piece, 4 * head_cols), F32)],
    )
    return (
        block_out,
        grads_out,
        row_grad[None],
        qv_grad.reshape(1, 2, 1, qv_cols),
        w_qkv_grad[None],
        w_out_grad[None],
        total[6:7, :piece][None],
        w_fc1_grad[None],
        w_fc2_grad.T[None],
    )


def solution(mesh):
    sizes = tuple(mesh.shape[axis] for axis in ("section", "dp", "tensor"))
    placed = (
        P("dp", None, "tensor", None),
        P("dp", None, "tensor", None),
        P("dp", None, None),
        P("section", None, "dp"),
        P("section", None, "tensor", "dp"),
        P("section", None, "dp", "tensor"),
        P("section", "tensor", "dp"),
        P("section", "tensor", "dp"),
        P("section", "dp", "tensor"),
        P("section", "tensor", "dp"),
    )
    return jax.shard_map(
        functools.partial(shards, sizes),
        mesh=mesh,
        in_specs=placed,
        out_specs=(
            P("section", "dp", None, "tensor", None),
            P("section", "dp", None, "tensor", None),
            P("section", None, ("dp", "tensor")),
            P("section", None, "tensor", "dp"),
            P("section", None, "dp", "tensor"),
            P("section", "tensor", "dp"),
            P("section", "tensor", "dp"),
            P("section", "dp", "tensor"),
            P("section", "tensor", "dp"),
        ),
        check_vma=False,
    )
```

time: 990 us -> 268 us (0.27)
  waiting for transfers between devices: 543 us -> 101 us
  blocking collectives: 199 us -> 0 us
  matrix products: 98.6 us -> 0 us
  starting transfers between devices: 7.64 us -> 76.6 us
  Pallas kernels: 0 us -> 64 us
  local copies, waits for them, and re-layouts: 70.7 us -> 8.21 us
  other arithmetic: 40.7 us -> 2.81 us
    reduce_scatter x13 -> x2, waiting for transfers between devices: 264 us -> 3.64 us  [over_dp(): return lax.psum_scatter(joined, 'dp', scatter_dimension=0, tiled=True)]
    unnamed x27 -> x5, waiting for transfers between devices: 250 us -> 0.75 us
    all_gather x16 -> x0, blocking collectives: 188 us -> none  [the longest x3 34.3 us: layer_backward(): grad_rows = lax.all_gather(grad_low, 'tensor', axis=0, tiled=True)]
    dot_general x75 -> x0, matrix products: 98.6 us -> none  [the longest x18 24.6 us: inner_rows(): lax.dot_general(left, right, (((0,), (0,)), ((), ())), preferred_element_...]
    ppermute x4 -> x63, starting transfers between devices: 6.22 us -> 76.2 us  [the longest x48 55.7 us: to_tensor(): lax.ppermute(v, 'tensor', [(i, i ^ k) for i in range(tensor)])]
    pallas_call x0 -> x27, Pallas kernels: none -> 64 us  [call(): pl.pallas_call(body, out_shape=tuple(outs), in_specs=specs, out_specs=(vm...]
    ppermute x4 -> x63, waiting for transfers between devices: 5.21 us -> 65.3 us  [the longest x48 55.1 us: to_tensor(): lax.ppermute(v, 'tensor', [(i, i ^ k) for i in range(tensor)])]
    unnamed x402 -> x27, local copies, waits for them, and re-layouts: 42.1 us -> 6.87 us
  transfers between devices with their start and end apart: 25 -> 68, of which waited for: 21 -> 46; matrix products, arithmetic and copies ran while one was open for 10% -> 2% of each run, Pallas kernels for 0% -> 19%
where the time goes in v1:
time: 268 us; the launch traced here: 266 us
  waiting for transfers between devices  101 us (38%)
  starting transfers between devices  76.6 us (29%)
  Pallas kernels  64 us (24%)
  between operations  14.3 us (5%)
  local copies, waits for them, and re-layouts  8.21 us (3%)
  other arithmetic  2.81 us (1%)
    pallas_call x27, Pallas kernels, call(): pl.pallas_call(body, out_shape=tuple(outs), in_specs=specs, out_specs=(vm...  64 us
    ppermute x48, starting transfers between devices, to_tensor(): lax.ppermute(v, 'tensor', [(i, i ^ k) for i in range(tensor)])  55.7 us
    ppermute x48, waiting for transfers between devices, to_tensor(): lax.ppermute(v, 'tensor', [(i, i ^ k) for i in range(tensor)])  55.1 us
    all_gather x1, waiting for transfers between devices, shards(): lax.all_gather(attn_piece, here, axis=0, tiled=True).reshape(2, width, -1)  17.8 us
    all_gather x2, waiting for transfers between devices, shards(): lax.all_gather(part.reshape(2 * half, hidden), here, axis=0, tiled=True)  13.1 us
    ppermute x3, starting transfers between devices, to_dp(): lax.ppermute(v, ('section', 'dp'), [(layer * dp + i, layer * dp + (i ^ k)...  10.1 us
    unnamed x27, local copies, waits for them, and re-layouts  6.87 us
    ppermute x3, waiting for transfers between devices, to_dp(): lax.ppermute(v, ('section', 'dp'), [(layer * dp + i, layer * dp + (i ^ k)...  6.11 us
  transfers between devices with their start and end apart: 68, of which 46 were waited for; matrix products, arithmetic and copies ran while one was open for 2% of the time, Pallas kernels for 19%

profile of v1, /device:TPU:0, one launch (start us, length us, event | category | flops | bytes accessed | tf_op | source)
XLA Modules:
  0.0 266.5 jit_solution(14127581504335086000)
XLA Ops:
  12.9 4.0 %collective-permute-start.4 = (bf16[16,192]{1,0:T(8,128)(2,1)S(1)}, bf16[16,192]{1,0:T(8,128)(2,1)S(1)}, u32[]{:S(2)}, u32[]{:S(2)}) collective-permute-start(bf16[16,192]{1,0:T(8,128)(2,1)S(1)} %pad.9), channel_id=1, source_target_pairs={{0,8},{4,12},{8,0},{12,4},{1,9},{5,13},{9,1},{13,5},{2,10},{6,14},... | collective-permute-start | bytes 18440 | tf_op jit(solution)/shard_map/ppermute | solution.py:499
  18.6 2.7 %collective-permute-start.2 = (bf16[64,768]{1,0:T(8,128)(2,1)S(1)}, bf16[64,768]{1,0:T(8,128)(2,1)S(1)}, u32[]{:S(2)}, u32[]{:S(2)}) collective-permute-start(bf16[64,768]{1,0:T(8,128)(2,1)S(1)} %dynamic-slice_bitcast_fusion.1.refs_0_.refs_1_), channel_id=1, source_target_pairs={{0,3},{1,2},{2,1},{3,0},{4,7},{5,6},{6,5},{7,4},{8,11},{9,10},{10,... | collective-permute-start | bytes 294920 | tf_op jit(solution)/shard_map/ppermute | solution.py:462
  26.7 17.8 %all-gather.4.cloned.1.call-done = bf16[1536,768]{1,0:T(8,128)(2,1)} async-done(((bf16[192,768]{1,0:T(8,128)(2,1)}), bf16[1536,768]{1,0:T(8,128)(2,1)}) %all-gather.4.cloned.1.call-update) | async-done | bytes 2359312 | tf_op jit(solution)/shard_map/all_gather | solution.py:530
  44.5 3.5 %attn_fwd.2 = (bf16[256,768]{1,0:T(8,128)(2,1)}, bf16[256,768]{1,0:T(8,128)(2,1)}, bf16[256,768]{1,0:T(8,128)(2,1)}, f32[256,3]{1,0:T(8,128)}, f32[64,768]{1,0:T...) custom-call(bf16[64,768]{1,0:T(8,128)(2,1)S(1)} %dynamic-slice_bitcast_fusion.1.r, ...), custom_call_target="tpu_custom_call" | custom-call | flops 603979776 | bytes 4713472 | tf_op jit(solution)/shard_map/attn_fwd/pallas_call | solution.py:88
  60.9 2.6 collective-permute-done.12.refs_3_
  64.4 13.1 %all-gather.6.cloned.1.call-done = bf16[1536,768]{1,0:T(8,128)(2,1)} async-done(((bf16[192,768]{1,0:T(8,128)(2,1)}), bf16[1536,768]{1,0:T(8,128)(2,1)}) %all-gather.6.cloned.1.call-update) | async-done | bytes 2359312 | tf_op jit(solution)/shard_map/all_gather | solution.py:534
  77.5 3.4 %mlp_fwd.2 = (bf16[256,768]{1,0:T(8,128)(2,1)}, bf16[256,768]{1,0:T(8,128)(2,1)}, f32[256,768]{1,0:T(8,128)}, f32[64,768]{1,0:T(8,128)S(1)}, bf16[64,768]{1,0:T(...) custom-call(bf16[64,768]{1,0:T(8,128)(2,1)S(1)} %get-tuple-element.112.refs_0_, ...), custom_call_target="tpu_custom_call" | custom-call | flops 603979776 | bytes 4841472 | tf_op jit(solution)/shard_map/mlp_fwd/pallas_call | solution.py:88
  94.0 2.6 collective-permute-done.19.refs_3_
  97.5 3.6 %attn_fwd.3 = (bf16[256,768]{1,0:T(8,128)(2,1)}, bf16[256,768]{1,0:T(8,128)(2,1)}, bf16[256,768]{1,0:T(8,128)(2,1)}, f32[256,3]{1,0:T(8,128)}, f32[64,768]{1,0:T...) custom-call(bf16[64,768]{1,0:T(8,128)(2,1)S(1)} %end.1.refs_0_.refs_1_, ...), custom_call_target="tpu_custom_call" | custom-call | flops 603979776 | bytes 4713472 | tf_op jit(solution)/shard_map/attn_fwd/pallas_call | solution.py:88
  118.0 3.5 %mlp_fwd.3 = (bf16[256,768]{1,0:T(8,128)(2,1)}, bf16[256,768]{1,0:T(8,128)(2,1)}, f32[256,768]{1,0:T(8,128)}, f32[64,768]{1,0:T(8,128)}, bf16[64,768]{1,0:T(8,12...) custom-call(bf16[64,768]{1,0:T(8,128)(2,1)S(1)} %get-tuple-element.125.refs_0_, ...), custom_call_target="tpu_custom_call" | custom-call | flops 603979776 | bytes 4841472 | tf_op jit(solution)/shard_map/mlp_fwd/pallas_call | solution.py:88
  121.5 4.0 %mlp_bwd.2 = (bf16[256,768]{1,0:T(8,128)(2,1)}, bf16[256,768]{1,0:T(8,128)(2,1)}, f32[1,768]{1,0:T(1,128)}, f32[64,768]{1,0:T(8,128)S(1)}, bf16[64,768]{1,0:T(8,...) custom-call(bf16[64,768]{1,0:T(8,128)(2,1)S(1)} %dynamic-slice_bitcast_fusion.refs_0_, ...), custom_call_target="tpu_custom_call" | custom-call | flops 603979776 | bytes 4819968 | tf_op jit(solution)/shard_map/mlp_bwd/pallas_call | solution.py:88
  140.3 2.7 %collective-permute-done.34.refs_4_.refs_3_ = bf16[64,768]{1,0:T(8,128)(2,1)S(1)} collective-permute-done((bf16[64,768]{1,0:T(8,128)(2,1)S(1)}, bf16[64,768]{1,0:T(8,128)(2,1)S(1)}, u32[]{:S(2)}, u32[]{:S(2)}) %collective-permute-start.34) | collective-permute-done | bytes 98336 | tf_op jit(solution)/shard_map/ppermute | solution.py:462
  146.5 4.8 %attn_bwd.2 = (bf16[256,768]{1,0:T(8,128)(2,1)}, bf16[256,768]{1,0:T(8,128)(2,1)}, f32[2,192]{1,0:T(2,128)}, f32[64,768]{1,0:T(8,128)S(1)}, bf16[64,768]{1,0:T(8...) custom-call(bf16[64,768]{1,0:T(8,128)(2,1)S(1)} %get-tuple-element.137.refs_0_, ...), custom_call_target="tpu_custom_call" | custom-call | flops 603979776 | bytes 5870080 | tf_op jit(solution)/shard_map/attn_bwd/pallas_call | solution.py:88
  165.1 3.7 %attn_grads.2 = (bf16[4,112,768]{2,1,0:T(8,128)(2,1)S(1)}, bf16[4,112,768]{2,1,0:T(8,128)(2,1)S(1)}) custom-call(s32[3]{0:T(128)S(1)} %pad_add_fusion.2.meta.refs_0_, bf16[256,768]{1,0:T(8,128)(2,1)} %get-tuple-element.148.refs_1_, bf16[256,768]{1,0:T(8,128)(2,1)} %get-tuple-element.149.refs_2_, bf16[256,768]{1,0:T(8,128)(2,1)} %get-tuple-element.150.refs_3_, ...), custom_call_target="tpu_custom_call" | custom-call | flops 905969664 | bytes 5816844 | tf_op jit(solution)/shard_map/attn_grads/pallas_call | solution.py:88
  168.8 3.9 %mlp_bwd.3 = (bf16[256,768]{1,0:T(8,128)(2,1)}, bf16[256,768]{1,0:T(8,128)(2,1)}, f32[1,768]{1,0:T(1,128)}, f32[64,768]{1,0:T(8,128)S(1)}, bf16[64,768]{1,0:T(8,...) custom-call(bf16[64,768]{1,0:T(8,128)(2,1)S(1)} %get-tuple-element.146.refs_0_, ...), custom_call_target="tpu_custom_call" | custom-call | flops 603979776 | bytes 5508096 | tf_op jit(solution)/shard_map/mlp_bwd/pallas_call | solution.py:88
  188.7 3.0 %collective-permute-done.47.refs_6_.refs_3_ = bf16[64,768]{1,0:T(8,128)(2,1)S(1)} collective-permute-done((bf16[64,768]{1,0:T(8,128)(2,1)S(1)}, bf16[64,768]{1,0:T(8,128)(2,1)S(1)}, u32[]{:S(2)}, u32[]{:S(2)}) %collective-permute-start.47) | collective-permute-done | bytes 98336 | tf_op jit(solution)/shard_map/ppermute | solution.py:462
  199.9 5.4 %attn_bwd.3 = (bf16[256,768]{1,0:T(8,128)(2,1)}, bf16[256,768]{1,0:T(8,128)(2,1)}, f32[2,192]{1,0:T(2,128)}, f32[64,768]{1,0:T(8,128)S(1)}, bf16[128,768]{1,0:T(...) custom-call(bf16[64,768]{1,0:T(8,128)(2,1)S(1)} %get-tuple-element.166.refs_0_, ...), custom_call_target="tpu_custom_call" | custom-call | flops 603979776 | bytes 7148032 | tf_op jit(solution)/shard_map/attn_bwd/pallas_call | solution.py:88
  205.3 3.6 %attn_grads.3.grad = bf16[4,208,768]{2,1,0:T(8,128)(2,1)S(1)} custom-call(s32[3]{0:T(128)S(1)} %pad_add_fusion.2.meta.refs_0_, bf16[256,768]{1,0:T(8,128)(2,1)} %get-tuple-element.179.x, bf16[256,768]{1,0:T(8,128)(2,1)} %get-tuple-element.180.dh, bf16[256,768]{1,0:T(8,128)(2,1)} %get-tuple-element.181.a, bf16[256,768]{1,0:T(8,128)(2,1)} %get-tuple-element.167.refs_5_.oqkv, ...), custom_call_target="tpu_custom_call" | custom-call | flops 905969664 | bytes 5620236 | tf_op jit(solution)/shard_map/attn_grads/pallas_call | solution.py:88
  217.1 2.5 collective-permute-done.51.refs_4_
  225.5 2.8 %collective-permute-start.56 = (bf16[208,768]{1,0:T(8,128)(2,1)}, bf16[208,768]{1,0:T(8,128)(2,1)S(1)}, u32[]{:S(2)}, u32[]{:S(2)}) collective-permute-start(bf16[208,768]{1,0:T(8,128)(2,1)} %get-tuple-element.189), channel_id=1, source_target_pairs={{0,4},{4,0},{8,12},{12,8},{1,5},{5,1},{9,13},{13,9},{2,6},{6,2},{1... | collective-permute-start | bytes 958472 | tf_op jit(solution)/shard_map/ppermute | solution.py:471
  228.3 3.5 %collective-permute-start.57 = (bf16[208,768]{1,0:T(8,128)(2,1)}, bf16[208,768]{1,0:T(8,128)(2,1)S(1)}, u32[]{:S(2)}, u32[]{:S(2)}) collective-permute-start(bf16[208,768]{1,0:T(8,128)(2,1)} %get-tuple-element.190), channel_id=1, source_target_pairs={{0,8},{4,12},{8,0},{12,4},{1,9},{5,13},{9,1},{13,5},{2,10},{6,14},... | collective-permute-start | bytes 958472 | tf_op jit(solution)/shard_map/ppermute | solution.py:471
  231.7 3.9 %collective-permute-start.58 = (bf16[208,768]{1,0:T(8,128)(2,1)}, bf16[208,768]{1,0:T(8,128)(2,1)S(1)}, u32[]{:S(2)}, u32[]{:S(2)}) collective-permute-start(bf16[208,768]{1,0:T(8,128)(2,1)} %get-tuple-element.191), channel_id=1, source_target_pairs={{0,12},{4,8},{8,4},{12,0},{1,13},{5,9},{9,5},{13,1},{2,14},{6,10},... | collective-permute-start | bytes 958472 | tf_op jit(solution)/shard_map/ppermute | solution.py:471
  237.2 3.6 %reduce-scatter.5.cloned.1.call-done.mix = bf16[304,768]{1,0:T(8,128)(2,1)} async-done(((bf16[1216,768]{1,0:T(8,128)(2,1)}), bf16[304,768]{1,0:T(8,128)(2,1)}) %reduce-scatter.5.cloned.1.call-update) | async-done | bytes 466960 | tf_op jit(solution)/shard_map/reduce_scatter | solution.py:609
  243.2 5.4 %collective-permute-done.58.refs_2_ = bf16[208,768]{1,0:T(8,128)(2,1)S(1)} collective-permute-done((bf16[208,768]{1,0:T(8,128)(2,1)}, bf16[208,768]{1,0:T(8,128)(2,1)S(1)}, u32[]{:S(2)}, u32[]{:S(2)}) %collective-permute-start.58) | collective-permute-done | bytes 319520 | tf_op jit(solution)/shard_map/ppermute | solution.py:471
  (198 shorter events, 142.8 us)
Async XLA Ops:
  7.2 37.4 %all-gather.4.cloned.1.call-start = ((), (), s32[]{:S(2)}) async-start(), calls=%async_computation.2 | async-start | bytes 2654208 | tf_op jit(solution)/shard_map/all_gather | solution.py:530
  9.4 68.0 %all-gather.6.cloned.1.call-start = ((), (), s32[]{:S(2)}) async-start(), calls=%async_computation.3 | async-start | bytes 2654208 | tf_op jit(solution)/shard_map/all_gather | solution.py:534
  12.1 104.7 %all-gather.8.cloned.1.call-start = ((), (), s32[]{:S(2)}) async-start(), calls=%async_computation.4 | async-start | bytes 2654208 | tf_op jit(solution)/shard_map/all_gather | solution.py:534
  12.8 182.0 %reduce-scatter.3.cloned.1.call-start = ((), (), s32[]{:S(2)}) async-start(), calls=%async_computation.5 | async-start | bytes 1474560 | tf_op jit(solution)/shard_map/reduce_scatter | solution.py:609
  12.9 9.1 %collective-permute-start.4 = (bf16[16,192]{1,0:T(8,128)(2,1)S(1)}, bf16[16,192]{1,0:T(8,128)(2,1)S(1)}, u32[]{:S(2)}, u32[]{:S(2)}) collective-permute-start(bf16[16,192]{1,0:T(8,128)(2,1)S(1)} %pad.9), channel_id=1, source_target_pairs={{0,8},{4,12},{8,0},{12,4},{1,9},{5,13},{9,1},{13,5},{2,10},{6,14},... | collective-permute-start | bytes 18440 | tf_op jit(solution)/shard_map/ppermute | solution.py:499
  18.6 7.5 %collective-permute-start.2 = (bf16[64,768]{1,0:T(8,128)(2,1)S(1)}, bf16[64,768]{1,0:T(8,128)(2,1)S(1)}, u32[]{:S(2)}, u32[]{:S(2)}) collective-permute-start(bf16[64,768]{1,0:T(8,128)(2,1)S(1)} %dynamic-slice_bitcast_fusion.1.refs_0_.refs_1_), channel_id=1, source_target_pairs={{0,3},{1,2},{2,1},{3,0},{4,7},{5,6},{6,5},{7,4},{8,11},{9,10},{10,... | collective-permute-start | bytes 294920 | tf_op jit(solution)/shard_map/ppermute | solution.py:462
  109.7 6.5 %collective-permute-start.28 = (bf16[64,768]{1,0:T(8,128)(2,1)S(1)}, bf16[64,768]{1,0:T(8,128)(2,1)S(1)}, u32[]{:S(2)}, u32[]{:S(2)}) collective-permute-start(bf16[64,768]{1,0:T(8,128)(2,1)S(1)} %get-tuple-element.125.refs_0_), channel_id=1, source_target_pairs={{0,3},{1,2},{2,1},{3,0},{4,7},{5,6},{6,5},{7,4},{8,11},{9,10},{10,... | collective-permute-start | bytes 294920 | tf_op jit(solution)/shard_map/ppermute | solution.py:462
  110.9 7.1 %collective-permute-start.27 = (bf16[64,768]{1,0:T(8,128)(2,1)S(1)}, bf16[64,768]{1,0:T(8,128)(2,1)S(1)}, u32[]{:S(2)}, u32[]{:S(2)}) collective-permute-start(bf16[64,768]{1,0:T(8,128)(2,1)S(1)} %get-tuple-element.125.refs_0_), channel_id=1, source_target_pairs={{0,2},{1,3},{2,0},{3,1},{4,6},{5,7},{6,4},{7,5},{8,10},{9,11},{10,... | collective-permute-start | bytes 294920 | tf_op jit(solution)/shard_map/ppermute | solution.py:462
  113.2 8.2 %collective-permute-start.25 = (bf16[64,768]{1,0:T(8,128)(2,1)S(1)}, bf16[64,768]{1,0:T(8,128)(2,1)S(1)}, u32[]{:S(2)}, u32[]{:S(2)}) collective-permute-start(bf16[64,768]{1,0:T(8,128)(2,1)S(1)} %dynamic-slice_bitcast_fusion.refs_0_), channel_id=1, source_target_pairs={{0,3},{1,2},{2,1},{3,0},{4,7},{5,6},{6,5},{7,4},{8,11},{9,10},{10,... | collective-permute-start | bytes 294920 | tf_op jit(solution)/shard_map/ppermute | solution.py:462
  114.5 7.0 %collective-permute-start.24 = (bf16[64,768]{1,0:T(8,128)(2,1)S(1)}, bf16[64,768]{1,0:T(8,128)(2,1)S(1)}, u32[]{:S(2)}, u32[]{:S(2)}) collective-permute-start(bf16[64,768]{1,0:T(8,128)(2,1)S(1)} %dynamic-slice_bitcast_fusion.refs_0_), channel_id=1, source_target_pairs={{0,2},{1,3},{2,0},{3,1},{4,6},{5,7},{6,4},{7,5},{8,10},{9,11},{10,... | collective-permute-start | bytes 294920 | tf_op jit(solution)/shard_map/ppermute | solution.py:462
  134.8 10.2 %collective-permute-start.35 = (bf16[4,192,768]{2,1,0:T(8,128)(2,1)S(1)}, bf16[4,192,768]{2,1,0:T(8,128)(2,1)S(1)}, u32[]{:S(2)}, u32[]{:S(2)}) collective-permute-start(bf16[4,192,768]{2,1,0:T(8,128)(2,1)S(1)} %get-tuple-element.140), channel_id=1, source_target_pairs={{0,16},{16,0},{1,17},{17,1},{2,18},{18,2},{3,19},{19,3},{4,20},{20... | collective-permute-start | bytes 3538952 | tf_op jit(solution)/shard_map/ppermute | solution.py:595
  146.3 94.5 %reduce-scatter.5.cloned.1.call-start = ((), (), s32[]{:S(2)}) async-start(), calls=%async_computation.6 | async-start | bytes 2334720 | tf_op jit(solution)/shard_map/reduce_scatter | solution.py:609
  161.4 7.3 %collective-permute-start.41 = (bf16[64,768]{1,0:T(8,128)(2,1)S(1)}, bf16[64,768]{1,0:T(8,128)(2,1)S(1)}, u32[]{:S(2)}, u32[]{:S(2)}) collective-permute-start(bf16[64,768]{1,0:T(8,128)(2,1)S(1)} %get-tuple-element.146.refs_0_), channel_id=1, source_target_pairs={{0,3},{1,2},{2,1},{3,0},{4,7},{5,6},{6,5},{7,4},{8,11},{9,10},{10,... | collective-permute-start | bytes 294920 | tf_op jit(solution)/shard_map/ppermute | solution.py:462
  182.7 11.2 %collective-permute-start.48 = (bf16[4,192,768]{2,1,0:T(8,128)(2,1)S(1)}, bf16[4,192,768]{2,1,0:T(8,128)(2,1)S(1)}, u32[]{:S(2)}, u32[]{:S(2)}) collective-permute-start(bf16[4,192,768]{2,1,0:T(8,128)(2,1)S(1)} %get-tuple-element.172), channel_id=1, source_target_pairs={{0,16},{16,0},{1,17},{17,1},{2,18},{18,2},{3,19},{19,3},{4,20},{20... | collective-permute-start | bytes 3538952 | tf_op jit(solution)/shard_map/ppermute | solution.py:595
  182.8 10.2 %collective-permute-start.49 = (bf16[4,112,768]{2,1,0:T(8,128)(2,1)S(1)}, bf16[4,112,768]{2,1,0:T(8,128)(2,1)S(1)}, u32[]{:S(2)}, u32[]{:S(2)}) collective-permute-start(bf16[4,112,768]{2,1,0:T(8,128)(2,1)S(1)} %get-tuple-element.173), channel_id=1, source_target_pairs={{0,16},{16,0},{1,17},{17,1},{2,18},{18,2},{3,19},{19,3},{4,20},{20... | collective-permute-start | bytes 2064392 | tf_op jit(solution)/shard_map/ppermute | solution.py:595
  210.2 6.9 %collective-permute-start.50 = (bf16[128,768]{1,0:T(8,128)(2,1)}, bf16[128,768]{1,0:T(8,128)(2,1)S(1)}, u32[]{:S(2)}, u32[]{:S(2)}) collective-permute-start(bf16[128,768]{1,0:T(8,128)(2,1)} %get-tuple-element.175), channel_id=1, source_target_pairs={{0,1},{1,0},{2,3},{3,2},{4,5},{5,4},{6,7},{7,6},{8,9},{9,8},{10,11... | collective-permute-start | bytes 589832 | tf_op jit(solution)/shard_map/ppermute | solution.py:462
  211.4 8.2 %collective-permute-start.51 = (bf16[128,768]{1,0:T(8,128)(2,1)}, bf16[128,768]{1,0:T(8,128)(2,1)S(1)}, u32[]{:S(2)}, u32[]{:S(2)}) collective-permute-start(bf16[128,768]{1,0:T(8,128)(2,1)} %get-tuple-element.176), channel_id=1, source_target_pairs={{0,2},{1,3},{2,0},{3,1},{4,6},{5,7},{6,4},{7,5},{8,10},{9,11},{10,... | collective-permute-start | bytes 589832 | tf_op jit(solution)/shard_map/ppermute | solution.py:462
  212.3 9.4 %collective-permute-start.52 = (bf16[128,768]{1,0:T(8,128)(2,1)}, bf16[128,768]{1,0:T(8,128)(2,1)S(1)}, u32[]{:S(2)}, u32[]{:S(2)}) collective-permute-start(bf16[128,768]{1,0:T(8,128)(2,1)} %get-tuple-element.177), channel_id=1, source_target_pairs={{0,3},{1,2},{2,1},{3,0},{4,7},{5,6},{6,5},{7,4},{8,11},{9,10},{10,... | collective-permute-start | bytes 589832 | tf_op jit(solution)/shard_map/ppermute | solution.py:462
  223.2 12.4 %collective-permute-start.54 = (bf16[64,768]{1,0:T(8,128)(2,1)S(1)}, bf16[64,768]{1,0:T(8,128)(2,1)S(1)}, u32[]{:S(2)}, u32[]{:S(2)}) collective-permute-start(bf16[64,768]{1,0:T(8,128)(2,1)S(1)} %broadcast_select_fusion.4), channel_id=1, source_target_pairs={{0,16},{16,0},{1,17},{17,1},{2,18},{18,2},{3,19},{19,3},{4,20},{20... | collective-permute-start | bytes 294920 | tf_op jit(solution)/shard_map/ppermute | solution.py:595
  225.4 11.0 %collective-permute-start.55 = (f32[64,768]{1,0:T(8,128)S(1)}, f32[64,768]{1,0:T(8,128)S(1)}, u32[]{:S(2)}, u32[]{:S(2)}) collective-permute-start(f32[64,768]{1,0:T(8,128)S(1)} %broadcast_select_fusion.2), channel_id=1, source_target_pairs={{0,16},{16,0},{1,17},{17,1},{2,18},{18,2},{3,19},{19,3},{4,20},{20... | collective-permute-start | bytes 589832 | tf_op jit(solution)/shard_map/ppermute | solution.py:595
  225.5 17.7 %collective-permute-start.56 = (bf16[208,768]{1,0:T(8,128)(2,1)}, bf16[208,768]{1,0:T(8,128)(2,1)S(1)}, u32[]{:S(2)}, u32[]{:S(2)}) collective-permute-start(bf16[208,768]{1,0:T(8,128)(2,1)} %get-tuple-element.189), channel_id=1, source_target_pairs={{0,4},{4,0},{8,12},{12,8},{1,5},{5,1},{9,13},{13,9},{2,6},{6,2},{1... | collective-permute-start | bytes 958472 | tf_op jit(solution)/shard_map/ppermute | solution.py:471
  228.3 15.0 %collective-permute-start.57 = (bf16[208,768]{1,0:T(8,128)(2,1)}, bf16[208,768]{1,0:T(8,128)(2,1)S(1)}, u32[]{:S(2)}, u32[]{:S(2)}) collective-permute-start(bf16[208,768]{1,0:T(8,128)(2,1)} %get-tuple-element.190), channel_id=1, source_target_pairs={{0,8},{4,12},{8,0},{12,4},{1,9},{5,13},{9,1},{13,5},{2,10},{6,14},... | collective-permute-start | bytes 958472 | tf_op jit(solution)/shard_map/ppermute | solution.py:471
  231.7 16.9 %collective-permute-start.58 = (bf16[208,768]{1,0:T(8,128)(2,1)}, bf16[208,768]{1,0:T(8,128)(2,1)S(1)}, u32[]{:S(2)}, u32[]{:S(2)}) collective-permute-start(bf16[208,768]{1,0:T(8,128)(2,1)} %get-tuple-element.191), channel_id=1, source_target_pairs={{0,12},{4,8},{8,4},{12,0},{1,13},{5,9},{9,5},{13,1},{2,14},{6,10},... | collective-permute-start | bytes 958472 | tf_op jit(solution)/shard_map/ppermute | solution.py:471
  242.4 15.4 %collective-permute-start.62 = (bf16[288,768]{1,0:T(8,128)(2,1)S(1)}, bf16[288,768]{1,0:T(8,128)(2,1)S(1)}, u32[]{:S(2)}, u32[]{:S(2)}) collective-permute-start(bf16[288,768]{1,0:T(8,128)(2,1)S(1)} %turn.1), channel_id=1, source_target_pairs={{0,16},{16,0},{1,17},{17,1},{2,18},{18,2},{3,19},{19,3},{4,20},{20... | collective-permute-start | bytes 1327112 | tf_op jit(solution)/shard_map/ppermute | solution.py:595
  (57 other events, 286.2 us)
Sparse Core Ops, SparseCore 0:
  10.2 34.3 all-gather.3
  46.7 30.7 all-gather.5
  79.1 30.7 all-gather.7
  146.4 27.8 reduce-scatter.2
  200.1 40.7 reduce-scatter.4

commit v2 on v1

--- a/solution.py
+++ b/solution.py
@@ -1,3 +1,4 @@
+import dataclasses
 import functools
 import math
 
@@ -65,36 +66,87 @@
     return jax.ShapeDtypeStruct(shape, dtype)
 
 
-def kept(shape, dtype):
-    return pltpu.HBM(shape, dtype)
-
-
-def far(array):
+@dataclasses.dataclass
+class Far:
+    array: jax.Array
+
+
+@dataclasses.dataclass
+class Kept:
+    shape: tuple
+    dtype: type
+
+
+class Fetched:
+    def __init__(self, source, room, sem):
+        self.room, self.waiting, self.shape = room, True, room.shape
+        self.copy = pltpu.make_async_copy(source, room, sem)
+        self.copy.start()
+
+    def ready(self):
+        if self.waiting:
+            self.copy.wait()
+        self.waiting = False
+
+    def __getitem__(self, at):
+        self.ready()
+        return self.room[at]
+
+
+class Streamed:
+    def __init__(self, room, out, sem):
+        self.room, self.shape, self.dtype = room, room.shape, room.dtype
+        self.copy = pltpu.make_async_copy(room, out, sem)
+
+    def __setitem__(self, at, value):
+        self.room[at] = value
+        self.copy.start()
+
+
+def distant(array):
     return pltpu.with_memory_space_constraint(array, pltpu.HBM)
 
 
 def call(body, outs, name, flops, args, specs=None, scratch=(), after=()):
-    vmem = pl.BlockSpec(memory_space=pltpu.VMEM)
-    specs = specs or [vmem] * len(args)
-    if after:
-        inner, count, extra = body, len(args), len(after)
-        specs = specs + [pl.BlockSpec(memory_space=pl.ANY)] * extra
-        args = [*args, *after]
-
-        def body(*refs):
-            inner(*refs[:count], *refs[count + extra :])
-
-    nbytes = sum(math.prod(a.shape) * a.dtype.itemsize for a in (*args, *outs))
+    vmem, hbm = (pl.BlockSpec(memory_space=m) for m in (pltpu.VMEM, pltpu.HBM))
+    specs = list(specs or [vmem] * len(args))
+    heavy = name in ("mlp_bwd", "attn_bwd")
+    far = [i for i, a in enumerate(args) if heavy and isinstance(a, Far)]
+    late = [i for i, o in enumerate(outs) if heavy and isinstance(o, Kept)]
+    args = [distant(a.array) if isinstance(a, Far) else a for a in args]
+    for i in far:
+        specs[i] = hbm
+    rooms = [pltpu.VMEM(v.shape, v.dtype) for v in (*(args[i] for i in far), *(outs[i] for i in late))]
+    count = len(args)
+
+    def kernel(*refs):
+        ins, refs = list(refs[:count]), refs[count + len(after) :]
+        results, refs = list(refs[: len(outs)]), refs[len(outs) :]
+        own, spaces, sems = refs[: len(scratch)], refs[len(scratch) : -1], refs[-1]
+        for k, i in enumerate(far):
+            ins[i] = Fetched(ins[i], spaces[k], sems.at[k])
+        for k, i in enumerate(late, len(far)):
+            results[i] = Streamed(spaces[k], results[i], sems.at[k])
+        body(*ins, *results, *own)
+        for i in far:
+            ins[i].ready()
+        for i in late:
+            results[i].copy.wait()
+
     return pl.pallas_call(
-        body,
-        out_shape=tuple(outs),
-        in_specs=specs,
-        out_specs=(vmem,) * len(outs),
-        scratch_shapes=scratch,
+        kernel,
+        out_shape=tuple(pltpu.HBM(o.shape, o.dtype) if isinstance(o, Kept) else o for o in outs),
+        in_specs=specs + [pl.BlockSpec(memory_space=pl.ANY)] * len(after),
+        out_specs=tuple(hbm if i in late else vmem for i in range(len(outs))),
+        scratch_shapes=[*scratch, *rooms, pltpu.SemaphoreType.DMA((max(1, len(rooms)),))],
         compiler_params=pltpu.CompilerParams(vmem_limit_bytes=VMEM_LIMIT),
-        cost_estimate=pl.CostEstimate(flops=flops, bytes_accessed=nbytes, transcendentals=0),
+        cost_estimate=pl.CostEstimate(
+            flops=flops,
+            bytes_accessed=sum(math.prod(v.shape) * v.dtype.itemsize for v in args),
+            transcendentals=0,
+        ),
         name=name,
-    )(*args)
+    )(*args, *after)
 
 
 def attn_load(layer, weights, proj, sems):
@@ -158,7 +210,8 @@
         heads.append(dot((powers * (1.0 / total)).astype(BF16), v).astype(BF16))
     o = jnp.concatenate(heads, axis=1)
     oqkv_out[...] = jnp.concatenate([o, oqkv[:, width:]], axis=1)
-    lse_out[...] = jnp.concatenate(logs, axis=1)
+    blank = jnp.zeros((mask.shape[0], 128 - len(logs)), F32)
+    lse_out[...] = jnp.concatenate([*logs, blank], axis=1)
     store_blocks(partials, dot_t(o, proj[:, :width]), xs[0].shape[0])
 
 
@@ -252,6 +305,7 @@
     do = dot(dh, proj[:, :width]).astype(BF16)
     oqkv = oqkv_ref[...]
     allowed = mask[...] > 0.5
+    lse = lse[...]
     dqs, dks, dvs = [], [], []
     for h in range(width // HEAD_DIM):
         q, k, v = (
@@ -281,8 +335,7 @@
     rows = dhs[0].shape[0]
     partials[0][...] = da[:rows]
     for k, (out, ref) in enumerate(zip(partials[1:], carried), 1):
-        out[:rows] = da[k * rows : (k + 1) * rows].astype(BF16)
-        out[rows:] = ref[...]
+        out[...] = jnp.concatenate([da[k * rows : (k + 1) * rows].astype(BF16), ref[...]], axis=0)
 
 
 def attn_grads_body(layer, dp, meta, x, dh, a, oqkv, dqkv_ref, weights, sums_mid, hidden_sum, qv_sums, *refs):
@@ -369,7 +422,10 @@
 
 
 def join_body(dp, *refs):
-    keeps, sends, out = refs[: len(refs) // 2], refs[len(refs) // 2 : -1], refs[-1]
+    count = (len(refs) - 3) // 2
+    keeps, sends = refs[:count], refs[count : 2 * count]
+    passing, out, passed = refs[2 * count :]
+    passed[...] = passing[...]
     for j in range(dp):
         out[j] = jnp.concatenate(
             [
@@ -410,6 +466,10 @@
         out[...] = sum(blocks[1:], blocks[0])
 
 
+def rows_body(own, *refs):
+    refs[-1][...] = summed(own, refs[:-1])
+
+
 def finish_body(count, meta, mlp_1, mix, received, own, *refs):
     others, (qkv_out, out_out, fc1_out, fc2_out, attn) = refs[:count], refs[count:]
     first = meta[0] == 0
@@ -523,11 +583,11 @@
     attn_piece, keep, send = call(
         prepare_body,
         [struct((piece, 4 * head_cols), BF16)] + [struct((2, half, hidden), BF16)] * 2,
-        "prepare", 0, [meta, *(far(v) for v in (w_qkv[0], w_out[0], w_fc1[0], w_fc2[0].T))],
+        "prepare", 0, [meta, *(Far(v) for v in (w_qkv[0], w_out[0], w_fc1[0], w_fc2[0].T))],
         [smem] + [vmem] * 4,
     )
     here = ("section", "dp")
-    attn_w = far(lax.all_gather(attn_piece, here, axis=0, tiled=True).reshape(2, width, -1))
+    attn_w = distant(lax.all_gather(attn_piece, here, axis=0, tiled=True).reshape(2, width, -1))
     other = lax.ppermute(send, "section", [(0, 1), (1, 0)])
     mlp_w = []
     for part in (jnp.where(layer_first, keep, other), jnp.where(layer_first, other, keep)):
@@ -535,7 +595,7 @@
         whole = whole.reshape(2, dp, 2, half, hidden)
         if half % 16:
             whole = whole.transpose(2, 1, 0, 3, 4).reshape(1, 1, 2, width, hidden)
-        mlp_w.append(far(whole))
+        mlp_w.append(distant(whole))
     stacks, count, _, part_rows, _ = mlp_w[0].shape
     mlp_room = [
         pltpu.VMEM((2, count, stacks * part_rows, hidden), BF16),
@@ -544,7 +604,7 @@
 
     attn_room = [pltpu.VMEM((width, 4 * head_cols), BF16), pltpu.SemaphoreType.DMA((2,))]
     blocks = [struct((rows, width), F32)] + [struct((rows, width), BF16)] * (tensor - 1)
-    late_blocks = [kept(v.shape, v.dtype) for v in blocks]
+    late_blocks = [Kept(v.shape, v.dtype) for v in blocks]
     unit = 2 * tokens * width * width
 
     saved = []
@@ -554,10 +614,10 @@
         x_all, a, oqkv, lse, own, *away = call(
             functools.partial(attn_fwd_body, tensor, layer),
             [
-                kept((tokens, width), BF16),
-                kept((tokens, width), BF16),
-                kept((tokens, 4 * head_cols), BF16),
-                kept((tokens, head_cols // HEAD_DIM), F32),
+                Kept((tokens, width), BF16),
+                Kept((tokens, width), BF16),
+                Kept((tokens, 4 * head_cols), BF16),
+                Kept((tokens, 128), F32),
                 *blocks,
             ],
             "attn_fwd", 2 * unit, [*xs, params, mask, attn_w],
@@ -565,16 +625,16 @@
         )
         h, c = call(
             functools.partial(middle_body, tensor),
-            [kept((rows, width), F32), struct((rows, width), BF16)],
+            [Kept((rows, width), F32), struct((rows, width), BF16)],
             "middle", 0, [xs[0], own, *to_tensor(away), params],
         )
         late = layer == 1
         c_all, m, der, own, *away = call(
             functools.partial(mlp_fwd_body, tensor),
             [
-                kept((tokens, width), BF16),
-                kept((tokens, hidden), BF16),
-                kept((tokens, hidden), F32),
+                Kept((tokens, width), BF16),
+                Kept((tokens, hidden), BF16),
+                Kept((tokens, hidden), F32),
                 *(late_blocks if late else blocks),
             ],
             "mlp_fwd", 2 * unit, [*everywhere(c), params, mlp_w[layer]],
@@ -587,22 +647,21 @@
         (y,) = call(
             functools.partial(end_body, tensor),
             [struct((rows, width), BF16)],
-            "end", 0, [far(h), own, *to_tensor(away), params],
+            "end", 0, [Far(h), own, *to_tensor(away), params],
         )
         outputs.append(y)
         xs = everywhere(y)
 
     swap = lambda v: lax.ppermute(v, "section", [(0, 1), (1, 0)])
 
-    def joined_halves(pairs, after=()):
+    def joined_halves(pairs, passing, after=()):
         keeps, sends = [p[0] for p in pairs], [swap(p[1]) for p in pairs]
         rows_each = sum(k.shape[1] for k in keeps)
-        (joined,) = call(
+        return call(
             functools.partial(join_body, dp),
-            [struct((dp, rows_each, hidden), BF16)],
-            "join", 0, [*keeps, *sends], after=after,
-        )
-        return joined
+            [struct((dp, rows_each, hidden), BF16), struct(passing.shape, passing.dtype)],
+            "join", 0, [keeps[0], *map(distant, keeps[1:]), sends[0], *map(distant, sends[1:]), passing], after=after,
+        )
 
     def over_dp(joined):
         joined = joined.reshape(-1, hidden)
@@ -611,6 +670,7 @@
     input_grads = [None] * 2
     pairs = []
     extra = []
+    share = piece // tensor
     e, es = cots[0], cots
     for layer in (1, 0):
         params = smalls[layer]
@@ -618,12 +678,12 @@
         e_all, du, hidden_sum, own, *away = call(
             functools.partial(mlp_bwd_body, tensor),
             [
-                kept((tokens, width), BF16),
-                kept((tokens, hidden), BF16),
-                kept((1, hidden), F32),
+                Kept((tokens, width), BF16),
+                Kept((tokens, hidden), BF16),
+                struct((1, hidden), F32),
                 *blocks,
             ],
-            "mlp_bwd", 2 * unit, [*es, far(der), mlp_w[layer]],
+            "mlp_bwd", 2 * unit, [*es, Far(der), mlp_w[layer]],
             [vmem] * (tensor + 1) + [hbm], mlp_room, extra,
         )
         received = to_tensor(away)
@@ -631,36 +691,36 @@
             call,
             functools.partial(mlp_grads_body, dp),
             [struct((dp, 2 * half, hidden), BF16)] * 2,
-            "mlp_grads", 2 * unit, [meta, far(c_all), far(e_all), far(du), far(m)],
+            "mlp_grads", 2 * unit, [meta, Far(c_all), Far(e_all), Far(du), Far(m)],
             [smem] + [vmem] * 4, [pltpu.VMEM((2, width, hidden), F32)],
         )
         mlp_pair = mlp_grads(received)
         dh, dh_low, sums_mid = call(
             functools.partial(middle_back_body, tensor),
-            [kept((rows, width), F32), struct((rows, width), BF16), kept((4, width), F32)],
-            "middle_back", 0, [e, far(h), own, *received, params],
+            [Kept((rows, width), F32), struct((rows, width), BF16), struct((4, width), F32)],
+            "middle_back", 0, [e, Far(h), own, *received, params],
             after=[mlp_pair[0]],
         )
-        dhs = everywhere(dh_low)
         if layer == 1:
-            joined = joined_halves([mlp_pair], dhs[1:])
+            joined, dh_low = joined_halves([mlp_pair], dh_low)
             mlp_1 = over_dp(joined)
         else:
-            joined = joined_halves([mlp_pair, *pairs], [*dhs[1:], mlp_1])
+            joined, dh_low = joined_halves([mlp_pair, *pairs], dh_low, [mlp_1])
             mix = over_dp(joined)
+        dhs = everywhere(dh_low)
         dh_all, dqkv, qv_sums, own, *away = call(
             functools.partial(attn_bwd_body, tensor, layer),
             [
-                kept((tokens, width), BF16),
-                kept((tokens, 4 * head_cols), BF16),
-                kept((2, head_cols), F32),
+                Kept((tokens, width), BF16),
+                Kept((tokens, 4 * head_cols), BF16),
+                struct((2, head_cols), F32),
                 blocks[0],
                 *[struct((rows if layer == 1 else 2 * rows, width), BF16)] * (tensor - 1),
             ],
             "attn_bwd", 2 * unit,
-            [*dhs, attn_w, far(oqkv), far(lse), mask, *(() if layer == 1 else map(far, carried[1]))],
+            [*dhs, attn_w, Far(oqkv), Far(lse), mask, *(() if layer == 1 else map(Far, carried[1]))],
             [vmem] * tensor + [hbm] + [vmem] * (3 if layer == 1 else tensor + 2),
-            attn_room, [joined],
+            attn_room,
         )
         received = to_tensor(away)
         whole = direct and layer == 0
@@ -672,8 +732,8 @@
             else [struct((dp, half + 16, 4 * head_cols), BF16)] * 2,
             "attn_grads", 3 * unit,
             [
-                meta, far(x_all), far(dh_all), far(a), far(oqkv), far(dqkv), attn_w,
-                far(sums_mid), far(hidden_sum), far(qv_sums),
+                meta, Far(x_all), Far(dh_all), Far(a), Far(oqkv), Far(dqkv), attn_w,
+                sums_mid, hidden_sum, qv_sums,
             ],
             [smem] + [vmem] * 5 + [hbm] + [vmem] * 3,
             [pltpu.VMEM((width, 4 * head_cols), F32), *attn_room],
@@ -689,33 +749,41 @@
                 "split", 0, [meta, grad, to_other(grad, 1)], [smem, vmem, vmem],
             )
             attn_others = to_dp(attn_away, 0)
-            follows = attn_own
         else:
-            attn_0 = over_dp(joined_halves([attn_grads()]))
+            attn_0 = over_dp(joined_halves([attn_grads()], dh_low)[0])
             there = swap(attn_0)
             attn_own = jnp.concatenate(
                 [jnp.where(layer_first, v[:half], w[:half]) for v, w in ((attn_0, there), (there, attn_0))]
                 + [attn_0[half:]]
             ).astype(F32)
             attn_others = []
-            follows = attn_own
         if layer == 1:
             e, e_low = call(
                 functools.partial(end_back_body, tensor),
                 [struct((rows, width), F32), struct((rows, width), BF16)],
-                "end_back", 0, [far(dh), x, own, *received, params],
+                "end_back", 0, [Far(dh), x, own, *received, params],
             )
             es = everywhere(e_low)
             attn_pair = attn_grads(es[1:2])
             pairs.append(attn_pair)
             extra = [attn_pair[0]]
         else:
+            (sent,) = call(
+                turn_body, [struct((3 * half, hidden), BF16)], "turn", 0, [meta, mlp_1, mix],
+                [smem, vmem, vmem],
+            )
+            total, row_own, *row_away = call(
+                functools.partial(small_body, len(attn_others)),
+                [struct((16, width), F32)] + [struct((6, share), F32)] * tensor,
+                "small", 0, [meta, mix, attn_own, *attn_others],
+                [smem] + [vmem] * (2 + len(attn_others)),
+            )
             e, y = call(
                 functools.partial(last_body, tensor),
                 [struct((rows, width), F32), struct((rows, width), BF16)],
                 "last", 0,
-                [far(dh), x, own, *received, params, far(saved[1][5]), far(carried[0]), smalls[1]],
-                after=[follows],
+                [Far(dh), x, own, *received, params, Far(saved[1][5]), Far(carried[0]), smalls[1]],
+                after=[total],
             )
             outputs.append(y)
         input_grads[layer] = e
@@ -728,19 +796,8 @@
 
     block_out = both(outputs)
     grads_out = both(input_grads)
-    share = piece // tensor
-    (sent,) = call(
-        turn_body, [struct((3 * half, hidden), BF16)], "turn", 0, [meta, mlp_1, mix],
-        [smem, vmem, vmem],
-    )
     received = swap(sent)
-    total, row_own, *row_away = call(
-        functools.partial(small_body, len(attn_others)),
-        [struct((16, width), F32)] + [struct((6, share), F32)] * tensor,
-        "small", 0, [meta, mix, attn_own, *attn_others],
-        [smem] + [vmem] * (2 + len(attn_others)),
-    )
-    row_grad = row_own + sum(to_tensor(row_away))
+    row_away = to_tensor(row_away)
     qv_cols = head_cols // dp
     qv_grad = lax.dynamic_slice(
         total, (7, d * qv_cols), (2, qv_cols), allow_negative_indices=False
@@ -756,6 +813,9 @@
         "finish", 0, [meta, mlp_1, mix, received, attn_own, *attn_others],
         [smem] + [vmem] * (4 + len(attn_others)),
         [pltpu.VMEM((piece, 4 * head_cols), F32)],
+    )
+    (row_grad,) = call(
+        rows_body, [struct((6, share), F32)], "rows", 0, [row_own, *row_away], after=[w_fc1_grad]
     )
     return (
         block_out,

time: 268 us -> 261 us (0.974)
  waiting for transfers between devices: 101 us -> 97.2 us
  Pallas kernels: 64 us -> 60.5 us
    ppermute x48, waiting for transfers between devices: 55.1 us -> 46 us  [to_tensor(): lax.ppermute(v, 'tensor', [(i, i ^ k) for i in range(tensor)])]
    ppermute x3, waiting for transfers between devices: 6.11 us -> 1.52 us  [to_dp(): lax.ppermute(v, ('section', 'dp'), [(layer * dp + i, layer * dp + (i ^ k)...]
    reduce_scatter x2, waiting for transfers between devices: 3.64 us -> 7.79 us  [over_dp(): return lax.psum_scatter(joined, 'dp', scatter_dimension=0, tiled=True)]
    pallas_call x27 -> x28, Pallas kernels: 64 us -> 60.5 us  [call(): pl.pallas_call(kernel, out_shape=tuple((pltpu.HBM(o.shape, o.dtype) if is...]
    ppermute x1, waiting for transfers between devices: 0.16 us -> 3.57 us  [to_other(): return lax.ppermute(value, 'section', [(source, 1 - source)])]
    ppermute x6, waiting for transfers between devices: 0.02 us -> 2.89 us  [shards(): swap = lambda v: lax.ppermute(v, 'section', [(0, 1), (1, 0)])]
    unnamed x27 -> x45, local copies, waits for them, and re-layouts: 6.87 us -> 6.98 us
  transfers between devices with their start and end apart: 68 -> 68, of which waited for: 46 -> 44; matrix products, arithmetic and copies ran while one was open for 2% -> 2% of each run, Pallas kernels for 19% -> 19%
where the time goes in v2:
time: 261 us; the launch traced here: 260 us
  waiting for transfers between devices  97.2 us (37%)
  starting transfers between devices  76.3 us (29%)
  Pallas kernels  60.5 us (23%)
  between operations  14.5 us (6%)
  local copies, waits for them, and re-layouts  8.32 us (3%)
  other arithmetic  2.8 us (1%)
    pallas_call x28, Pallas kernels, call(): pl.pallas_call(kernel, out_shape=tuple((pltpu.HBM(o.shape, o.dtype) if is...  60.5 us
    ppermute x48, starting transfers between devices, to_tensor(): lax.ppermute(v, 'tensor', [(i, i ^ k) for i in range(tensor)])  57.4 us
    ppermute x48, waiting for transfers between devices, to_tensor(): lax.ppermute(v, 'tensor', [(i, i ^ k) for i in range(tensor)])  46 us
    all_gather x1, waiting for transfers between devices, shards(): lax.all_gather(attn_piece, here, axis=0, tiled=True).reshape(2, width, -1)  17.8 us
    all_gather x2, waiting for transfers between devices, shards(): lax.all_gather(part.reshape(2 * half, hidden), here, axis=0, tiled=True)  13 us
    ppermute x3, starting transfers between devices, to_dp(): lax.ppermute(v, ('section', 'dp'), [(layer * dp + i, layer * dp + (i ^ k)...  10.1 us
    reduce_scatter x2, waiting for transfers between devices, over_dp(): return lax.psum_scatter(joined, 'dp', scatter_dimension=0, tiled=True)  7.79 us
    unnamed x45, local copies, waits for them, and re-layouts  6.98 us
  transfers between devices with their start and end apart: 68, of which 44 were waited for; matrix products, arithmetic and copies ran while one was open for 2% of the time, Pallas kernels for 19%

profile of v2, /device:TPU:0, one launch (start us, length us, event | category | flops | bytes accessed | tf_op | source)
XLA Modules:
  0.0 259.7 jit_solution(18189478983106894311)
XLA Ops:
  13.0 4.0 %collective-permute-start.4 = (bf16[16,192]{1,0:T(8,128)(2,1)S(1)}, bf16[16,192]{1,0:T(8,128)(2,1)S(1)}, u32[]{:S(2)}, u32[]{:S(2)}) collective-permute-start(bf16[16,192]{1,0:T(8,128)(2,1)S(1)} %pad.9), channel_id=1, source_target_pairs={{0,8},{4,12},{8,0},{12,4},{1,9},{5,13},{9,1},{13,5},{2,10},{6,14},... | collective-permute-start | bytes 18440 | tf_op jit(solution)/shard_map/ppermute | solution.py:559
  18.6 2.7 %collective-permute-start.2 = (bf16[64,768]{1,0:T(8,128)(2,1)S(1)}, bf16[64,768]{1,0:T(8,128)(2,1)S(1)}, u32[]{:S(2)}, u32[]{:S(2)}) collective-permute-start(bf16[64,768]{1,0:T(8,128)(2,1)S(1)} %dynamic-slice_bitcast_fusion.1.refs_0_.refs_1_), channel_id=1, source_target_pairs={{0,3},{1,2},{2,1},{3,0},{4,7},{5,6},{6,5},{7,4},{8,11},{9,10},{10,... | collective-permute-start | bytes 294920 | tf_op jit(solution)/shard_map/ppermute | solution.py:522
  26.8 17.8 %all-gather.4.cloned.1.call-done = bf16[1536,768]{1,0:T(8,128)(2,1)} async-done(((bf16[192,768]{1,0:T(8,128)(2,1)}), bf16[1536,768]{1,0:T(8,128)(2,1)}) %all-gather.4.cloned.1.call-update) | async-done | bytes 2359312 | tf_op jit(solution)/shard_map/all_gather | solution.py:590
  44.5 3.6 %attn_fwd.2 = (bf16[256,768]{1,0:T(8,128)(2,1)}, bf16[256,768]{1,0:T(8,128)(2,1)}, bf16[256,768]{1,0:T(8,128)(2,1)}, f32[256,128]{1,0:T(8,128)}, f32[64,768]{1,0...) custom-call(bf16[64,768]{1,0:T(8,128)(2,1)S(1)} %dynamic-slice_bitcast_fusion.1, ...), custom_call_target="tpu_custom_call" | custom-call | flops 603979776 | bytes 3039232 | tf_op jit(solution)/shard_map/attn_fwd/pallas_call | solution.py:136
  61.0 2.6 %collective-permute-done.12.refs_3_ = bf16[64,768]{1,0:T(8,128)(2,1)S(1)} collective-permute-done((bf16[64,768]{1,0:T(8,128)(2,1)S(1)}, bf16[64,768]{1,0:T(8,128)(2,1)S(1)}, u32[]{:S(2)}, u32[]{:S(2)}) %collective-permute-start.12) | collective-permute-done | bytes 98336 | tf_op jit(solution)/shard_map/ppermute | solution.py:522
  64.5 13.0 %all-gather.6.cloned.1.call-done = bf16[1536,768]{1,0:T(8,128)(2,1)} async-done(((bf16[192,768]{1,0:T(8,128)(2,1)}), bf16[1536,768]{1,0:T(8,128)(2,1)}) %all-gather.6.cloned.1.call-update) | async-done | bytes 2359312 | tf_op jit(solution)/shard_map/all_gather | solution.py:594
  77.5 3.4 %mlp_fwd.2 = (bf16[256,768]{1,0:T(8,128)(2,1)}, bf16[256,768]{1,0:T(8,128)(2,1)}, f32[256,768]{1,0:T(8,128)}, f32[64,768]{1,0:T(8,128)S(1)}, bf16[64,768]{1,0:T(...) custom-call(bf16[64,768]{1,0:T(8,128)(2,1)S(1)} %get-tuple-element.116.refs_0_, ...), custom_call_target="tpu_custom_call" | custom-call | flops 603979776 | bytes 2777088 | tf_op jit(solution)/shard_map/mlp_fwd/pallas_call | solution.py:136
  94.0 2.6 collective-permute-done.19.refs_3_
  97.5 3.6 %attn_fwd.3 = (bf16[256,768]{1,0:T(8,128)(2,1)}, bf16[256,768]{1,0:T(8,128)(2,1)}, bf16[256,768]{1,0:T(8,128)(2,1)}, f32[256,128]{1,0:T(8,128)}, f32[64,768]{1,0...) custom-call(bf16[64,768]{1,0:T(8,128)(2,1)S(1)} %end.1.refs_0_.refs_1_, ...), custom_call_target="tpu_custom_call" | custom-call | flops 603979776 | bytes 3039232 | tf_op jit(solution)/shard_map/attn_fwd/pallas_call | solution.py:136
  118.0 3.5 %mlp_fwd.3 = (bf16[256,768]{1,0:T(8,128)(2,1)}, bf16[256,768]{1,0:T(8,128)(2,1)}, f32[256,768]{1,0:T(8,128)}, f32[64,768]{1,0:T(8,128)}, bf16[64,768]{1,0:T(8,12...) custom-call(bf16[64,768]{1,0:T(8,128)(2,1)S(1)} %get-tuple-element.129.refs_0_, ...), custom_call_target="tpu_custom_call" | custom-call | flops 603979776 | bytes 2777088 | tf_op jit(solution)/shard_map/mlp_fwd/pallas_call | solution.py:136
  121.5 3.1 %mlp_bwd.2 = (bf16[256,768]{1,0:T(8,128)(2,1)}, bf16[256,768]{1,0:T(8,128)(2,1)}, f32[1,768]{1,0:T(1,128)S(1)}, f32[64,768]{1,0:T(8,128)S(1)}, bf16[64,768]{1,0:...) custom-call(bf16[64,768]{1,0:T(8,128)(2,1)S(1)} %dynamic-slice_bitcast_fusion.refs_0_, ...), custom_call_target="tpu_custom_call" | custom-call | flops 603979776 | bytes 3538944 | tf_op jit(solution)/shard_map/mlp_bwd/pallas_call | solution.py:136
  142.0 2.4 collective-permute-done.35.refs_3_
  146.3 4.2 %attn_bwd.2 = (bf16[256,768]{1,0:T(8,128)(2,1)}, bf16[256,768]{1,0:T(8,128)(2,1)}, f32[2,192]{1,0:T(2,128)S(1)}, f32[64,768]{1,0:T(8,128)S(1)}, bf16[64,768]{1,0...) custom-call(bf16[64,768]{1,0:T(8,128)(2,1)S(1)} %get-tuple-element.143.refs_0_, ...), custom_call_target="tpu_custom_call" | custom-call | flops 603979776 | bytes 3538944 | tf_op jit(solution)/shard_map/attn_bwd/pallas_call | solution.py:136
  164.4 3.7 %attn_grads.2 = (bf16[4,112,768]{2,1,0:T(8,128)(2,1)S(1)}, bf16[4,112,768]{2,1,0:T(8,128)(2,1)S(1)}) custom-call(s32[3]{0:T(128)S(1)} %pad_add_fusion.2.refs_0_, bf16[256,768]{1,0:T(8,128)(2,1)} %get-tuple-element.153.refs_1_, bf16[256,768]{1,0:T(8,128)(2,1)} %get-tuple-element.154.refs_2_, bf16[256,768]{1,0:T(8,128)(2,1)} %get-tuple-element.155.refs_3_, ...), custom_call_target="tpu_custom_call" | custom-call | flops 905969664 | bytes 4342284 | tf_op jit(solution)/shard_map/attn_grads/pallas_call | solution.py:136
  168.1 3.3 %mlp_bwd.3 = (bf16[256,768]{1,0:T(8,128)(2,1)}, bf16[256,768]{1,0:T(8,128)(2,1)}, f32[1,768]{1,0:T(1,128)S(1)}, f32[64,768]{1,0:T(8,128)S(1)}, bf16[64,768]{1,0:...) custom-call(bf16[64,768]{1,0:T(8,128)(2,1)S(1)} %get-tuple-element.151.refs_0_, ...), custom_call_target="tpu_custom_call" | custom-call | flops 603979776 | bytes 3538944 | tf_op jit(solution)/shard_map/mlp_bwd/pallas_call | solution.py:136
  194.3 3.0 %collective-permute-done.49.refs_3_ = bf16[64,768]{1,0:T(8,128)(2,1)S(1)} collective-permute-done((bf16[64,768]{1,0:T(8,128)(2,1)S(1)}, bf16[64,768]{1,0:T(8,128)(2,1)S(1)}, u32[]{:S(2)}, u32[]{:S(2)}) %collective-permute-start.49) | collective-permute-done | bytes 98336 | tf_op jit(solution)/shard_map/ppermute | solution.py:522
  198.6 4.3 %attn_bwd.3 = (bf16[256,768]{1,0:T(8,128)(2,1)}, bf16[256,768]{1,0:T(8,128)(2,1)}, f32[2,192]{1,0:T(2,128)S(1)}, f32[64,768]{1,0:T(8,128)S(1)}, bf16[128,768]{1,...) custom-call(bf16[64,768]{1,0:T(8,128)(2,1)S(1)} %get-tuple-element.175.refs_0_, ...), custom_call_target="tpu_custom_call" | custom-call | flops 603979776 | bytes 3833856 | tf_op jit(solution)/shard_map/attn_bwd/pallas_call | solution.py:136
  203.0 3.6 %attn_grads.3.refs_1_ = bf16[4,208,768]{2,1,0:T(8,128)(2,1)S(1)} custom-call(s32[3]{0:T(128)S(1)} %copy-done.9, bf16[256,768]{1,0:T(8,128)(2,1)} %get-tuple-element.187.refs_1_, bf16[256,768]{1,0:T(8,128)(2,1)} %get-tuple-element.188.refs_2_, bf16[256,768]{1,0:T(8,128)(2,1)} %get-tuple-element.189.refs_3_, ...), custom_call_target="tpu_custom_call" | custom-call | flops 905969664 | bytes 4342284 | tf_op jit(solution)/shard_map/attn_grads/pallas_call | solution.py:136
  208.1 3.6 %collective-permute-done.53.refs_2_ = bf16[4,208,768]{2,1,0:T(8,128)(2,1)S(1)} collective-permute-done((bf16[4,208,768]{2,1,0:T(8,128)(2,1)S(1)}, bf16[4,208,768]{2,1,0:T(8,128)(2,1)S(1)}, u32[]{:S(2)}, u32[]{:S(2)}) %collective-permute-start.53) | collective-permute-done | bytes 1277984 | tf_op jit(solution)/shard_map/ppermute | solution.py:538
  213.3 2.5 collective-permute-start.54
  215.8 3.4 %collective-permute-start.55 = (bf16[208,768]{1,0:T(8,128)(2,1)}, bf16[208,768]{1,0:T(8,128)(2,1)S(1)}, u32[]{:S(2)}, u32[]{:S(2)}) collective-permute-start(bf16[208,768]{1,0:T(8,128)(2,1)} %get-tuple-element.196), channel_id=1, source_target_pairs={{0,8},{4,12},{8,0},{12,4},{1,9},{5,13},{9,1},{13,5},{2,10},{6,14},... | collective-permute-start | bytes 958472 | tf_op jit(solution)/shard_map/ppermute | solution.py:531
  219.2 4.3 %collective-permute-start.56 = (bf16[208,768]{1,0:T(8,128)(2,1)}, bf16[208,768]{1,0:T(8,128)(2,1)S(1)}, u32[]{:S(2)}, u32[]{:S(2)}) collective-permute-start(bf16[208,768]{1,0:T(8,128)(2,1)} %get-tuple-element.197), channel_id=1, source_target_pairs={{0,12},{4,8},{8,4},{12,0},{1,13},{5,9},{9,5},{13,1},{2,14},{6,10},... | collective-permute-start | bytes 958472 | tf_op jit(solution)/shard_map/ppermute | solution.py:531
  225.4 7.8 %reduce-scatter.5.cloned.1.call-done.refs_1_.refs_2_ = bf16[304,768]{1,0:T(8,128)(2,1)} async-done(((bf16[1216,768]{1,0:T(8,128)(2,1)}), bf16[304,768]{1,0:T(8,128)(2,1)}) %reduce-scatter.5.cloned.1.call-update) | async-done | bytes 466960 | tf_op jit(solution)/shard_map/reduce_scatter | solution.py:668
  234.8 2.9 %collective-permute-start.52 = (bf16[128,768]{1,0:T(8,128)(2,1)S(1)}, bf16[128,768]{1,0:T(8,128)(2,1)S(1)}, u32[]{:S(2)}, u32[]{:S(2)}) collective-permute-start(bf16[128,768]{1,0:T(8,128)(2,1)S(1)} %get-tuple-element.184), channel_id=1, source_target_pairs={{0,3},{1,2},{2,1},{3,0},{4,7},{5,6},{6,5},{7,4},{8,11},{9,10},{10,... | collective-permute-start | bytes 589832 | tf_op jit(solution)/shard_map/ppermute | solution.py:522
  (216 shorter events, 136.5 us)
Async XLA Ops:
  7.2 37.4 %all-gather.4.cloned.1.call-start = ((), (), s32[]{:S(2)}) async-start(), calls=%async_computation.2 | async-start | bytes 2654208 | tf_op jit(solution)/shard_map/all_gather | solution.py:590
  9.5 68.0 %all-gather.6.cloned.1.call-start = ((), (), s32[]{:S(2)}) async-start(), calls=%async_computation.3 | async-start | bytes 2654208 | tf_op jit(solution)/shard_map/all_gather | solution.py:594
  12.1 104.8 %all-gather.8.cloned.1.call-start = ((), (), s32[]{:S(2)}) async-start(), calls=%async_computation.4 | async-start | bytes 2654208 | tf_op jit(solution)/shard_map/all_gather | solution.py:594
  12.9 173.8 %reduce-scatter.3.cloned.1.call-start = ((), (), s32[]{:S(2)}) async-start(), calls=%async_computation.5 | async-start | bytes 1474560 | tf_op jit(solution)/shard_map/reduce_scatter | solution.py:668
  13.0 9.1 %collective-permute-start.4 = (bf16[16,192]{1,0:T(8,128)(2,1)S(1)}, bf16[16,192]{1,0:T(8,128)(2,1)S(1)}, u32[]{:S(2)}, u32[]{:S(2)}) collective-permute-start(bf16[16,192]{1,0:T(8,128)(2,1)S(1)} %pad.9), channel_id=1, source_target_pairs={{0,8},{4,12},{8,0},{12,4},{1,9},{5,13},{9,1},{13,5},{2,10},{6,14},... | collective-permute-start | bytes 18440 | tf_op jit(solution)/shard_map/ppermute | solution.py:559
  18.6 7.5 %collective-permute-start.2 = (bf16[64,768]{1,0:T(8,128)(2,1)S(1)}, bf16[64,768]{1,0:T(8,128)(2,1)S(1)}, u32[]{:S(2)}, u32[]{:S(2)}) collective-permute-start(bf16[64,768]{1,0:T(8,128)(2,1)S(1)} %dynamic-slice_bitcast_fusion.1.refs_0_.refs_1_), channel_id=1, source_target_pairs={{0,3},{1,2},{2,1},{3,0},{4,7},{5,6},{6,5},{7,4},{8,11},{9,10},{10,... | collective-permute-start | bytes 294920 | tf_op jit(solution)/shard_map/ppermute | solution.py:522
  109.8 6.5 %collective-permute-start.28 = (bf16[64,768]{1,0:T(8,128)(2,1)S(1)}, bf16[64,768]{1,0:T(8,128)(2,1)S(1)}, u32[]{:S(2)}, u32[]{:S(2)}) collective-permute-start(bf16[64,768]{1,0:T(8,128)(2,1)S(1)} %get-tuple-element.129.refs_0_), channel_id=1, source_target_pairs={{0,3},{1,2},{2,1},{3,0},{4,7},{5,6},{6,5},{7,4},{8,11},{9,10},{10,... | collective-permute-start | bytes 294920 | tf_op jit(solution)/shard_map/ppermute | solution.py:522
  111.0 6.9 %collective-permute-start.27 = (bf16[64,768]{1,0:T(8,128)(2,1)S(1)}, bf16[64,768]{1,0:T(8,128)(2,1)S(1)}, u32[]{:S(2)}, u32[]{:S(2)}) collective-permute-start(bf16[64,768]{1,0:T(8,128)(2,1)S(1)} %get-tuple-element.129.refs_0_), channel_id=1, source_target_pairs={{0,2},{1,3},{2,0},{3,1},{4,6},{5,7},{6,4},{7,5},{8,10},{9,11},{10,... | collective-permute-start | bytes 294920 | tf_op jit(solution)/shard_map/ppermute | solution.py:522
  113.4 8.1 %collective-permute-start.25 = (bf16[64,768]{1,0:T(8,128)(2,1)S(1)}, bf16[64,768]{1,0:T(8,128)(2,1)S(1)}, u32[]{:S(2)}, u32[]{:S(2)}) collective-permute-start(bf16[64,768]{1,0:T(8,128)(2,1)S(1)} %dynamic-slice_bitcast_fusion.refs_0_), channel_id=1, source_target_pairs={{0,3},{1,2},{2,1},{3,0},{4,7},{5,6},{6,5},{7,4},{8,11},{9,10},{10,... | collective-permute-start | bytes 294920 | tf_op jit(solution)/shard_map/ppermute | solution.py:522
  114.6 6.9 %collective-permute-start.24 = (bf16[64,768]{1,0:T(8,128)(2,1)S(1)}, bf16[64,768]{1,0:T(8,128)(2,1)S(1)}, u32[]{:S(2)}, u32[]{:S(2)}) collective-permute-start(bf16[64,768]{1,0:T(8,128)(2,1)S(1)} %dynamic-slice_bitcast_fusion.refs_0_), channel_id=1, source_target_pairs={{0,2},{1,3},{2,0},{3,1},{4,6},{5,7},{6,4},{7,5},{8,10},{9,11},{10,... | collective-permute-start | bytes 294920 | tf_op jit(solution)/shard_map/ppermute | solution.py:522
  138.2 95.0 %reduce-scatter.5.cloned.1.call-start = ((), (), s32[]{:S(2)}) async-start(), calls=%async_computation.6 | async-start | bytes 2334720 | tf_op jit(solution)/shard_map/reduce_scatter | solution.py:668
  160.7 7.4 %collective-permute-start.41 = (bf16[64,768]{1,0:T(8,128)(2,1)S(1)}, bf16[64,768]{1,0:T(8,128)(2,1)S(1)}, u32[]{:S(2)}, u32[]{:S(2)}) collective-permute-start(bf16[64,768]{1,0:T(8,128)(2,1)S(1)} %get-tuple-element.151.refs_0_), channel_id=1, source_target_pairs={{0,3},{1,2},{2,1},{3,0},{4,7},{5,6},{6,5},{7,4},{8,11},{9,10},{10,... | collective-permute-start | bytes 294920 | tf_op jit(solution)/shard_map/ppermute | solution.py:522
  190.7 6.6 %collective-permute-start.49 = (bf16[64,768]{1,0:T(8,128)(2,1)S(1)}, bf16[64,768]{1,0:T(8,128)(2,1)S(1)}, u32[]{:S(2)}, u32[]{:S(2)}) collective-permute-start(bf16[64,768]{1,0:T(8,128)(2,1)S(1)} %get-tuple-element.175.refs_0_), channel_id=1, source_target_pairs={{0,3},{1,2},{2,1},{3,0},{4,7},{5,6},{6,5},{7,4},{8,11},{9,10},{10,... | collective-permute-start | bytes 294920 | tf_op jit(solution)/shard_map/ppermute | solution.py:522
  192.1 6.5 %collective-permute-start.48 = (bf16[64,768]{1,0:T(8,128)(2,1)S(1)}, bf16[64,768]{1,0:T(8,128)(2,1)S(1)}, u32[]{:S(2)}, u32[]{:S(2)}) collective-permute-start(bf16[64,768]{1,0:T(8,128)(2,1)S(1)} %get-tuple-element.175.refs_0_), channel_id=1, source_target_pairs={{0,2},{1,3},{2,0},{3,1},{4,6},{5,7},{6,4},{7,5},{8,10},{9,11},{10,... | collective-permute-start | bytes 294920 | tf_op jit(solution)/shard_map/ppermute | solution.py:522
  213.3 21.5 %collective-permute-start.54 = (bf16[208,768]{1,0:T(8,128)(2,1)}, bf16[208,768]{1,0:T(8,128)(2,1)S(1)}, u32[]{:S(2)}, u32[]{:S(2)}) collective-permute-start(bf16[208,768]{1,0:T(8,128)(2,1)} %get-tuple-element.195), channel_id=1, source_target_pairs={{0,4},{4,0},{8,12},{12,8},{1,5},{5,1},{9,13},{13,9},{2,6},{6,2},{1... | collective-permute-start | bytes 958472 | tf_op jit(solution)/shard_map/ppermute | solution.py:531
  215.8 22.0 %collective-permute-start.55 = (bf16[208,768]{1,0:T(8,128)(2,1)}, bf16[208,768]{1,0:T(8,128)(2,1)S(1)}, u32[]{:S(2)}, u32[]{:S(2)}) collective-permute-start(bf16[208,768]{1,0:T(8,128)(2,1)} %get-tuple-element.196), channel_id=1, source_target_pairs={{0,8},{4,12},{8,0},{12,4},{1,9},{5,13},{9,1},{13,5},{2,10},{6,14},... | collective-permute-start | bytes 958472 | tf_op jit(solution)/shard_map/ppermute | solution.py:531
  219.2 20.1 %collective-permute-start.56 = (bf16[208,768]{1,0:T(8,128)(2,1)}, bf16[208,768]{1,0:T(8,128)(2,1)S(1)}, u32[]{:S(2)}, u32[]{:S(2)}) collective-permute-start(bf16[208,768]{1,0:T(8,128)(2,1)} %get-tuple-element.197), channel_id=1, source_target_pairs={{0,12},{4,8},{8,4},{12,0},{1,13},{5,9},{9,5},{13,1},{2,14},{6,10},... | collective-permute-start | bytes 958472 | tf_op jit(solution)/shard_map/ppermute | solution.py:531
  223.5 18.6 %collective-permute-start.50 = (bf16[128,768]{1,0:T(8,128)(2,1)S(1)}, bf16[128,768]{1,0:T(8,128)(2,1)}, u32[]{:S(2)}, u32[]{:S(2)}) collective-permute-start(bf16[128,768]{1,0:T(8,128)(2,1)S(1)} %copy-done.15), channel_id=1, source_target_pairs={{0,1},{1,0},{2,3},{3,2},{4,5},{5,4},{6,7},{7,6},{8,9},{9,8},{10,11... | collective-permute-start | bytes 589832 | tf_op jit(solution)/shard_map/ppermute | solution.py:522
  224.5 19.1 %collective-permute-start.51 = (bf16[128,768]{1,0:T(8,128)(2,1)S(1)}, bf16[128,768]{1,0:T(8,128)(2,1)}, u32[]{:S(2)}, u32[]{:S(2)}) collective-permute-start(bf16[128,768]{1,0:T(8,128)(2,1)S(1)} %get-tuple-element.183), channel_id=1, source_target_pairs={{0,2},{1,3},{2,0},{3,1},{4,6},{5,7},{6,4},{7,5},{8,10},{9,11},{10,... | collective-permute-start | bytes 589832 | tf_op jit(solution)/shard_map/ppermute | solution.py:522
  234.8 9.3 %collective-permute-start.52 = (bf16[128,768]{1,0:T(8,128)(2,1)S(1)}, bf16[128,768]{1,0:T(8,128)(2,1)S(1)}, u32[]{:S(2)}, u32[]{:S(2)}) collective-permute-start(bf16[128,768]{1,0:T(8,128)(2,1)S(1)} %get-tuple-element.184), channel_id=1, source_target_pairs={{0,3},{1,2},{2,1},{3,0},{4,7},{5,6},{6,5},{7,4},{8,11},{9,10},{10,... | collective-permute-start | bytes 589832 | tf_op jit(solution)/shard_map/ppermute | solution.py:522
  237.8 11.6 %collective-permute-start.62 = (bf16[288,768]{1,0:T(8,128)(2,1)S(1)}, bf16[288,768]{1,0:T(8,128)(2,1)S(1)}, u32[]{:S(2)}, u32[]{:S(2)}) collective-permute-start(bf16[288,768]{1,0:T(8,128)(2,1)S(1)} %turn.1), channel_id=1, source_target_pairs={{0,16},{16,0},{1,17},{17,1},{2,18},{18,2},{3,19},{19,3},{4,20},{20... | collective-permute-start | bytes 1327112 | tf_op jit(solution)/shard_map/ppermute | solution.py:655
  240.0 11.5 %collective-permute-start.59 = (f32[6,48]{1,0:T(8,128)S(1)}, f32[6,48]{1,0:T(8,128)S(1)}, u32[]{:S(2)}, u32[]{:S(2)}) collective-permute-start(f32[6,48]{1,0:T(8,128)S(1)} %get-tuple-element.202), channel_id=1, source_target_pairs={{0,1},{1,0},{2,3},{3,2},{4,5},{5,4},{6,7},{7,6},{8,9},{9,8},{10,11... | collective-permute-start | bytes 3464 | tf_op jit(solution)/shard_map/ppermute | solution.py:522
  242.1 9.4 %collective-permute-start.60 = (f32[6,48]{1,0:T(8,128)S(1)}, f32[6,48]{1,0:T(8,128)S(1)}, u32[]{:S(2)}, u32[]{:S(2)}) collective-permute-start(f32[6,48]{1,0:T(8,128)S(1)} %get-tuple-element.203), channel_id=1, source_target_pairs={{0,2},{1,3},{2,0},{3,1},{4,6},{5,7},{6,4},{7,5},{8,10},{9,11},{10,... | collective-permute-start | bytes 3464 | tf_op jit(solution)/shard_map/ppermute | solution.py:522
  243.5 8.0 %collective-permute-start.61 = (f32[6,48]{1,0:T(8,128)S(1)}, f32[6,48]{1,0:T(8,128)S(1)}, u32[]{:S(2)}, u32[]{:S(2)}) collective-permute-start(f32[6,48]{1,0:T(8,128)S(1)} %get-tuple-element.204), channel_id=1, source_target_pairs={{0,3},{1,2},{2,1},{3,0},{4,7},{5,6},{6,5},{7,4},{8,11},{9,10},{10,... | collective-permute-start | bytes 3464 | tf_op jit(solution)/shard_map/ppermute | solution.py:522
  (66 other events, 509.1 us)
Sparse Core Ops, SparseCore 0:
  10.2 34.3 all-gather.3
  46.7 30.7 all-gather.5
  79.1 30.7 all-gather.7
  138.3 27.9 reduce-scatter.2
  190.8 42.3 reduce-scatter.4

commit v3 on v2

--- a/solution.py
+++ b/solution.py
@@ -660,7 +660,7 @@
         return call(
             functools.partial(join_body, dp),
             [struct((dp, rows_each, hidden), BF16), struct(passing.shape, passing.dtype)],
-            "join", 0, [keeps[0], *map(distant, keeps[1:]), sends[0], *map(distant, sends[1:]), passing], after=after,
+            "join", 0, [keeps[0], *map(distant, keeps[1:]), *sends, passing], after=after,
         )
 
     def over_dp(joined):
@@ -697,7 +697,7 @@
         mlp_pair = mlp_grads(received)
         dh, dh_low, sums_mid = call(
             functools.partial(middle_back_body, tensor),
-            [Kept((rows, width), F32), struct((rows, width), BF16), struct((4, width), F32)],
+            [Kept((rows, width), F32), struct((rows, width), BF16), Kept((4, width), F32)],
             "middle_back", 0, [e, Far(h), own, *received, params],
             after=[mlp_pair[0]],
         )
@@ -705,7 +705,7 @@
             joined, dh_low = joined_halves([mlp_pair], dh_low)
             mlp_1 = over_dp(joined)
         else:
-            joined, dh_low = joined_halves([mlp_pair, *pairs], dh_low, [mlp_1])
+            joined, dh_low = joined_halves([mlp_pair, *pairs], dh_low, [distant(mlp_1)])
             mix = over_dp(joined)
         dhs = everywhere(dh_low)
         dh_all, dqkv, qv_sums, own, *away = call(
@@ -733,7 +733,7 @@
             "attn_grads", 3 * unit,
             [
                 meta, Far(x_all), Far(dh_all), Far(a), Far(oqkv), Far(dqkv), attn_w,
-                sums_mid, hidden_sum, qv_sums,
+                distant(sums_mid), hidden_sum, qv_sums,
             ],
             [smem] + [vmem] * 5 + [hbm] + [vmem] * 3,
             [pltpu.VMEM((width, 4 * head_cols), F32), *attn_room],

time: 261 us -> 261 us (level)
    unnamed x45 -> x41, local copies, waits for them, and re-layouts: 6.98 us -> 6.53 us
where the time goes in v3:
time: 261 us; the launch traced here: 260 us
  waiting for transfers between devices  97.9 us (38%)
  starting transfers between devices  76.3 us (29%)
  Pallas kernels  60.4 us (23%)
  between operations  14.5 us (6%)
  local copies, waits for them, and re-layouts  7.88 us (3%)
  other arithmetic  2.8 us (1%)
    pallas_call x28, Pallas kernels, call(): pl.pallas_call(kernel, out_shape=tuple((pltpu.HBM(o.shape, o.dtype) if is...  60.4 us
    ppermute x48, starting transfers between devices, to_tensor(): lax.ppermute(v, 'tensor', [(i, i ^ k) for i in range(tensor)])  57.4 us
    ppermute x48, waiting for transfers between devices, to_tensor(): lax.ppermute(v, 'tensor', [(i, i ^ k) for i in range(tensor)])  46 us
    all_gather x1, waiting for transfers between devices, shards(): lax.all_gather(attn_piece, here, axis=0, tiled=True).reshape(2, width, -1)  17.8 us
    all_gather x2, waiting for transfers between devices, shards(): lax.all_gather(part.reshape(2 * half, hidden), here, axis=0, tiled=True)  13 us
    ppermute x3, starting transfers between devices, to_dp(): lax.ppermute(v, ('section', 'dp'), [(layer * dp + i, layer * dp + (i ^ k)...  10.1 us
    reduce_scatter x2, waiting for transfers between devices, over_dp(): return lax.psum_scatter(joined, 'dp', scatter_dimension=0, tiled=True)  7.84 us
    unnamed x41, local copies, waits for them, and re-layouts  6.53 us
  transfers between devices with their start and end apart: 68, of which 44 were waited for; matrix products, arithmetic and copies ran while one was open for 2% of the time, Pallas kernels for 19%

profile of v3, /device:TPU:0, one launch (start us, length us, event | category | flops | bytes accessed | tf_op | source)
XLA Modules:
  0.0 259.7 jit_solution(12319573553498918600)
XLA Ops:
  13.0 4.0 %collective-permute-start.4 = (bf16[16,192]{1,0:T(8,128)(2,1)S(1)}, bf16[16,192]{1,0:T(8,128)(2,1)S(1)}, u32[]{:S(2)}, u32[]{:S(2)}) collective-permute-start(bf16[16,192]{1,0:T(8,128)(2,1)S(1)} %pad.9), channel_id=1, source_target_pairs={{0,8},{4,12},{8,0},{12,4},{1,9},{5,13},{9,1},{13,5},{2,10},{6,14},... | collective-permute-start | bytes 18440 | tf_op jit(solution)/shard_map/ppermute | solution.py:559
  18.6 2.7 %collective-permute-start.2 = (bf16[64,768]{1,0:T(8,128)(2,1)S(1)}, bf16[64,768]{1,0:T(8,128)(2,1)S(1)}, u32[]{:S(2)}, u32[]{:S(2)}) collective-permute-start(bf16[64,768]{1,0:T(8,128)(2,1)S(1)} %dynamic-slice_bitcast_fusion.1.refs_0_.refs_1_), channel_id=1, source_target_pairs={{0,3},{1,2},{2,1},{3,0},{4,7},{5,6},{6,5},{7,4},{8,11},{9,10},{10,... | collective-permute-start | bytes 294920 | tf_op jit(solution)/shard_map/ppermute | solution.py:522
  26.8 17.8 %all-gather.4.cloned.1.call-done = bf16[1536,768]{1,0:T(8,128)(2,1)} async-done(((bf16[192,768]{1,0:T(8,128)(2,1)}), bf16[1536,768]{1,0:T(8,128)(2,1)}) %all-gather.4.cloned.1.call-update) | async-done | bytes 2359312 | tf_op jit(solution)/shard_map/all_gather | solution.py:590
  44.5 3.6 %attn_fwd.2 = (bf16[256,768]{1,0:T(8,128)(2,1)}, bf16[256,768]{1,0:T(8,128)(2,1)}, bf16[256,768]{1,0:T(8,128)(2,1)}, f32[256,128]{1,0:T(8,128)}, f32[64,768]{1,0...) custom-call(bf16[64,768]{1,0:T(8,128)(2,1)S(1)} %dynamic-slice_bitcast_fusion.1, ...), custom_call_target="tpu_custom_call" | custom-call | flops 603979776 | bytes 3039232 | tf_op jit(solution)/shard_map/attn_fwd/pallas_call | solution.py:136
  61.0 2.6 %collective-permute-done.12.refs_3_ = bf16[64,768]{1,0:T(8,128)(2,1)S(1)} collective-permute-done((bf16[64,768]{1,0:T(8,128)(2,1)S(1)}, bf16[64,768]{1,0:T(8,128)(2,1)S(1)}, u32[]{:S(2)}, u32[]{:S(2)}) %collective-permute-start.12) | collective-permute-done | bytes 98336 | tf_op jit(solution)/shard_map/ppermute | solution.py:522
  64.5 13.0 %all-gather.6.cloned.1.call-done = bf16[1536,768]{1,0:T(8,128)(2,1)} async-done(((bf16[192,768]{1,0:T(8,128)(2,1)}), bf16[1536,768]{1,0:T(8,128)(2,1)}) %all-gather.6.cloned.1.call-update) | async-done | bytes 2359312 | tf_op jit(solution)/shard_map/all_gather | solution.py:594
  77.5 3.3 %mlp_fwd.2 = (bf16[256,768]{1,0:T(8,128)(2,1)}, bf16[256,768]{1,0:T(8,128)(2,1)}, f32[256,768]{1,0:T(8,128)}, f32[64,768]{1,0:T(8,128)S(1)}, bf16[64,768]{1,0:T(...) custom-call(bf16[64,768]{1,0:T(8,128)(2,1)S(1)} %get-tuple-element.116.refs_0_, ...), custom_call_target="tpu_custom_call" | custom-call | flops 603979776 | bytes 2777088 | tf_op jit(solution)/shard_map/mlp_fwd/pallas_call | solution.py:136
  94.0 2.6 collective-permute-done.19.refs_3_
  97.5 3.6 %attn_fwd.3 = (bf16[256,768]{1,0:T(8,128)(2,1)}, bf16[256,768]{1,0:T(8,128)(2,1)}, bf16[256,768]{1,0:T(8,128)(2,1)}, f32[256,128]{1,0:T(8,128)}, f32[64,768]{1,0...) custom-call(bf16[64,768]{1,0:T(8,128)(2,1)S(1)} %end.1.refs_0_.refs_1_, ...), custom_call_target="tpu_custom_call" | custom-call | flops 603979776 | bytes 3039232 | tf_op jit(solution)/shard_map/attn_fwd/pallas_call | solution.py:136
  118.0 3.5 %mlp_fwd.3 = (bf16[256,768]{1,0:T(8,128)(2,1)}, bf16[256,768]{1,0:T(8,128)(2,1)}, f32[256,768]{1,0:T(8,128)}, f32[64,768]{1,0:T(8,128)}, bf16[64,768]{1,0:T(8,12...) custom-call(bf16[64,768]{1,0:T(8,128)(2,1)S(1)} %get-tuple-element.129.refs_0_, ...), custom_call_target="tpu_custom_call" | custom-call | flops 603979776 | bytes 2777088 | tf_op jit(solution)/shard_map/mlp_fwd/pallas_call | solution.py:136
  121.5 3.1 %mlp_bwd.2 = (bf16[256,768]{1,0:T(8,128)(2,1)}, bf16[256,768]{1,0:T(8,128)(2,1)}, f32[1,768]{1,0:T(1,128)S(1)}, f32[64,768]{1,0:T(8,128)S(1)}, bf16[64,768]{1,0:...) custom-call(bf16[64,768]{1,0:T(8,128)(2,1)S(1)} %dynamic-slice_bitcast_fusion.refs_0_, ...), custom_call_target="tpu_custom_call" | custom-call | flops 603979776 | bytes 3538944 | tf_op jit(solution)/shard_map/mlp_bwd/pallas_call | solution.py:136
  141.9 2.4 collective-permute-done.35.refs_3_
  146.3 4.2 %attn_bwd.2 = (bf16[256,768]{1,0:T(8,128)(2,1)}, bf16[256,768]{1,0:T(8,128)(2,1)}, f32[2,192]{1,0:T(2,128)S(1)}, f32[64,768]{1,0:T(8,128)S(1)}, bf16[64,768]{1,0...) custom-call(bf16[64,768]{1,0:T(8,128)(2,1)S(1)} %get-tuple-element.143.refs_0_, ...), custom_call_target="tpu_custom_call" | custom-call | flops 603979776 | bytes 3538944 | tf_op jit(solution)/shard_map/attn_bwd/pallas_call | solution.py:136
  164.4 3.7 %attn_grads.2 = (bf16[4,112,768]{2,1,0:T(8,128)(2,1)S(1)}, bf16[4,112,768]{2,1,0:T(8,128)(2,1)S(1)}) custom-call(s32[3]{0:T(128)S(1)} %pad_add_fusion.2.refs_0_, bf16[256,768]{1,0:T(8,128)(2,1)} %get-tuple-element.153.refs_1_, bf16[256,768]{1,0:T(8,128)(2,1)} %get-tuple-element.154.refs_2_, bf16[256,768]{1,0:T(8,128)(2,1)} %get-tuple-element.155.refs_3_, ...), custom_call_target="tpu_custom_call" | custom-call | flops 905969664 | bytes 4342284 | tf_op jit(solution)/shard_map/attn_grads/pallas_call | solution.py:136
  168.1 3.3 %mlp_bwd.3 = (bf16[256,768]{1,0:T(8,128)(2,1)}, bf16[256,768]{1,0:T(8,128)(2,1)}, f32[1,768]{1,0:T(1,128)S(1)}, f32[64,768]{1,0:T(8,128)S(1)}, bf16[64,768]{1,0:...) custom-call(bf16[64,768]{1,0:T(8,128)(2,1)S(1)} %get-tuple-element.151.refs_0_, ...), custom_call_target="tpu_custom_call" | custom-call | flops 603979776 | bytes 3538944 | tf_op jit(solution)/shard_map/mlp_bwd/pallas_call | solution.py:136
  194.3 3.0 %collective-permute-done.49.refs_3_ = bf16[64,768]{1,0:T(8,128)(2,1)S(1)} collective-permute-done((bf16[64,768]{1,0:T(8,128)(2,1)S(1)}, bf16[64,768]{1,0:T(8,128)(2,1)S(1)}, u32[]{:S(2)}, u32[]{:S(2)}) %collective-permute-start.49) | collective-permute-done | bytes 98336 | tf_op jit(solution)/shard_map/ppermute | solution.py:522
  198.6 4.3 %attn_bwd.3 = (bf16[256,768]{1,0:T(8,128)(2,1)}, bf16[256,768]{1,0:T(8,128)(2,1)}, f32[2,192]{1,0:T(2,128)S(1)}, f32[64,768]{1,0:T(8,128)S(1)}, bf16[128,768]{1,...) custom-call(bf16[64,768]{1,0:T(8,128)(2,1)S(1)} %get-tuple-element.175.refs_0_, ...), custom_call_target="tpu_custom_call" | custom-call | flops 603979776 | bytes 3833856 | tf_op jit(solution)/shard_map/attn_bwd/pallas_call | solution.py:136
  203.0 3.7 %attn_grads.3.refs_1_ = bf16[4,208,768]{2,1,0:T(8,128)(2,1)S(1)} custom-call(s32[3]{0:T(128)S(1)} %copy-done.10, bf16[256,768]{1,0:T(8,128)(2,1)} %get-tuple-element.187.refs_1_, bf16[256,768]{1,0:T(8,128)(2,1)} %get-tuple-element.188.refs_2_, bf16[256,768]{1,0:T(8,128)(2,1)} %get-tuple-element.189.refs_3_, ...), custom_call_target="tpu_custom_call" | custom-call | flops 905969664 | bytes 4342284 | tf_op jit(solution)/shard_map/attn_grads/pallas_call | solution.py:136
  208.1 3.6 %collective-permute-done.53.refs_2_ = bf16[4,208,768]{2,1,0:T(8,128)(2,1)S(1)} collective-permute-done((bf16[4,208,768]{2,1,0:T(8,128)(2,1)S(1)}, bf16[4,208,768]{2,1,0:T(8,128)(2,1)S(1)}, u32[]{:S(2)}, u32[]{:S(2)}) %collective-permute-start.53) | collective-permute-done | bytes 1277984 | tf_op jit(solution)/shard_map/ppermute | solution.py:538
  213.3 2.5 collective-permute-start.54
  215.8 3.4 %collective-permute-start.55 = (bf16[208,768]{1,0:T(8,128)(2,1)}, bf16[208,768]{1,0:T(8,128)(2,1)S(1)}, u32[]{:S(2)}, u32[]{:S(2)}) collective-permute-start(bf16[208,768]{1,0:T(8,128)(2,1)} %get-tuple-element.196), channel_id=1, source_target_pairs={{0,8},{4,12},{8,0},{12,4},{1,9},{5,13},{9,1},{13,5},{2,10},{6,14},... | collective-permute-start | bytes 958472 | tf_op jit(solution)/shard_map/ppermute | solution.py:531
  219.2 4.3 %collective-permute-start.56 = (bf16[208,768]{1,0:T(8,128)(2,1)}, bf16[208,768]{1,0:T(8,128)(2,1)S(1)}, u32[]{:S(2)}, u32[]{:S(2)}) collective-permute-start(bf16[208,768]{1,0:T(8,128)(2,1)} %get-tuple-element.197), channel_id=1, source_target_pairs={{0,12},{4,8},{8,4},{12,0},{1,13},{5,9},{9,5},{13,1},{2,14},{6,10},... | collective-permute-start | bytes 958472 | tf_op jit(solution)/shard_map/ppermute | solution.py:531
  225.4 7.8 %reduce-scatter.5.cloned.1.call-done.refs_1_.refs_2_ = bf16[304,768]{1,0:T(8,128)(2,1)} async-done(((bf16[1216,768]{1,0:T(8,128)(2,1)}), bf16[304,768]{1,0:T(8,128)(2,1)}) %reduce-scatter.5.cloned.1.call-update) | async-done | bytes 466960 | tf_op jit(solution)/shard_map/reduce_scatter | solution.py:668
  234.8 2.9 %collective-permute-start.52 = (bf16[128,768]{1,0:T(8,128)(2,1)S(1)}, bf16[128,768]{1,0:T(8,128)(2,1)S(1)}, u32[]{:S(2)}, u32[]{:S(2)}) collective-permute-start(bf16[128,768]{1,0:T(8,128)(2,1)S(1)} %get-tuple-element.184), channel_id=1, source_target_pairs={{0,3},{1,2},{2,1},{3,0},{4,7},{5,6},{6,5},{7,4},{8,11},{9,10},{10,... | collective-permute-start | bytes 589832 | tf_op jit(solution)/shard_map/ppermute | solution.py:522
  (212 shorter events, 136.5 us)
Async XLA Ops:
  7.2 37.4 %all-gather.4.cloned.1.call-start = ((), (), s32[]{:S(2)}) async-start(), calls=%async_computation.2 | async-start | bytes 2654208 | tf_op jit(solution)/shard_map/all_gather | solution.py:590
  9.5 68.0 %all-gather.6.cloned.1.call-start = ((), (), s32[]{:S(2)}) async-start(), calls=%async_computation.3 | async-start | bytes 2654208 | tf_op jit(solution)/shard_map/all_gather | solution.py:594
  12.1 104.8 %all-gather.8.cloned.1.call-start = ((), (), s32[]{:S(2)}) async-start(), calls=%async_computation.4 | async-start | bytes 2654208 | tf_op jit(solution)/shard_map/all_gather | solution.py:594
  12.9 173.8 %reduce-scatter.3.cloned.1.call-start = ((), (), s32[]{:S(2)}) async-start(), calls=%async_computation.5 | async-start | bytes 1474560 | tf_op jit(solution)/shard_map/reduce_scatter | solution.py:668
  13.0 9.1 %collective-permute-start.4 = (bf16[16,192]{1,0:T(8,128)(2,1)S(1)}, bf16[16,192]{1,0:T(8,128)(2,1)S(1)}, u32[]{:S(2)}, u32[]{:S(2)}) collective-permute-start(bf16[16,192]{1,0:T(8,128)(2,1)S(1)} %pad.9), channel_id=1, source_target_pairs={{0,8},{4,12},{8,0},{12,4},{1,9},{5,13},{9,1},{13,5},{2,10},{6,14},... | collective-permute-start | bytes 18440 | tf_op jit(solution)/shard_map/ppermute | solution.py:559
  18.6 7.5 %collective-permute-start.2 = (bf16[64,768]{1,0:T(8,128)(2,1)S(1)}, bf16[64,768]{1,0:T(8,128)(2,1)S(1)}, u32[]{:S(2)}, u32[]{:S(2)}) collective-permute-start(bf16[64,768]{1,0:T(8,128)(2,1)S(1)} %dynamic-slice_bitcast_fusion.1.refs_0_.refs_1_), channel_id=1, source_target_pairs={{0,3},{1,2},{2,1},{3,0},{4,7},{5,6},{6,5},{7,4},{8,11},{9,10},{10,... | collective-permute-start | bytes 294920 | tf_op jit(solution)/shard_map/ppermute | solution.py:522
  109.8 6.5 %collective-permute-start.28 = (bf16[64,768]{1,0:T(8,128)(2,1)S(1)}, bf16[64,768]{1,0:T(8,128)(2,1)S(1)}, u32[]{:S(2)}, u32[]{:S(2)}) collective-permute-start(bf16[64,768]{1,0:T(8,128)(2,1)S(1)} %get-tuple-element.129.refs_0_), channel_id=1, source_target_pairs={{0,3},{1,2},{2,1},{3,0},{4,7},{5,6},{6,5},{7,4},{8,11},{9,10},{10,... | collective-permute-start | bytes 294920 | tf_op jit(solution)/shard_map/ppermute | solution.py:522
  111.0 6.9 %collective-permute-start.27 = (bf16[64,768]{1,0:T(8,128)(2,1)S(1)}, bf16[64,768]{1,0:T(8,128)(2,1)S(1)}, u32[]{:S(2)}, u32[]{:S(2)}) collective-permute-start(bf16[64,768]{1,0:T(8,128)(2,1)S(1)} %get-tuple-element.129.refs_0_), channel_id=1, source_target_pairs={{0,2},{1,3},{2,0},{3,1},{4,6},{5,7},{6,4},{7,5},{8,10},{9,11},{10,... | collective-permute-start | bytes 294920 | tf_op jit(solution)/shard_map/ppermute | solution.py:522
  113.4 8.1 %collective-permute-start.25 = (bf16[64,768]{1,0:T(8,128)(2,1)S(1)}, bf16[64,768]{1,0:T(8,128)(2,1)S(1)}, u32[]{:S(2)}, u32[]{:S(2)}) collective-permute-start(bf16[64,768]{1,0:T(8,128)(2,1)S(1)} %dynamic-slice_bitcast_fusion.refs_0_), channel_id=1, source_target_pairs={{0,3},{1,2},{2,1},{3,0},{4,7},{5,6},{6,5},{7,4},{8,11},{9,10},{10,... | collective-permute-start | bytes 294920 | tf_op jit(solution)/shard_map/ppermute | solution.py:522
  114.6 6.9 %collective-permute-start.24 = (bf16[64,768]{1,0:T(8,128)(2,1)S(1)}, bf16[64,768]{1,0:T(8,128)(2,1)S(1)}, u32[]{:S(2)}, u32[]{:S(2)}) collective-permute-start(bf16[64,768]{1,0:T(8,128)(2,1)S(1)} %dynamic-slice_bitcast_fusion.refs_0_), channel_id=1, source_target_pairs={{0,2},{1,3},{2,0},{3,1},{4,6},{5,7},{6,4},{7,5},{8,10},{9,11},{10,... | collective-permute-start | bytes 294920 | tf_op jit(solution)/shard_map/ppermute | solution.py:522
  138.2 95.1 %reduce-scatter.5.cloned.1.call-start = ((), (), s32[]{:S(2)}) async-start(), calls=%async_computation.6 | async-start | bytes 2334720 | tf_op jit(solution)/shard_map/reduce_scatter | solution.py:668
  160.7 7.4 %collective-permute-start.41 = (bf16[64,768]{1,0:T(8,128)(2,1)S(1)}, bf16[64,768]{1,0:T(8,128)(2,1)S(1)}, u32[]{:S(2)}, u32[]{:S(2)}) collective-permute-start(bf16[64,768]{1,0:T(8,128)(2,1)S(1)} %get-tuple-element.151.refs_0_), channel_id=1, source_target_pairs={{0,3},{1,2},{2,1},{3,0},{4,7},{5,6},{6,5},{7,4},{8,11},{9,10},{10,... | collective-permute-start | bytes 294920 | tf_op jit(solution)/shard_map/ppermute | solution.py:522
  190.7 6.6 %collective-permute-start.49 = (bf16[64,768]{1,0:T(8,128)(2,1)S(1)}, bf16[64,768]{1,0:T(8,128)(2,1)S(1)}, u32[]{:S(2)}, u32[]{:S(2)}) collective-permute-start(bf16[64,768]{1,0:T(8,128)(2,1)S(1)} %get-tuple-element.175.refs_0_), channel_id=1, source_target_pairs={{0,3},{1,2},{2,1},{3,0},{4,7},{5,6},{6,5},{7,4},{8,11},{9,10},{10,... | collective-permute-start | bytes 294920 | tf_op jit(solution)/shard_map/ppermute | solution.py:522
  192.1 6.5 %collective-permute-start.48 = (bf16[64,768]{1,0:T(8,128)(2,1)S(1)}, bf16[64,768]{1,0:T(8,128)(2,1)S(1)}, u32[]{:S(2)}, u32[]{:S(2)}) collective-permute-start(bf16[64,768]{1,0:T(8,128)(2,1)S(1)} %get-tuple-element.175.refs_0_), channel_id=1, source_target_pairs={{0,2},{1,3},{2,0},{3,1},{4,6},{5,7},{6,4},{7,5},{8,10},{9,11},{10,... | collective-permute-start | bytes 294920 | tf_op jit(solution)/shard_map/ppermute | solution.py:522
  213.3 21.6 %collective-permute-start.54 = (bf16[208,768]{1,0:T(8,128)(2,1)}, bf16[208,768]{1,0:T(8,128)(2,1)S(1)}, u32[]{:S(2)}, u32[]{:S(2)}) collective-permute-start(bf16[208,768]{1,0:T(8,128)(2,1)} %get-tuple-element.195), channel_id=1, source_target_pairs={{0,4},{4,0},{8,12},{12,8},{1,5},{5,1},{9,13},{13,9},{2,6},{6,2},{1... | collective-permute-start | bytes 958472 | tf_op jit(solution)/shard_map/ppermute | solution.py:531
  215.8 22.0 %collective-permute-start.55 = (bf16[208,768]{1,0:T(8,128)(2,1)}, bf16[208,768]{1,0:T(8,128)(2,1)S(1)}, u32[]{:S(2)}, u32[]{:S(2)}) collective-permute-start(bf16[208,768]{1,0:T(8,128)(2,1)} %get-tuple-element.196), channel_id=1, source_target_pairs={{0,8},{4,12},{8,0},{12,4},{1,9},{5,13},{9,1},{13,5},{2,10},{6,14},... | collective-permute-start | bytes 958472 | tf_op jit(solution)/shard_map/ppermute | solution.py:531
  219.2 20.1 %collective-permute-start.56 = (bf16[208,768]{1,0:T(8,128)(2,1)}, bf16[208,768]{1,0:T(8,128)(2,1)S(1)}, u32[]{:S(2)}, u32[]{:S(2)}) collective-permute-start(bf16[208,768]{1,0:T(8,128)(2,1)} %get-tuple-element.197), channel_id=1, source_target_pairs={{0,12},{4,8},{8,4},{12,0},{1,13},{5,9},{9,5},{13,1},{2,14},{6,10},... | collective-permute-start | bytes 958472 | tf_op jit(solution)/shard_map/ppermute | solution.py:531
  223.4 18.6 %collective-permute-start.50 = (bf16[128,768]{1,0:T(8,128)(2,1)S(1)}, bf16[128,768]{1,0:T(8,128)(2,1)}, u32[]{:S(2)}, u32[]{:S(2)}) collective-permute-start(bf16[128,768]{1,0:T(8,128)(2,1)S(1)} %copy-done.14), channel_id=1, source_target_pairs={{0,1},{1,0},{2,3},{3,2},{4,5},{5,4},{6,7},{7,6},{8,9},{9,8},{10,11... | collective-permute-start | bytes 589832 | tf_op jit(solution)/shard_map/ppermute | solution.py:522
  224.4 19.1 %collective-permute-start.51 = (bf16[128,768]{1,0:T(8,128)(2,1)S(1)}, bf16[128,768]{1,0:T(8,128)(2,1)}, u32[]{:S(2)}, u32[]{:S(2)}) collective-permute-start(bf16[128,768]{1,0:T(8,128)(2,1)S(1)} %get-tuple-element.183), channel_id=1, source_target_pairs={{0,2},{1,3},{2,0},{3,1},{4,6},{5,7},{6,4},{7,5},{8,10},{9,11},{10,... | collective-permute-start | bytes 589832 | tf_op jit(solution)/shard_map/ppermute | solution.py:522
  234.8 9.2 %collective-permute-start.52 = (bf16[128,768]{1,0:T(8,128)(2,1)S(1)}, bf16[128,768]{1,0:T(8,128)(2,1)S(1)}, u32[]{:S(2)}, u32[]{:S(2)}) collective-permute-start(bf16[128,768]{1,0:T(8,128)(2,1)S(1)} %get-tuple-element.184), channel_id=1, source_target_pairs={{0,3},{1,2},{2,1},{3,0},{4,7},{5,6},{6,5},{7,4},{8,11},{9,10},{10,... | collective-permute-start | bytes 589832 | tf_op jit(solution)/shard_map/ppermute | solution.py:522
  237.8 11.6 %collective-permute-start.62 = (bf16[288,768]{1,0:T(8,128)(2,1)S(1)}, bf16[288,768]{1,0:T(8,128)(2,1)S(1)}, u32[]{:S(2)}, u32[]{:S(2)}) collective-permute-start(bf16[288,768]{1,0:T(8,128)(2,1)S(1)} %turn.1), channel_id=1, source_target_pairs={{0,16},{16,0},{1,17},{17,1},{2,18},{18,2},{3,19},{19,3},{4,20},{20... | collective-permute-start | bytes 1327112 | tf_op jit(solution)/shard_map/ppermute | solution.py:655
  240.0 11.5 %collective-permute-start.59 = (f32[6,48]{1,0:T(8,128)S(1)}, f32[6,48]{1,0:T(8,128)S(1)}, u32[]{:S(2)}, u32[]{:S(2)}) collective-permute-start(f32[6,48]{1,0:T(8,128)S(1)} %get-tuple-element.202), channel_id=1, source_target_pairs={{0,1},{1,0},{2,3},{3,2},{4,5},{5,4},{6,7},{7,6},{8,9},{9,8},{10,11... | collective-permute-start | bytes 3464 | tf_op jit(solution)/shard_map/ppermute | solution.py:522
  242.1 9.4 %collective-permute-start.60 = (f32[6,48]{1,0:T(8,128)S(1)}, f32[6,48]{1,0:T(8,128)S(1)}, u32[]{:S(2)}, u32[]{:S(2)}) collective-permute-start(f32[6,48]{1,0:T(8,128)S(1)} %get-tuple-element.203), channel_id=1, source_target_pairs={{0,2},{1,3},{2,0},{3,1},{4,6},{5,7},{6,4},{7,5},{8,10},{9,11},{10,... | collective-permute-start | bytes 3464 | tf_op jit(solution)/shard_map/ppermute | solution.py:522
  243.5 8.0 %collective-permute-start.61 = (f32[6,48]{1,0:T(8,128)S(1)}, f32[6,48]{1,0:T(8,128)S(1)}, u32[]{:S(2)}, u32[]{:S(2)}) collective-permute-start(f32[6,48]{1,0:T(8,128)S(1)} %get-tuple-element.204), channel_id=1, source_target_pairs={{0,3},{1,2},{2,1},{3,0},{4,7},{5,6},{6,5},{7,4},{8,11},{9,10},{10,... | collective-permute-start | bytes 3464 | tf_op jit(solution)/shard_map/ppermute | solution.py:522
  (64 other events, 504.3 us)
Sparse Core Ops, SparseCore 0:
  10.2 34.3 all-gather.3
  46.7 30.7 all-gather.5
  79.1 30.7 all-gather.7
  138.3 27.9 reduce-scatter.2
  190.8 42.3 reduce-scatter.4

commit v4 on v3

--- a/solution.py
+++ b/solution.py
@@ -398,8 +398,11 @@
     low_out[...] = grad.astype(BF16)
 
 
-def prepare_body(meta, w_qkv, w_out, w_fc1, w_fc2, attn_out, keep, send):
+def prepare_attn_body(w_qkv, w_out, attn_out):
     attn_out[...] = jnp.concatenate([w_out[...].T, w_qkv[0], w_qkv[1], w_qkv[2]], axis=1)
+
+
+def prepare_mlp_body(meta, w_fc1, w_fc2, keep, send):
     half = keep.shape[1]
     first = meta[0] == 0
     for g, values in enumerate((w_fc1[...], w_fc2[...])):
@@ -580,11 +583,13 @@
             smalls.append(jnp.concatenate([whole[:7], bias], axis=0))
 
     half = piece // 2
-    attn_piece, keep, send = call(
-        prepare_body,
-        [struct((piece, 4 * head_cols), BF16)] + [struct((2, half, hidden), BF16)] * 2,
-        "prepare", 0, [meta, *(Far(v) for v in (w_qkv[0], w_out[0], w_fc1[0], w_fc2[0].T))],
-        [smem] + [vmem] * 4,
+    (attn_piece,) = call(
+        prepare_attn_body, [struct((piece, 4 * head_cols), BF16)], "prepare_attn", 0,
+        [Far(w_qkv[0]), Far(w_out[0])],
+    )
+    keep, send = call(
+        prepare_mlp_body, [struct((2, half, hidden), BF16)] * 2, "prepare_mlp", 0,
+        [meta, Far(w_fc1[0]), Far(w_fc2[0].T)], [smem, vmem, vmem], after=[attn_piece],
     )
     here = ("section", "dp")
     attn_w = distant(lax.all_gather(attn_piece, here, axis=0, tiled=True).reshape(2, width, -1))

time: 261 us -> 261 us (level)
    pallas_call x28 -> x29, Pallas kernels: 60.4 us -> 61.3 us  [call(): pl.pallas_call(kernel, out_shape=tuple((pltpu.HBM(o.shape, o.dtype) if is...]
  transfers between devices with their start and end apart: 68 -> 68, of which waited for: 44 -> 44; matrix products, arithmetic and copies ran while one was open for 2% -> 2% of each run, Pallas kernels for 19% -> 20%
where the time goes in v4:
time: 261 us; the launch traced here: 260 us
  waiting for transfers between devices  97.2 us (37%)
  starting transfers between devices  76.1 us (29%)
  Pallas kernels  61.3 us (23%)
  between operations  14.5 us (6%)
  local copies, waits for them, and re-layouts  7.87 us (3%)
  other arithmetic  2.8 us (1%)
    pallas_call x29, Pallas kernels, call(): pl.pallas_call(kernel, out_shape=tuple((pltpu.HBM(o.shape, o.dtype) if is...  61.3 us
    ppermute x48, starting transfers between devices, to_tensor(): lax.ppermute(v, 'tensor', [(i, i ^ k) for i in range(tensor)])  57.1 us
    ppermute x48, waiting for transfers between devices, to_tensor(): lax.ppermute(v, 'tensor', [(i, i ^ k) for i in range(tensor)])  46 us
    all_gather x1, waiting for transfers between devices, shards(): lax.all_gather(attn_piece, here, axis=0, tiled=True).reshape(2, width, -1)  17.1 us
    all_gather x2, waiting for transfers between devices, shards(): lax.all_gather(part.reshape(2 * half, hidden), here, axis=0, tiled=True)  12.8 us
    ppermute x3, starting transfers between devices, to_dp(): lax.ppermute(v, ('section', 'dp'), [(layer * dp + i, layer * dp + (i ^ k)...  10.1 us
    reduce_scatter x2, waiting for transfers between devices, over_dp(): return lax.psum_scatter(joined, 'dp', scatter_dimension=0, tiled=True)  7.72 us
    unnamed x41, local copies, waits for them, and re-layouts  6.52 us
  transfers between devices with their start and end apart: 68, of which 44 were waited for; matrix products, arithmetic and copies ran while one was open for 2% of the time, Pallas kernels for 20%

profile of v4, /device:TPU:0, one launch (start us, length us, event | category | flops | bytes accessed | tf_op | source)
XLA Modules:
  0.0 259.8 jit_solution(11648248150100385700)
XLA Ops:
  13.9 4.0 %collective-permute-start.4 = (bf16[16,192]{1,0:T(8,128)(2,1)S(1)}, bf16[16,192]{1,0:T(8,128)(2,1)S(1)}, u32[]{:S(2)}, u32[]{:S(2)}) collective-permute-start(bf16[16,192]{1,0:T(8,128)(2,1)S(1)} %pad.9), channel_id=1, source_target_pairs={{0,8},{4,12},{8,0},{12,4},{1,9},{5,13},{9,1},{13,5},{2,10},{6,14},... | collective-permute-start | bytes 18440 | tf_op jit(solution)/shard_map/ppermute | solution.py:562
  19.6 2.7 %collective-permute-start.2 = (bf16[64,768]{1,0:T(8,128)(2,1)S(1)}, bf16[64,768]{1,0:T(8,128)(2,1)S(1)}, u32[]{:S(2)}, u32[]{:S(2)}) collective-permute-start(bf16[64,768]{1,0:T(8,128)(2,1)S(1)} %dynamic-slice_bitcast_fusion.1.refs_0_.refs_1_), channel_id=1, source_target_pairs={{0,3},{1,2},{2,1},{3,0},{4,7},{5,6},{6,5},{7,4},{8,11},{9,10},{10,... | collective-permute-start | bytes 294920 | tf_op jit(solution)/shard_map/ppermute | solution.py:525
  27.7 17.1 %all-gather.4.cloned.1.call-done = bf16[1536,768]{1,0:T(8,128)(2,1)} async-done(((bf16[192,768]{1,0:T(8,128)(2,1)}), bf16[1536,768]{1,0:T(8,128)(2,1)}) %all-gather.4.cloned.1.call-update) | async-done | bytes 2359312 | tf_op jit(solution)/shard_map/all_gather | solution.py:595
  44.8 3.6 %attn_fwd.2 = (bf16[256,768]{1,0:T(8,128)(2,1)}, bf16[256,768]{1,0:T(8,128)(2,1)}, bf16[256,768]{1,0:T(8,128)(2,1)}, f32[256,128]{1,0:T(8,128)}, f32[64,768]{1,0...) custom-call(bf16[64,768]{1,0:T(8,128)(2,1)S(1)} %dynamic-slice_bitcast_fusion.1, ...), custom_call_target="tpu_custom_call" | custom-call | flops 603979776 | bytes 3039232 | tf_op jit(solution)/shard_map/attn_fwd/pallas_call | solution.py:136
  61.1 2.5 collective-permute-done.12.refs_3_
  64.7 12.8 %all-gather.6.cloned.1.call-done = bf16[1536,768]{1,0:T(8,128)(2,1)} async-done(((bf16[192,768]{1,0:T(8,128)(2,1)}), bf16[1536,768]{1,0:T(8,128)(2,1)}) %all-gather.6.cloned.1.call-update) | async-done | bytes 2359312 | tf_op jit(solution)/shard_map/all_gather | solution.py:599
  77.5 3.3 %mlp_fwd.2 = (bf16[256,768]{1,0:T(8,128)(2,1)}, bf16[256,768]{1,0:T(8,128)(2,1)}, f32[256,768]{1,0:T(8,128)}, f32[64,768]{1,0:T(8,128)S(1)}, bf16[64,768]{1,0:T(...) custom-call(bf16[64,768]{1,0:T(8,128)(2,1)S(1)} %get-tuple-element.114.refs_0_, ...), custom_call_target="tpu_custom_call" | custom-call | flops 603979776 | bytes 2777088 | tf_op jit(solution)/shard_map/mlp_fwd/pallas_call | solution.py:136
  94.0 2.6 collective-permute-done.19.refs_3_
  97.5 3.6 %attn_fwd.3 = (bf16[256,768]{1,0:T(8,128)(2,1)}, bf16[256,768]{1,0:T(8,128)(2,1)}, bf16[256,768]{1,0:T(8,128)(2,1)}, f32[256,128]{1,0:T(8,128)}, f32[64,768]{1,0...) custom-call(bf16[64,768]{1,0:T(8,128)(2,1)S(1)} %end.1.refs_0_.refs_1_, ...), custom_call_target="tpu_custom_call" | custom-call | flops 603979776 | bytes 3039232 | tf_op jit(solution)/shard_map/attn_fwd/pallas_call | solution.py:136
  118.2 3.5 %mlp_fwd.3 = (bf16[256,768]{1,0:T(8,128)(2,1)}, bf16[256,768]{1,0:T(8,128)(2,1)}, f32[256,768]{1,0:T(8,128)}, f32[64,768]{1,0:T(8,128)}, bf16[64,768]{1,0:T(8,12...) custom-call(bf16[64,768]{1,0:T(8,128)(2,1)S(1)} %get-tuple-element.127.refs_0_, ...), custom_call_target="tpu_custom_call" | custom-call | flops 603979776 | bytes 2777088 | tf_op jit(solution)/shard_map/mlp_fwd/pallas_call | solution.py:136
  121.8 3.1 %mlp_bwd.2 = (bf16[256,768]{1,0:T(8,128)(2,1)}, bf16[256,768]{1,0:T(8,128)(2,1)}, f32[1,768]{1,0:T(1,128)S(1)}, f32[64,768]{1,0:T(8,128)S(1)}, bf16[64,768]{1,0:...) custom-call(bf16[64,768]{1,0:T(8,128)(2,1)S(1)} %dynamic-slice_bitcast_fusion.refs_0_, ...), custom_call_target="tpu_custom_call" | custom-call | flops 603979776 | bytes 3538944 | tf_op jit(solution)/shard_map/mlp_bwd/pallas_call | solution.py:136
  142.2 2.4 collective-permute-done.35.refs_3_
  146.6 4.2 %attn_bwd.2 = (bf16[256,768]{1,0:T(8,128)(2,1)}, bf16[256,768]{1,0:T(8,128)(2,1)}, f32[2,192]{1,0:T(2,128)S(1)}, f32[64,768]{1,0:T(8,128)S(1)}, bf16[64,768]{1,0...) custom-call(bf16[64,768]{1,0:T(8,128)(2,1)S(1)} %get-tuple-element.141.refs_0_, ...), custom_call_target="tpu_custom_call" | custom-call | flops 603979776 | bytes 3538944 | tf_op jit(solution)/shard_map/attn_bwd/pallas_call | solution.py:136
  164.5 3.7 %attn_grads.2 = (bf16[4,112,768]{2,1,0:T(8,128)(2,1)S(1)}, bf16[4,112,768]{2,1,0:T(8,128)(2,1)S(1)}) custom-call(s32[3]{0:T(128)S(1)} %pad_add_fusion.2.refs_0_, bf16[256,768]{1,0:T(8,128)(2,1)} %get-tuple-element.151.refs_1_, bf16[256,768]{1,0:T(8,128)(2,1)} %get-tuple-element.152.refs_2_, bf16[256,768]{1,0:T(8,128)(2,1)} %get-tuple-element.153.refs_3_, ...), custom_call_target="tpu_custom_call" | custom-call | flops 905969664 | bytes 4342284 | tf_op jit(solution)/shard_map/attn_grads/pallas_call | solution.py:136
  168.2 3.3 %mlp_bwd.3 = (bf16[256,768]{1,0:T(8,128)(2,1)}, bf16[256,768]{1,0:T(8,128)(2,1)}, f32[1,768]{1,0:T(1,128)S(1)}, f32[64,768]{1,0:T(8,128)S(1)}, bf16[64,768]{1,0:...) custom-call(bf16[64,768]{1,0:T(8,128)(2,1)S(1)} %get-tuple-element.149.refs_0_, ...), custom_call_target="tpu_custom_call" | custom-call | flops 603979776 | bytes 3538944 | tf_op jit(solution)/shard_map/mlp_bwd/pallas_call | solution.py:136
  194.3 3.0 %collective-permute-done.49.refs_3_ = bf16[64,768]{1,0:T(8,128)(2,1)S(1)} collective-permute-done((bf16[64,768]{1,0:T(8,128)(2,1)S(1)}, bf16[64,768]{1,0:T(8,128)(2,1)S(1)}, u32[]{:S(2)}, u32[]{:S(2)}) %collective-permute-start.49) | collective-permute-done | bytes 98336 | tf_op jit(solution)/shard_map/ppermute | solution.py:525
  198.7 4.3 %attn_bwd.3 = (bf16[256,768]{1,0:T(8,128)(2,1)}, bf16[256,768]{1,0:T(8,128)(2,1)}, f32[2,192]{1,0:T(2,128)S(1)}, f32[64,768]{1,0:T(8,128)S(1)}, bf16[128,768]{1,...) custom-call(bf16[64,768]{1,0:T(8,128)(2,1)S(1)} %get-tuple-element.173.refs_0_, ...), custom_call_target="tpu_custom_call" | custom-call | flops 603979776 | bytes 3833856 | tf_op jit(solution)/shard_map/attn_bwd/pallas_call | solution.py:136
  203.0 3.6 %attn_grads.3.refs_1_ = bf16[4,208,768]{2,1,0:T(8,128)(2,1)S(1)} custom-call(s32[3]{0:T(128)S(1)} %copy-done.10, bf16[256,768]{1,0:T(8,128)(2,1)} %get-tuple-element.185.refs_1_, bf16[256,768]{1,0:T(8,128)(2,1)} %get-tuple-element.186.refs_2_, bf16[256,768]{1,0:T(8,128)(2,1)} %get-tuple-element.187.refs_3_, ...), custom_call_target="tpu_custom_call" | custom-call | flops 905969664 | bytes 4342284 | tf_op jit(solution)/shard_map/attn_grads/pallas_call | solution.py:136
  208.2 3.6 %collective-permute-done.53.refs_2_ = bf16[4,208,768]{2,1,0:T(8,128)(2,1)S(1)} collective-permute-done((bf16[4,208,768]{2,1,0:T(8,128)(2,1)S(1)}, bf16[4,208,768]{2,1,0:T(8,128)(2,1)S(1)}, u32[]{:S(2)}, u32[]{:S(2)}) %collective-permute-start.53) | collective-permute-done | bytes 1277984 | tf_op jit(solution)/shard_map/ppermute | solution.py:541
  213.4 2.5 collective-permute-start.54
  215.8 3.4 %collective-permute-start.55 = (bf16[208,768]{1,0:T(8,128)(2,1)}, bf16[208,768]{1,0:T(8,128)(2,1)S(1)}, u32[]{:S(2)}, u32[]{:S(2)}) collective-permute-start(bf16[208,768]{1,0:T(8,128)(2,1)} %get-tuple-element.194), channel_id=1, source_target_pairs={{0,8},{4,12},{8,0},{12,4},{1,9},{5,13},{9,1},{13,5},{2,10},{6,14},... | collective-permute-start | bytes 958472 | tf_op jit(solution)/shard_map/ppermute | solution.py:534
  219.2 4.3 %collective-permute-start.56 = (bf16[208,768]{1,0:T(8,128)(2,1)}, bf16[208,768]{1,0:T(8,128)(2,1)S(1)}, u32[]{:S(2)}, u32[]{:S(2)}) collective-permute-start(bf16[208,768]{1,0:T(8,128)(2,1)} %get-tuple-element.195), channel_id=1, source_target_pairs={{0,12},{4,8},{8,4},{12,0},{1,13},{5,9},{9,5},{13,1},{2,14},{6,10},... | collective-permute-start | bytes 958472 | tf_op jit(solution)/shard_map/ppermute | solution.py:534
  225.5 7.7 %reduce-scatter.5.cloned.1.call-done.refs_1_.refs_2_ = bf16[304,768]{1,0:T(8,128)(2,1)} async-done(((bf16[1216,768]{1,0:T(8,128)(2,1)}), bf16[304,768]{1,0:T(8,128)(2,1)}) %reduce-scatter.5.cloned.1.call-update) | async-done | bytes 466960 | tf_op jit(solution)/shard_map/reduce_scatter | solution.py:673
  234.8 2.9 %collective-permute-start.52 = (bf16[128,768]{1,0:T(8,128)(2,1)S(1)}, bf16[128,768]{1,0:T(8,128)(2,1)S(1)}, u32[]{:S(2)}, u32[]{:S(2)}) collective-permute-start(bf16[128,768]{1,0:T(8,128)(2,1)S(1)} %get-tuple-element.182), channel_id=1, source_target_pairs={{0,3},{1,2},{2,1},{3,0},{4,7},{5,6},{6,5},{7,4},{8,11},{9,10},{10,... | collective-permute-start | bytes 589832 | tf_op jit(solution)/shard_map/ppermute | solution.py:525
  (213 shorter events, 137.6 us)
Async XLA Ops:
  7.2 37.6 %all-gather.4.cloned.1.call-start = ((), (), s32[]{:S(2)}) async-start(), calls=%async_computation.2 | async-start | bytes 2654208 | tf_op jit(solution)/shard_map/all_gather | solution.py:595
  9.2 68.4 %all-gather.6.cloned.1.call-start = ((), (), s32[]{:S(2)}) async-start(), calls=%async_computation.3 | async-start | bytes 2654208 | tf_op jit(solution)/shard_map/all_gather | solution.py:599
  13.1 103.8 %all-gather.8.cloned.1.call-start = ((), (), s32[]{:S(2)}) async-start(), calls=%async_computation.4 | async-start | bytes 2654208 | tf_op jit(solution)/shard_map/all_gather | solution.py:599
  13.8 173.0 %reduce-scatter.3.cloned.1.call-start = ((), (), s32[]{:S(2)}) async-start(), calls=%async_computation.5 | async-start | bytes 1474560 | tf_op jit(solution)/shard_map/reduce_scatter | solution.py:673
  13.9 9.1 %collective-permute-start.4 = (bf16[16,192]{1,0:T(8,128)(2,1)S(1)}, bf16[16,192]{1,0:T(8,128)(2,1)S(1)}, u32[]{:S(2)}, u32[]{:S(2)}) collective-permute-start(bf16[16,192]{1,0:T(8,128)(2,1)S(1)} %pad.9), channel_id=1, source_target_pairs={{0,8},{4,12},{8,0},{12,4},{1,9},{5,13},{9,1},{13,5},{2,10},{6,14},... | collective-permute-start | bytes 18440 | tf_op jit(solution)/shard_map/ppermute | solution.py:562
  19.6 7.6 %collective-permute-start.2 = (bf16[64,768]{1,0:T(8,128)(2,1)S(1)}, bf16[64,768]{1,0:T(8,128)(2,1)S(1)}, u32[]{:S(2)}, u32[]{:S(2)}) collective-permute-start(bf16[64,768]{1,0:T(8,128)(2,1)S(1)} %dynamic-slice_bitcast_fusion.1.refs_0_.refs_1_), channel_id=1, source_target_pairs={{0,3},{1,2},{2,1},{3,0},{4,7},{5,6},{6,5},{7,4},{8,11},{9,10},{10,... | collective-permute-start | bytes 294920 | tf_op jit(solution)/shard_map/ppermute | solution.py:525
  109.8 6.7 %collective-permute-start.28 = (bf16[64,768]{1,0:T(8,128)(2,1)S(1)}, bf16[64,768]{1,0:T(8,128)(2,1)S(1)}, u32[]{:S(2)}, u32[]{:S(2)}) collective-permute-start(bf16[64,768]{1,0:T(8,128)(2,1)S(1)} %get-tuple-element.127.refs_0_), channel_id=1, source_target_pairs={{0,3},{1,2},{2,1},{3,0},{4,7},{5,6},{6,5},{7,4},{8,11},{9,10},{10,... | collective-permute-start | bytes 294920 | tf_op jit(solution)/shard_map/ppermute | solution.py:525
  111.0 7.2 %collective-permute-start.27 = (bf16[64,768]{1,0:T(8,128)(2,1)S(1)}, bf16[64,768]{1,0:T(8,128)(2,1)S(1)}, u32[]{:S(2)}, u32[]{:S(2)}) collective-permute-start(bf16[64,768]{1,0:T(8,128)(2,1)S(1)} %get-tuple-element.127.refs_0_), channel_id=1, source_target_pairs={{0,2},{1,3},{2,0},{3,1},{4,6},{5,7},{6,4},{7,5},{8,10},{9,11},{10,... | collective-permute-start | bytes 294920 | tf_op jit(solution)/shard_map/ppermute | solution.py:525
  113.4 8.4 %collective-permute-start.25 = (bf16[64,768]{1,0:T(8,128)(2,1)S(1)}, bf16[64,768]{1,0:T(8,128)(2,1)S(1)}, u32[]{:S(2)}, u32[]{:S(2)}) collective-permute-start(bf16[64,768]{1,0:T(8,128)(2,1)S(1)} %dynamic-slice_bitcast_fusion.refs_0_), channel_id=1, source_target_pairs={{0,3},{1,2},{2,1},{3,0},{4,7},{5,6},{6,5},{7,4},{8,11},{9,10},{10,... | collective-permute-start | bytes 294920 | tf_op jit(solution)/shard_map/ppermute | solution.py:525
  114.6 7.1 %collective-permute-start.24 = (bf16[64,768]{1,0:T(8,128)(2,1)S(1)}, bf16[64,768]{1,0:T(8,128)(2,1)S(1)}, u32[]{:S(2)}, u32[]{:S(2)}) collective-permute-start(bf16[64,768]{1,0:T(8,128)(2,1)S(1)} %dynamic-slice_bitcast_fusion.refs_0_), channel_id=1, source_target_pairs={{0,2},{1,3},{2,0},{3,1},{4,6},{5,7},{6,4},{7,5},{8,10},{9,11},{10,... | collective-permute-start | bytes 294920 | tf_op jit(solution)/shard_map/ppermute | solution.py:525
  138.4 94.8 %reduce-scatter.5.cloned.1.call-start = ((), (), s32[]{:S(2)}) async-start(), calls=%async_computation.6 | async-start | bytes 2334720 | tf_op jit(solution)/shard_map/reduce_scatter | solution.py:673
  160.8 7.4 %collective-permute-start.41 = (bf16[64,768]{1,0:T(8,128)(2,1)S(1)}, bf16[64,768]{1,0:T(8,128)(2,1)S(1)}, u32[]{:S(2)}, u32[]{:S(2)}) collective-permute-start(bf16[64,768]{1,0:T(8,128)(2,1)S(1)} %get-tuple-element.149.refs_0_), channel_id=1, source_target_pairs={{0,3},{1,2},{2,1},{3,0},{4,7},{5,6},{6,5},{7,4},{8,11},{9,10},{10,... | collective-permute-start | bytes 294920 | tf_op jit(solution)/shard_map/ppermute | solution.py:525
  190.8 6.6 %collective-permute-start.49 = (bf16[64,768]{1,0:T(8,128)(2,1)S(1)}, bf16[64,768]{1,0:T(8,128)(2,1)S(1)}, u32[]{:S(2)}, u32[]{:S(2)}) collective-permute-start(bf16[64,768]{1,0:T(8,128)(2,1)S(1)} %get-tuple-element.173.refs_0_), channel_id=1, source_target_pairs={{0,3},{1,2},{2,1},{3,0},{4,7},{5,6},{6,5},{7,4},{8,11},{9,10},{10,... | collective-permute-start | bytes 294920 | tf_op jit(solution)/shard_map/ppermute | solution.py:525
  192.2 6.5 %collective-permute-start.48 = (bf16[64,768]{1,0:T(8,128)(2,1)S(1)}, bf16[64,768]{1,0:T(8,128)(2,1)S(1)}, u32[]{:S(2)}, u32[]{:S(2)}) collective-permute-start(bf16[64,768]{1,0:T(8,128)(2,1)S(1)} %get-tuple-element.173.refs_0_), channel_id=1, source_target_pairs={{0,2},{1,3},{2,0},{3,1},{4,6},{5,7},{6,4},{7,5},{8,10},{9,11},{10,... | collective-permute-start | bytes 294920 | tf_op jit(solution)/shard_map/ppermute | solution.py:525
  213.4 21.5 %collective-permute-start.54 = (bf16[208,768]{1,0:T(8,128)(2,1)}, bf16[208,768]{1,0:T(8,128)(2,1)S(1)}, u32[]{:S(2)}, u32[]{:S(2)}) collective-permute-start(bf16[208,768]{1,0:T(8,128)(2,1)} %get-tuple-element.193), channel_id=1, source_target_pairs={{0,4},{4,0},{8,12},{12,8},{1,5},{5,1},{9,13},{13,9},{2,6},{6,2},{1... | collective-permute-start | bytes 958472 | tf_op jit(solution)/shard_map/ppermute | solution.py:534
  215.8 21.9 %collective-permute-start.55 = (bf16[208,768]{1,0:T(8,128)(2,1)}, bf16[208,768]{1,0:T(8,128)(2,1)S(1)}, u32[]{:S(2)}, u32[]{:S(2)}) collective-permute-start(bf16[208,768]{1,0:T(8,128)(2,1)} %get-tuple-element.194), channel_id=1, source_target_pairs={{0,8},{4,12},{8,0},{12,4},{1,9},{5,13},{9,1},{13,5},{2,10},{6,14},... | collective-permute-start | bytes 958472 | tf_op jit(solution)/shard_map/ppermute | solution.py:534
  219.2 20.1 %collective-permute-start.56 = (bf16[208,768]{1,0:T(8,128)(2,1)}, bf16[208,768]{1,0:T(8,128)(2,1)S(1)}, u32[]{:S(2)}, u32[]{:S(2)}) collective-permute-start(bf16[208,768]{1,0:T(8,128)(2,1)} %get-tuple-element.195), channel_id=1, source_target_pairs={{0,12},{4,8},{8,4},{12,0},{1,13},{5,9},{9,5},{13,1},{2,14},{6,10},... | collective-permute-start | bytes 958472 | tf_op jit(solution)/shard_map/ppermute | solution.py:534
  223.5 18.6 %collective-permute-start.50 = (bf16[128,768]{1,0:T(8,128)(2,1)S(1)}, bf16[128,768]{1,0:T(8,128)(2,1)}, u32[]{:S(2)}, u32[]{:S(2)}) collective-permute-start(bf16[128,768]{1,0:T(8,128)(2,1)S(1)} %copy-done.14), channel_id=1, source_target_pairs={{0,1},{1,0},{2,3},{3,2},{4,5},{5,4},{6,7},{7,6},{8,9},{9,8},{10,11... | collective-permute-start | bytes 589832 | tf_op jit(solution)/shard_map/ppermute | solution.py:525
  224.7 18.9 %collective-permute-start.51 = (bf16[128,768]{1,0:T(8,128)(2,1)S(1)}, bf16[128,768]{1,0:T(8,128)(2,1)}, u32[]{:S(2)}, u32[]{:S(2)}) collective-permute-start(bf16[128,768]{1,0:T(8,128)(2,1)S(1)} %get-tuple-element.181), channel_id=1, source_target_pairs={{0,2},{1,3},{2,0},{3,1},{4,6},{5,7},{6,4},{7,5},{8,10},{9,11},{10,... | collective-permute-start | bytes 589832 | tf_op jit(solution)/shard_map/ppermute | solution.py:525
  234.8 9.3 %collective-permute-start.52 = (bf16[128,768]{1,0:T(8,128)(2,1)S(1)}, bf16[128,768]{1,0:T(8,128)(2,1)S(1)}, u32[]{:S(2)}, u32[]{:S(2)}) collective-permute-start(bf16[128,768]{1,0:T(8,128)(2,1)S(1)} %get-tuple-element.182), channel_id=1, source_target_pairs={{0,3},{1,2},{2,1},{3,0},{4,7},{5,6},{6,5},{7,4},{8,11},{9,10},{10,... | collective-permute-start | bytes 589832 | tf_op jit(solution)/shard_map/ppermute | solution.py:525
  237.7 11.7 %collective-permute-start.62 = (bf16[288,768]{1,0:T(8,128)(2,1)S(1)}, bf16[288,768]{1,0:T(8,128)(2,1)S(1)}, u32[]{:S(2)}, u32[]{:S(2)}) collective-permute-start(bf16[288,768]{1,0:T(8,128)(2,1)S(1)} %turn.1), channel_id=1, source_target_pairs={{0,16},{16,0},{1,17},{17,1},{2,18},{18,2},{3,19},{19,3},{4,20},{20... | collective-permute-start | bytes 1327112 | tf_op jit(solution)/shard_map/ppermute | solution.py:660
  240.0 11.5 %collective-permute-start.59 = (f32[6,48]{1,0:T(8,128)S(1)}, f32[6,48]{1,0:T(8,128)S(1)}, u32[]{:S(2)}, u32[]{:S(2)}) collective-permute-start(f32[6,48]{1,0:T(8,128)S(1)} %get-tuple-element.200), channel_id=1, source_target_pairs={{0,1},{1,0},{2,3},{3,2},{4,5},{5,4},{6,7},{7,6},{8,9},{9,8},{10,11... | collective-permute-start | bytes 3464 | tf_op jit(solution)/shard_map/ppermute | solution.py:525
  242.1 9.4 %collective-permute-start.60 = (f32[6,48]{1,0:T(8,128)S(1)}, f32[6,48]{1,0:T(8,128)S(1)}, u32[]{:S(2)}, u32[]{:S(2)}) collective-permute-start(f32[6,48]{1,0:T(8,128)S(1)} %get-tuple-element.201), channel_id=1, source_target_pairs={{0,2},{1,3},{2,0},{3,1},{4,6},{5,7},{6,4},{7,5},{8,10},{9,11},{10,... | collective-permute-start | bytes 3464 | tf_op jit(solution)/shard_map/ppermute | solution.py:525
  243.6 8.0 %collective-permute-start.61 = (f32[6,48]{1,0:T(8,128)S(1)}, f32[6,48]{1,0:T(8,128)S(1)}, u32[]{:S(2)}, u32[]{:S(2)}) collective-permute-start(f32[6,48]{1,0:T(8,128)S(1)} %get-tuple-element.202), channel_id=1, source_target_pairs={{0,3},{1,2},{2,1},{3,0},{4,7},{5,6},{6,5},{7,4},{8,11},{9,10},{10,... | collective-permute-start | bytes 3464 | tf_op jit(solution)/shard_map/ppermute | solution.py:525
  (64 other events, 506.7 us)
Sparse Core Ops, SparseCore 0:
  10.2 34.5 all-gather.3
  47.0 30.4 all-gather.5
  79.1 30.7 all-gather.7
  138.5 27.7 reduce-scatter.2
  190.9 42.2 reduce-scatter.4
